TPU v7x, 32 devices: a whole 2x2x4 slice. The times are simulated.
32 devices in a mesh: section: 4 (over z), dp: 2 (over x), mp: 4 (over y, core).
Axes of the slice: x: 2, y: 2, z: 4, core: 2. Of those that a mesh axis runs over, the one named last changes fastest.
Arguments:
- inputs: bfloat16 [8, 512, 768], P('dp', 'mp'), may hold values from -7 to 7
- attn_qkv: bfloat16 [3, 768, 768], P(None, None, 'mp'), may hold values from -0.21875 to 0.21875
- attn_out: bfloat16 [768, 768], P('mp'), may hold values from -0.875 to 0.875
- conv_in: bfloat16 [2, 768, 768], P(None, None, 'mp'), may hold values from -0.21875 to 0.21875
- conv_kernel: bfloat16 [7, 768], P(None, 'mp'), may hold values from -3 to 3
- conv_out: bfloat16 [768, 768], P('mp'), may hold values from -0.3125 to 0.3125
- ffn_up: bfloat16 [2, 768, 3072], P(None, None, 'mp'), may hold values from -0.21875 to 0.21875
- ffn_down: bfloat16 [2, 3072, 768], P(None, 'mp'), may hold values from -0.15625 to 0.15625
- norm_gain: float32 [4, 768], replicated, may hold values from 0.5 to 1.5
- norm_bias: float32 [4, 768], replicated, may hold values from -1.5 to 1.5
- kernel_half: int32 [1], replicated, may hold values from 1 to 3
- batch_plan: int32 [2, 2, 2], replicated, may hold values from -1 to 3, as said below
- masked_positions: int32 [8, 77], P('dp'), may hold values from 0 to 511, as said below
- out_grad: bfloat16 [8, 77, 768], P('dp'), may hold values from -6 to 6
Outputs:
- layer_out: bfloat16 [8, 512, 768], P('dp', 'mp')
- input_grad: float32 [8, 512, 768], P('dp', 'mp')
- grad_attn_qkv: float32 [3, 768, 768], P(None, None, 'mp')
- grad_attn_out: float32 [768, 768], P('mp')
- grad_conv_in: float32 [2, 768, 768], P(None, None, 'mp')
- grad_conv_kernel: float32 [7, 768], P(None, 'mp')
- grad_conv_out: float32 [768, 768], P('mp')
- grad_ffn_up: float32 [2, 768, 3072], P(None, None, 'mp')
- grad_ffn_down: float32 [2, 3072, 768], P(None, 'mp')
- grad_norm_gain: float32 [4, 768], replicated
- grad_norm_bias: float32 [4, 768], replicated
- stream_rms: float32 [2, 8], replicated
Inputs may be any that keep to these rules, and one draw needn't show every extreme that they name: In each replica batch_plan[r, m, 0] over m is a permutation of 0 to 1. batch_plan[r, m, 1] is -1 or a slot from 2 to 3; in a replica the paired micro-batches use the slots 2, 3 and so on, each once. Some replica pairs every micro-batch and some replica has a micro-batch of one sequence. `masked_positions`: positions of one sequence are distinct.
All inputs are finite; a program needn't handle non-finite values.
Results may differ from a plain program's by a relative error of at most 0.02.
Values may be sent and summed in bfloat16 or wider, within the bound.
A program may use at most 128 MiB of HBM per device.

v0:
```python
import jax
import jax.numpy as jnp
from jax import lax
from jax.sharding import PartitionSpec as P

HEAD = 64
TAPS = 7


EPSILON = 1e-05


def shifted(array, axis, by):
    peers = lax.axis_size(axis)
    return lax.ppermute(array, axis, [(i, (i + by) % peers) for i in range(peers)])


def norm_forward(summed, gain_row, bias_row):
    centre = summed - jnp.mean(summed, axis=-1, keepdims=True)
    variance = jnp.mean(centre * centre, axis=-1, keepdims=True)
    inverse = lax.rsqrt(variance + EPSILON)
    normed = centre * inverse
    return (normed * gain_row + bias_row, normed, inverse)


def norm_backward(grad_out, normed, inverse, gain_row):
    scaled = grad_out * gain_row
    first_mean = jnp.mean(scaled, axis=-1, keepdims=True)
    second_mean = jnp.mean(scaled * normed, axis=-1, keepdims=True)
    return inverse * (scaled - first_mean - normed * second_mean)


def spread_rows(shard):
    return lax.all_gather(shard, "mp", axis=1, tiled=True)


def branch_total(partial_value):
    return lax.psum_scatter(partial_value, "mp", scatter_dimension=1, tiled=True)


def grad_rows(shard):
    return lax.all_gather(shard.astype(jnp.bfloat16), "mp", axis=1, tiled=True)


def input_total(partial_value):
    return lax.psum_scatter(partial_value, "mp", scatter_dimension=1, tiled=True)


def keep_item(buffer, item, position, active):
    old_item = lax.dynamic_index_in_dim(buffer, position, 0, keepdims=False)
    return lax.dynamic_update_index_in_dim(
        buffer, jnp.where(active > 0, item, old_item), position, 0
    )


def place_rows(buffer, new_values, slot_pair, present, active):
    for member in range(2):
        slot_id = jnp.maximum(slot_pair[member], 0)
        old_rows = lax.dynamic_index_in_dim(buffer, slot_id, 0, keepdims=False)
        new_rows = jnp.where(present[member] * active > 0, new_values[member], old_rows)
        buffer = lax.dynamic_update_index_in_dim(buffer, new_rows, slot_id, 0)
    return buffer


def column(position):
    return (jnp.arange(8) == position).astype(jnp.float32)


def on_device(
    inputs,
    attn_qkv,
    attn_out,
    conv_in,
    conv_kernel,
    conv_out,
    ffn_up,
    ffn_down,
    norm_gain,
    norm_bias,
    kernel_half,
    batch_plan,
    masked_positions,
    out_grad,
):
    sections = lax.axis_size("section")
    section_id = lax.axis_index("section")
    replica = lax.axis_index("dp")
    dp_count = lax.axis_size("dp")
    mp_index = lax.axis_index("mp")
    slot_count, shard_rows, model_width = inputs.shape
    micro_count = batch_plan.shape[1]
    seq_len = shard_rows * lax.axis_size("mp")
    replica_plan = lax.dynamic_index_in_dim(batch_plan, replica, 0, keepdims=False)
    margin = TAPS // 2
    tap_mask = (jnp.abs(jnp.arange(TAPS) - margin) <= kernel_half[0]).astype(jnp.float32)
    tap_weights = conv_kernel.astype(jnp.float32) * tap_mask[:, None]
    scale = HEAD ** (-0.5)

    def attention_parts(hidden):
        seq_count, length = (hidden.shape[0], hidden.shape[1])
        heads_here = attn_qkv.shape[2] // HEAD
        projected = jnp.einsum(
            "bld,kdc->kblc", hidden, attn_qkv, preferred_element_type=jnp.float32
        ).astype(jnp.bfloat16)
        projected_heads = projected.reshape(3, seq_count, length, heads_here, HEAD)
        queries, key_rows, value_rows = (projected_heads[0], projected_heads[1], projected_heads[2])
        scores = (
            jnp.einsum("bqhe,bkhe->bhqk", queries, key_rows, preferred_element_type=jnp.float32)
            * scale
        )
        softmax_rows = jax.nn.softmax(scores, axis=-1)
        weights = softmax_rows.astype(jnp.bfloat16)
        mixture = jnp.einsum(
            "bhqk,bkhe->bqhe", weights, value_rows, preferred_element_type=jnp.float32
        )
        mixture = mixture.astype(jnp.bfloat16).reshape(seq_count, length, heads_here * HEAD)
        return (queries, key_rows, value_rows, softmax_rows, weights, mixture)

    def attention_forward(hidden):
        mixture = attention_parts(hidden)[5]
        return jnp.einsum("blc,cd->bld", mixture, attn_out, preferred_element_type=jnp.float32)

    def attention_backward(hidden, grad_full, grad_acc, active):
        queries, key_rows, value_rows, softmax_rows, weights, mixture = attention_parts(hidden)
        seq_count, length, heads_here = (queries.shape[0], queries.shape[1], queries.shape[2])
        grad_mix = jnp.einsum(
            "bld,cd->blc", grad_full, attn_out, preferred_element_type=jnp.float32
        ).astype(jnp.bfloat16)
        grad_outw = jnp.einsum(
            "blc,bld->cd", mixture, grad_full, preferred_element_type=jnp.float32
        )
        grad_heads = grad_mix.reshape(seq_count, length, heads_here, HEAD)
        grad_values = jnp.einsum(
            "bhqk,bqhe->bkhe", weights, grad_heads, preferred_element_type=jnp.float32
        ).astype(jnp.bfloat16)
        grad_probs = jnp.einsum(
            "bqhe,bkhe->bhqk", grad_heads, value_rows, preferred_element_type=jnp.float32
        )
        grad_scores = softmax_rows * (
            grad_probs - jnp.sum(grad_probs * softmax_rows, axis=-1, keepdims=True)
        )
        grad_scores = grad_scores.astype(jnp.bfloat16)
        grad_queries = (
            jnp.einsum("bhqk,bkhe->bqhe", grad_scores, key_rows, preferred_element_type=jnp.float32)
            * scale
        ).astype(jnp.bfloat16)
        grad_keys = (
            jnp.einsum("bhqk,bqhe->bkhe", grad_scores, queries, preferred_element_type=jnp.float32)
            * scale
        ).astype(jnp.bfloat16)
        grad_proj = jnp.stack([grad_queries, grad_keys, grad_values]).reshape(
            3, seq_count, length, heads_here * HEAD
        )
        grad_qkv = jnp.einsum(
            "bld,kblc->kdc", hidden, grad_proj, preferred_element_type=jnp.float32
        )
        grad_hidden = jnp.einsum(
            "kblc,kdc->bld", grad_proj, attn_qkv, preferred_element_type=jnp.float32
        )
        members = list(grad_acc)
        members[0] = members[0] + active * grad_qkv
        members[1] = members[1] + active * grad_outw
        return (grad_hidden, tuple(members))

    def ffn_forward(hidden, layer_id):
        before = jnp.einsum(
            "bld,df->blf", hidden, ffn_up[layer_id], preferred_element_type=jnp.float32
        )
        units = jax.nn.gelu(before, approximate=False).astype(jnp.bfloat16)
        return jnp.einsum(
            "blf,fd->bld", units, ffn_down[layer_id], preferred_element_type=jnp.float32
        )

    def ffn_backward(hidden, grad_full, grad_acc, active, layer_id):
        before = jnp.einsum(
            "bld,df->blf", hidden, ffn_up[layer_id], preferred_element_type=jnp.float32
        )
        units, gelu_pull = jax.vjp(
            lambda inner_rows: jax.nn.gelu(inner_rows, approximate=False), before
        )
        units_low = units.astype(jnp.bfloat16)
        grad_units = jnp.einsum(
            "bld,fd->blf", grad_full, ffn_down[layer_id], preferred_element_type=jnp.float32
        )
        grad_before = gelu_pull(grad_units)[0].astype(jnp.bfloat16)
        grad_down = jnp.einsum(
            "blf,bld->fd", units_low, grad_full, preferred_element_type=jnp.float32
        )
        grad_up = jnp.einsum("bld,blf->df", hidden, grad_before, preferred_element_type=jnp.float32)
        grad_hidden = jnp.einsum(
            "blf,df->bld", grad_before, ffn_up[layer_id], preferred_element_type=jnp.float32
        )
        members = list(grad_acc)
        members[5] = members[5].at[layer_id].add(active * grad_up)
        members[6] = members[6].at[layer_id].add(active * grad_down)
        return (grad_hidden, tuple(members))

    def conv_parts(hidden):
        length = hidden.shape[1]
        projected = jnp.einsum("bld,kdc->kblc", hidden, conv_in, preferred_element_type=jnp.float32)
        value_rows, gate_rows = (projected[0], projected[1])
        gate_sig = jax.nn.sigmoid(gate_rows)
        gated = value_rows * gate_sig
        padded = jnp.pad(gated, ((0, 0), (margin, margin), (0, 0)))
        mixture = jnp.zeros_like(gated)
        for offset in range(TAPS):
            mixture = (
                mixture + tap_weights[offset][None, None, :] * padded[:, offset : offset + length]
            )
        return (value_rows, gate_sig, padded, mixture.astype(jnp.bfloat16))

    def conv_forward(hidden):
        mixture_low = conv_parts(hidden)[3]
        return jnp.einsum("blc,cd->bld", mixture_low, conv_out, preferred_element_type=jnp.float32)

    def conv_backward(hidden, grad_full, grad_acc, active):
        length = hidden.shape[1]
        value_rows, gate_sig, padded, mixture_low = conv_parts(hidden)
        grad_mix = jnp.einsum(
            "bld,cd->blc", grad_full, conv_out, preferred_element_type=jnp.float32
        )
        grad_outw = jnp.einsum(
            "blc,bld->cd", mixture_low, grad_full, preferred_element_type=jnp.float32
        )
        grad_pad = jnp.pad(grad_mix, ((0, 0), (margin, margin), (0, 0)))
        grad_gated = jnp.zeros_like(grad_mix)
        kernel_rows = []
        for offset in range(TAPS):
            start_row = 2 * margin - offset
            grad_gated = (
                grad_gated
                + tap_weights[offset][None, None, :] * grad_pad[:, start_row : start_row + length]
            )
            kernel_rows.append(jnp.sum(padded[:, offset : offset + length] * grad_mix, axis=(0, 1)))
        grad_kernel = jnp.stack(kernel_rows) * tap_mask[:, None]
        grad_value = (grad_gated * gate_sig).astype(jnp.bfloat16)
        grad_gate = (grad_gated * value_rows * gate_sig * (1.0 - gate_sig)).astype(jnp.bfloat16)
        grad_proj = jnp.stack([grad_value, grad_gate])
        grad_inw = jnp.einsum(
            "bld,kblc->kdc", hidden, grad_proj, preferred_element_type=jnp.float32
        )
        grad_hidden = jnp.einsum(
            "kblc,kdc->bld", grad_proj, conv_in, preferred_element_type=jnp.float32
        )
        members = list(grad_acc)
        members[2] = members[2] + active * grad_inw
        members[3] = members[3] + active * grad_kernel
        members[4] = members[4] + active * grad_outw
        return (grad_hidden, tuple(members))

    forward_fns = [
        attention_forward,
        lambda hidden: ffn_forward(hidden, 0),
        conv_forward,
        lambda hidden: ffn_forward(hidden, 1),
    ]
    back_fns = [
        attention_backward,
        lambda hidden, grad_full, grad_acc, active: ffn_backward(
            hidden, grad_full, grad_acc, active, 0
        ),
        conv_backward,
        lambda hidden, grad_full, grad_acc, active: ffn_backward(
            hidden, grad_full, grad_acc, active, 1
        ),
    ]

    def slots_of(micro_id):
        slot_pair = lax.dynamic_index_in_dim(replica_plan, micro_id, 0, keepdims=False)
        present = jnp.stack([jnp.float32(1.0), (slot_pair[1] >= 0).astype(jnp.float32)])
        return (slot_pair, present)

    def pick_rows(slot_pair, present):
        first_rows = lax.dynamic_index_in_dim(inputs, slot_pair[0], 0, keepdims=False)
        second_rows = lax.dynamic_index_in_dim(
            inputs, jnp.maximum(slot_pair[1], 0), 0, keepdims=False
        )
        second_rows = jnp.where(present[1] > 0, second_rows, jnp.zeros_like(second_rows))
        return jnp.stack([first_rows, second_rows])

    def cotangent_rows(slot_pair, present):
        positions = jnp.arange(shard_rows) + mp_index * shard_rows
        pieces = []
        for member in range(2):
            slot_id = jnp.maximum(slot_pair[member], 0)
            where_rows = lax.dynamic_index_in_dim(masked_positions, slot_id, 0, keepdims=False)
            grad_values = lax.dynamic_index_in_dim(out_grad, slot_id, 0, keepdims=False)
            hit_table = (where_rows[:, None] == positions[None, :]).astype(jnp.bfloat16)
            pieces.append(
                jnp.einsum("nr,nd->rd", hit_table, grad_values, preferred_element_type=jnp.float32)
                * present[member]
            )
        return jnp.stack(pieces)

    def section_forward(section_in, branch_fn, gain_row, bias_row, present):
        hidden = spread_rows(section_in)
        branch_out = branch_total(branch_fn(hidden))
        stream_rows = section_in.astype(jnp.float32)
        summed = stream_rows + branch_out
        normed_out = norm_forward(summed, gain_row, bias_row)[0]
        weight_rows = present[:, None, None]
        stream_term = jnp.sum(weight_rows * stream_rows * stream_rows)
        branch_term = jnp.sum(weight_rows * branch_out * branch_out)
        return (hidden, summed, normed_out, stream_term, branch_term)

    def section_backward(
        grad_out, hidden, summed, gain_row, bias_row, branch_back, grad_acc, active
    ):
        normed, inverse = norm_forward(summed, gain_row, bias_row)[1:]
        gain_term = active * jnp.sum(grad_out * normed, axis=(0, 1))
        bias_term = active * jnp.sum(grad_out, axis=(0, 1))
        grad_sum = norm_backward(grad_out, normed, inverse, gain_row)
        grad_full = grad_rows(grad_sum)
        grad_hidden, grad_acc = branch_back(hidden, grad_full, grad_acc, active)
        return (grad_sum + input_total(grad_hidden), grad_acc, gain_term, bias_term)

    grad_acc = tuple(
        (
            jnp.zeros(weight.shape, jnp.float32)
            for weight in (attn_qkv, attn_out, conv_in, conv_kernel, conv_out, ffn_up, ffn_down)
        )
    )
    gain_acc = jnp.zeros((4, model_width), jnp.float32)
    bias_acc = jnp.zeros((4, model_width), jnp.float32)
    out_rows = jnp.zeros((slot_count, shard_rows, model_width), jnp.float32)
    in_rows = jnp.zeros((slot_count, shard_rows, model_width), jnp.float32)
    stat_vec = jnp.zeros((8,), jnp.float32)
    tick_count = micro_count + sections - 1
    block_pos = (section_id + 2) % sections
    is_first = (block_pos == 0).astype(jnp.float32)
    is_last = (block_pos == sections - 1).astype(jnp.float32)
    section_row = (jnp.arange(4) == block_pos).astype(jnp.float32)

    def forward_tick(tick_id, state_tuple):
        incoming, kept_hidden, kept_sum, out_buffer, stat_sum = state_tuple
        micro_id = tick_id - block_pos
        active = ((micro_id >= 0) & (micro_id < micro_count)).astype(jnp.float32)
        micro_id = jnp.clip(micro_id, 0, micro_count - 1)
        slot_pair, present = slots_of(micro_id)
        section_in = jnp.where(block_pos == 0, pick_rows(slot_pair, present), incoming)
        hidden, summed, normed_out, stream_term, branch_term = section_forward(
            section_in,
            lambda full_rows: lax.switch(block_pos, forward_fns, full_rows),
            norm_gain[block_pos],
            norm_bias[block_pos],
            present,
        )
        stat_sum = stat_sum + active * (
            stream_term * column(block_pos) + branch_term * column(block_pos + 4)
        )
        kept_hidden = keep_item(kept_hidden, hidden, micro_id, active)
        kept_sum = keep_item(kept_sum, summed, micro_id, active)
        final_rows = normed_out.astype(jnp.bfloat16)
        out_buffer = place_rows(
            out_buffer, final_rows.astype(jnp.float32), slot_pair, present, active * is_last
        )
        incoming = shifted(final_rows, "section", 1)
        return (incoming, kept_hidden, kept_sum, out_buffer, stat_sum)

    start_fwd = (
        jnp.zeros((2, shard_rows, model_width), jnp.bfloat16),
        jnp.zeros((micro_count, 2, seq_len, model_width), jnp.bfloat16),
        jnp.zeros((micro_count, 2, shard_rows, model_width), jnp.float32),
        out_rows,
        stat_vec,
    )
    incoming, kept_hidden, kept_sum, out_rows, stat_vec = lax.fori_loop(
        0, tick_count, forward_tick, start_fwd
    )

    def switch_back(hidden, grad_full, grad_state, active):
        return lax.switch(block_pos, back_fns, hidden, grad_full, grad_state, active)

    def backward_tick(tick_id, state_tuple):
        incoming, grad_state, gain_state, bias_state, in_buffer = state_tuple
        micro_id = tick_id - (sections - 1 - block_pos)
        active = ((micro_id >= 0) & (micro_id < micro_count)).astype(jnp.float32)
        micro_id = jnp.clip(micro_id, 0, micro_count - 1)
        slot_pair, present = slots_of(micro_id)
        grad_out = jnp.where(
            block_pos == sections - 1, cotangent_rows(slot_pair, present), incoming
        )
        hidden = lax.dynamic_index_in_dim(kept_hidden, micro_id, 0, keepdims=False)
        summed = lax.dynamic_index_in_dim(kept_sum, micro_id, 0, keepdims=False)
        grad_in, grad_state, gain_term, bias_term = section_backward(
            grad_out,
            hidden,
            summed,
            norm_gain[block_pos],
            norm_bias[block_pos],
            switch_back,
            grad_state,
            active,
        )
        gain_state = gain_state + section_row[:, None] * gain_term[None, :]
        bias_state = bias_state + section_row[:, None] * bias_term[None, :]
        in_buffer = place_rows(in_buffer, grad_in, slot_pair, present, active * is_first)
        incoming = shifted(grad_in, "section", -1)
        return (incoming, grad_state, gain_state, bias_state, in_buffer)

    start_back = (
        jnp.zeros((2, shard_rows, model_width), jnp.float32),
        grad_acc,
        gain_acc,
        bias_acc,
        in_rows,
    )
    incoming, grad_acc, gain_acc, bias_acc, in_rows = lax.fori_loop(
        0, tick_count, backward_tick, start_back
    )
    grad_qkv, grad_outw, grad_inw, grad_kernel, grad_convw, grad_up, grad_down = grad_acc
    grad_qkv, grad_outw, grad_inw, grad_kernel, grad_convw, grad_up, grad_down = (
        lax.psum(grad_qkv.astype(jnp.bfloat16), ("section", "dp")).astype(jnp.float32),
        lax.psum(grad_outw.astype(jnp.bfloat16), ("section", "dp")).astype(jnp.float32),
        lax.psum(grad_inw.astype(jnp.bfloat16), ("section", "dp")).astype(jnp.float32),
        lax.psum(grad_kernel.astype(jnp.bfloat16), ("section", "dp")).astype(jnp.float32),
        lax.psum(grad_convw.astype(jnp.bfloat16), ("section", "dp")).astype(jnp.float32),
        lax.psum(grad_up.astype(jnp.bfloat16), ("section", "dp")).astype(jnp.float32),
        lax.psum(grad_down.astype(jnp.bfloat16), ("section", "dp")).astype(jnp.float32),
    )
    replica_rows = (jnp.arange(dp_count) == replica).astype(jnp.float32)[:, None] * stat_vec[
        None, :
    ]
    gain_sum, bias_sum, stat_sum = lax.psum(
        (gain_acc, bias_acc, replica_rows), ("section", "dp", "mp")
    )
    out_sum, in_sum = (
        lax.psum(out_rows.astype(jnp.bfloat16), "section").astype(jnp.float32),
        lax.psum(in_rows.astype(jnp.bfloat16), "section").astype(jnp.float32),
    )
    pairs_used = jnp.sum((batch_plan[:, :, 1] >= 0).astype(jnp.float32), axis=1) + micro_count
    stream_rms = jnp.sqrt(stat_sum / (pairs_used * (seq_len * model_width))[:, None])
    return (
        out_sum.astype(jnp.bfloat16),
        in_sum,
        grad_qkv,
        grad_outw,
        grad_inw,
        grad_kernel,
        grad_convw,
        grad_up,
        grad_down,
        gain_sum,
        bias_sum,
        stream_rms,
    )


def solution(mesh):
    return jax.shard_map(
        on_device,
        mesh=mesh,
        in_specs=(
            P("dp", "mp", None),
            P(None, None, "mp"),
            P("mp", None),
            P(None, None, "mp"),
            P(None, "mp"),
            P("mp", None),
            P(None, None, "mp"),
            P(None, "mp", None),
            P(),
            P(),
            P(),
            P(),
            P("dp", None),
            P("dp", None, None),
        ),
        out_specs=(
            P("dp", "mp", None),
            P("dp", "mp", None),
            P(None, None, "mp"),
            P("mp", None),
            P(None, None, "mp"),
            P(None, "mp"),
            P("mp", None),
            P(None, None, "mp"),
            P(None, "mp", None),
            P(),
            P(),
            P(),
        ),
        check_vma=False,
    )
```

profile of v0, /device:TPU:0, one launch (start us, length us, event | category | flops | bytes accessed | tf_op | source)
XLA Modules:
  0.0 1559.5 jit_solution(3751602549416609479)
XLA Ops:
  17.5 469.3 %while.64 = (s32[]{:T(128)}, bf16[2,128,768]{2,1,0:T(8,128)(2,1)S(1)}, bf16[2,2,512,768]{3,2,1,0:T(8,128)(2,1)}, f32[2,2,128,768]{3,2,1,0:T(8,128)S(1)}, bf16[4,...) while((s32[]{:T(128)}, ...), condition=%wide.region_12.13_spmd.clone, body=%wide.region_0.12_spmd.clone.sunk | while | flops 2488762624 | bytes 84987920 | solution.py:367
  23.9 22.5 %all-gather.3.cloned.1.call-done = bf16[2,512,768]{2,1,0:T(8,128)(2,1)} async-done(((bf16[2,128,768]{2,1,0:T(8,128)(2,1)}), bf16[2,512,768]{2,1,0:T(8,128)(2,1)}) %all-gather.3.cloned.1.call-update) | async-done | bytes 1572880 | tf_op jit(solution)/shard_map/while/body/eval_jaxpr/all_gather | solution.py:34
  59.3 38.8 %reduce-scatter.3.cloned.1.call-done = f32[2,128,768]{2,1,0:T(8,128)} async-done(((f32[2,512,768]{2,1,0:T(8,128)}), f32[2,128,768]{2,1,0:T(8,128)}) %reduce-scatter.3.cloned.1.call-update) | async-done | bytes 786448 | tf_op jit(solution)/shard_map/while/body/eval_jaxpr/reduce_scatter | solution.py:38
  121.4 18.0 %all-gather.3.cloned.1.call-done = bf16[2,512,768]{2,1,0:T(8,128)(2,1)} async-done(((bf16[2,128,768]{2,1,0:T(8,128)(2,1)}), bf16[2,512,768]{2,1,0:T(8,128)(2,1)}) %all-gather.3.cloned.1.call-update) | async-done | bytes 1572880 | tf_op jit(solution)/shard_map/while/body/eval_jaxpr/all_gather | solution.py:34
  152.3 38.9 %reduce-scatter.3.cloned.1.call-done = f32[2,128,768]{2,1,0:T(8,128)} async-done(((f32[2,512,768]{2,1,0:T(8,128)}), f32[2,128,768]{2,1,0:T(8,128)}) %reduce-scatter.3.cloned.1.call-update) | async-done | bytes 786448 | tf_op jit(solution)/shard_map/while/body/eval_jaxpr/reduce_scatter | solution.py:38
  214.4 18.0 %all-gather.3.cloned.1.call-done = bf16[2,512,768]{2,1,0:T(8,128)(2,1)} async-done(((bf16[2,128,768]{2,1,0:T(8,128)(2,1)}), bf16[2,512,768]{2,1,0:T(8,128)(2,1)}) %all-gather.3.cloned.1.call-update) | async-done | bytes 1572880 | tf_op jit(solution)/shard_map/while/body/eval_jaxpr/all_gather | solution.py:34
  245.3 38.9 %reduce-scatter.3.cloned.1.call-done = f32[2,128,768]{2,1,0:T(8,128)} async-done(((f32[2,512,768]{2,1,0:T(8,128)}), f32[2,128,768]{2,1,0:T(8,128)}) %reduce-scatter.3.cloned.1.call-update) | async-done | bytes 786448 | tf_op jit(solution)/shard_map/while/body/eval_jaxpr/reduce_scatter | solution.py:38
  307.4 18.0 %all-gather.3.cloned.1.call-done = bf16[2,512,768]{2,1,0:T(8,128)(2,1)} async-done(((bf16[2,128,768]{2,1,0:T(8,128)(2,1)}), bf16[2,512,768]{2,1,0:T(8,128)(2,1)}) %all-gather.3.cloned.1.call-update) | async-done | bytes 1572880 | tf_op jit(solution)/shard_map/while/body/eval_jaxpr/all_gather | solution.py:34
  338.3 38.8 %reduce-scatter.3.cloned.1.call-done = f32[2,128,768]{2,1,0:T(8,128)} async-done(((f32[2,512,768]{2,1,0:T(8,128)}), f32[2,128,768]{2,1,0:T(8,128)}) %reduce-scatter.3.cloned.1.call-update) | async-done | bytes 786448 | tf_op jit(solution)/shard_map/while/body/eval_jaxpr/reduce_scatter | solution.py:38
  400.3 18.0 %all-gather.3.cloned.1.call-done = bf16[2,512,768]{2,1,0:T(8,128)(2,1)} async-done(((bf16[2,128,768]{2,1,0:T(8,128)(2,1)}), bf16[2,512,768]{2,1,0:T(8,128)(2,1)}) %all-gather.3.cloned.1.call-update) | async-done | bytes 1572880 | tf_op jit(solution)/shard_map/while/body/eval_jaxpr/all_gather | solution.py:34
  431.3 38.9 %reduce-scatter.3.cloned.1.call-done = f32[2,128,768]{2,1,0:T(8,128)} async-done(((f32[2,512,768]{2,1,0:T(8,128)}), f32[2,128,768]{2,1,0:T(8,128)}) %reduce-scatter.3.cloned.1.call-update) | async-done | bytes 786448 | tf_op jit(solution)/shard_map/while/body/eval_jaxpr/reduce_scatter | solution.py:38
  498.8 730.5 %while.65 = (s32[]{:T(128)}, f32[2,128,768]{2,1,0:T(8,128)}, f32[3,768,192]{2,1,0:T(8,128)}, f32[192,768]{1,0:T(8,128)}, f32[2,768,192]{2,1,0:T(8,128)}, /*index...) while((s32[]{:T(128)}, f32[2,128,768]{2,1,0:T(8,128)}, ...), condition=%wide.region_36.37_spmd.clone, body=%wide.region_14.36_spmd.clone.sunk | while | flops 6154360320 | bytes 202220944 | solution.py:408
  512.7 15.2 all-gather.5.cloned.1.call-done
  527.9 33.5 %conditional.7 = (f32[2,512,768]{2,1,0:T(8,128)}, f32[3,768,192]{2,1,0:T(8,128)}, f32[192,768]{1,0:T(8,128)}, f32[2,768,192]{2,1,0:T(8,128)}, f32[7,192]{1,0:T(8...) conditional(s32[]{:T(128)} %get-tuple-element.2568, ...), branch_computations={%region_19.22_spmd, %region_23.23_spmd, %region_24.31_spmd, %regio... | conditional | flops 6117654528 | bytes 155210304 | solution.py:372
  562.1 57.5 %reduce-scatter.5.cloned.1.call-done = f32[2,128,768]{2,1,0:T(8,128)} async-done(((f32[2,512,768]{2,1,0:T(8,128)}), f32[2,128,768]{2,1,0:T(8,128)}) %reduce-scatter.5.cloned.1.call-update) | async-done | bytes 786448 | tf_op jit(solution)/shard_map/while/body/eval_jaxpr/reduce_scatter | solution.py:46
  655.8 17.9 %all-gather.5.cloned.1.call-done = bf16[2,512,768]{2,1,0:T(8,128)(2,1)} async-done(((bf16[2,128,768]{2,1,0:T(8,128)(2,1)}), bf16[2,512,768]{2,1,0:T(8,128)(2,1)}) %all-gather.5.cloned.1.call-update) | async-done | bytes 1572880 | tf_op jit(solution)/shard_map/while/body/eval_jaxpr/all_gather | solution.py:42
  673.7 33.4 %conditional.7 = (f32[2,512,768]{2,1,0:T(8,128)}, f32[3,768,192]{2,1,0:T(8,128)}, f32[192,768]{1,0:T(8,128)}, f32[2,768,192]{2,1,0:T(8,128)}, f32[7,192]{1,0:T(8...) conditional(s32[]{:T(128)} %get-tuple-element.2568, ...), branch_computations={%region_19.22_spmd, %region_23.23_spmd, %region_24.31_spmd, %regio... | conditional | flops 6117654528 | bytes 155210304 | solution.py:372
  707.8 57.6 %reduce-scatter.5.cloned.1.call-done = f32[2,128,768]{2,1,0:T(8,128)} async-done(((f32[2,512,768]{2,1,0:T(8,128)}), f32[2,128,768]{2,1,0:T(8,128)}) %reduce-scatter.5.cloned.1.call-update) | async-done | bytes 786448 | tf_op jit(solution)/shard_map/while/body/eval_jaxpr/reduce_scatter | solution.py:46
  801.7 17.9 %all-gather.5.cloned.1.call-done = bf16[2,512,768]{2,1,0:T(8,128)(2,1)} async-done(((bf16[2,128,768]{2,1,0:T(8,128)(2,1)}), bf16[2,512,768]{2,1,0:T(8,128)(2,1)}) %all-gather.5.cloned.1.call-update) | async-done | bytes 1572880 | tf_op jit(solution)/shard_map/while/body/eval_jaxpr/all_gather | solution.py:42
  819.6 33.2 %conditional.7 = (f32[2,512,768]{2,1,0:T(8,128)}, f32[3,768,192]{2,1,0:T(8,128)}, f32[192,768]{1,0:T(8,128)}, f32[2,768,192]{2,1,0:T(8,128)}, f32[7,192]{1,0:T(8...) conditional(s32[]{:T(128)} %get-tuple-element.2568, ...), branch_computations={%region_19.22_spmd, %region_23.23_spmd, %region_24.31_spmd, %regio... | conditional | flops 6117654528 | bytes 155210304 | solution.py:372
  853.5 57.8 %reduce-scatter.5.cloned.1.call-done = f32[2,128,768]{2,1,0:T(8,128)} async-done(((f32[2,512,768]{2,1,0:T(8,128)}), f32[2,128,768]{2,1,0:T(8,128)}) %reduce-scatter.5.cloned.1.call-update) | async-done | bytes 786448 | tf_op jit(solution)/shard_map/while/body/eval_jaxpr/reduce_scatter | solution.py:46
  947.8 17.9 %all-gather.5.cloned.1.call-done = bf16[2,512,768]{2,1,0:T(8,128)(2,1)} async-done(((bf16[2,128,768]{2,1,0:T(8,128)(2,1)}), bf16[2,512,768]{2,1,0:T(8,128)(2,1)}) %all-gather.5.cloned.1.call-update) | async-done | bytes 1572880 | tf_op jit(solution)/shard_map/while/body/eval_jaxpr/all_gather | solution.py:42
  965.8 33.5 %conditional.7 = (f32[2,512,768]{2,1,0:T(8,128)}, f32[3,768,192]{2,1,0:T(8,128)}, f32[192,768]{1,0:T(8,128)}, f32[2,768,192]{2,1,0:T(8,128)}, f32[7,192]{1,0:T(8...) conditional(s32[]{:T(128)} %get-tuple-element.2568, ...), branch_computations={%region_19.22_spmd, %region_23.23_spmd, %region_24.31_spmd, %regio... | conditional | flops 6117654528 | bytes 155210304 | solution.py:372
  1000.0 57.5 %reduce-scatter.5.cloned.1.call-done = f32[2,128,768]{2,1,0:T(8,128)} async-done(((f32[2,512,768]{2,1,0:T(8,128)}), f32[2,128,768]{2,1,0:T(8,128)}) %reduce-scatter.5.cloned.1.call-update) | async-done | bytes 786448 | tf_op jit(solution)/shard_map/while/body/eval_jaxpr/reduce_scatter | solution.py:46
  1065.7 13.4 collective-permute-done.1
  1093.7 17.9 %all-gather.5.cloned.1.call-done = bf16[2,512,768]{2,1,0:T(8,128)(2,1)} async-done(((bf16[2,128,768]{2,1,0:T(8,128)(2,1)}), bf16[2,512,768]{2,1,0:T(8,128)(2,1)}) %all-gather.5.cloned.1.call-update) | async-done | bytes 1572880 | tf_op jit(solution)/shard_map/while/body/eval_jaxpr/all_gather | solution.py:42
  1111.6 33.4 %conditional.7 = (f32[2,512,768]{2,1,0:T(8,128)}, f32[3,768,192]{2,1,0:T(8,128)}, f32[192,768]{1,0:T(8,128)}, f32[2,768,192]{2,1,0:T(8,128)}, f32[7,192]{1,0:T(8...) conditional(s32[]{:T(128)} %get-tuple-element.2568, ...), branch_computations={%region_19.22_spmd, %region_23.23_spmd, %region_24.31_spmd, %regio... | conditional | flops 6117654528 | bytes 155210304 | solution.py:372
  1145.7 57.6 %reduce-scatter.5.cloned.1.call-done = f32[2,128,768]{2,1,0:T(8,128)} async-done(((f32[2,512,768]{2,1,0:T(8,128)}), f32[2,128,768]{2,1,0:T(8,128)}) %reduce-scatter.5.cloned.1.call-update) | async-done | bytes 786448 | tf_op jit(solution)/shard_map/while/body/eval_jaxpr/reduce_scatter | solution.py:46
  1211.5 13.4 collective-permute-done.1
  1247.1 23.3 %psum.89 = bf16[7,192]{1,0:T(8,128)(2,1)S(1)} all-reduce(bf16[7,192]{1,0:T(8,128)(2,1)S(1)} %convert_element_type.269), channel_id=1, replica_groups=mesh['section'=4,'dp'=2,'mp'=4] {'section','dp'}, use_global_device_ids=true, to_apply=%region_41.42 | all-reduce | flops 1344 | bytes 5376 | tf_op jit(solution)/shard_map/psum | solution.py:416
  1271.1 39.5 %all-reduce.3 = (f32[4,768]{1,0:T(4,128)}, f32[4,768]{1,0:T(4,128)}, f32[2,8]{1,0:T(2,128)S(1)}) all-reduce(f32[4,768]{1,0:T(4,128)S(1)} %copy-done.53, f32[4,768]{1,0:T(4,128)S(1)} %copy-done.50, f32[2,8]{1,0:T(2,128)S(1)} %broadcast_multiply_fusion.6), channel_id=1, replica_groups=mesh['section'=4,'dp'=2,'mp'=4] {'section','dp','mp'}, use_global_device_ids=true, to_apply=%region_45.46 | all-reduce | flops 6160 | bytes 49280 | tf_op jit(solution)/shard_map/psum | solution.py:424
  1313.9 224.3 %all-reduce.9.cloned.1.call-done = (bf16[3,768,192]{1,2,0:T(8,128)(2,1)}, bf16[192,768]{1,0:T(8,128)(2,1)}, bf16[2,768,192]{1,2,0:T(8,128)(2,1)}, bf16[192,768]{...) async-done(((bf16[3,768,192]{1,2,0:T(8,128)(2,1)}, bf16[192,768]{1,0:T(8,128)(2,1)}, bf16[2,768,192]{1,2,0:T(8,128)(2,1)}, ...) | async-done | bytes 6782992 | tf_op jit(solution)/shard_map/psum | solution.py:413
  (849 shorter events, 525.3 us)
Async XLA Ops:
  17.5 28.9 %all-gather.3.cloned.1.call-start = ((), (), s32[]{:S(2)}) async-start(), calls=%async_computation.4 | async-start | bytes 1966080 | tf_op jit(solution)/shard_map/while/body/eval_jaxpr/all_gather | solution.py:34
  23.9 74.3 %reduce-scatter.3.cloned.1.call-start = ((), (), s32[]{:S(2)}) async-start(), calls=%async_computation.5 | async-start | bytes 3932160 | tf_op jit(solution)/shard_map/while/body/eval_jaxpr/reduce_scatter | solution.py:38
  102.1 12.7 collective-permute-start
  114.9 24.5 %all-gather.3.cloned.1.call-start = ((), (), s32[]{:S(2)}) async-start(), calls=%async_computation.4 | async-start | bytes 1966080 | tf_op jit(solution)/shard_map/while/body/eval_jaxpr/all_gather | solution.py:34
  121.3 69.8 %reduce-scatter.3.cloned.1.call-start = ((), (), s32[]{:S(2)}) async-start(), calls=%async_computation.5 | async-start | bytes 3932160 | tf_op jit(solution)/shard_map/while/body/eval_jaxpr/reduce_scatter | solution.py:38
  195.1 12.7 collective-permute-start
  207.9 24.5 %all-gather.3.cloned.1.call-start = ((), (), s32[]{:S(2)}) async-start(), calls=%async_computation.4 | async-start | bytes 1966080 | tf_op jit(solution)/shard_map/while/body/eval_jaxpr/all_gather | solution.py:34
  214.3 69.8 %reduce-scatter.3.cloned.1.call-start = ((), (), s32[]{:S(2)}) async-start(), calls=%async_computation.5 | async-start | bytes 3932160 | tf_op jit(solution)/shard_map/while/body/eval_jaxpr/reduce_scatter | solution.py:38
  288.1 12.7 collective-permute-start
  300.9 24.5 %all-gather.3.cloned.1.call-start = ((), (), s32[]{:S(2)}) async-start(), calls=%async_computation.4 | async-start | bytes 1966080 | tf_op jit(solution)/shard_map/while/body/eval_jaxpr/all_gather | solution.py:34
  307.3 69.8 %reduce-scatter.3.cloned.1.call-start = ((), (), s32[]{:S(2)}) async-start(), calls=%async_computation.5 | async-start | bytes 3932160 | tf_op jit(solution)/shard_map/while/body/eval_jaxpr/reduce_scatter | solution.py:38
  381.1 12.7 collective-permute-start
  393.8 24.5 %all-gather.3.cloned.1.call-start = ((), (), s32[]{:S(2)}) async-start(), calls=%async_computation.4 | async-start | bytes 1966080 | tf_op jit(solution)/shard_map/while/body/eval_jaxpr/all_gather | solution.py:34
  400.3 69.8 %reduce-scatter.3.cloned.1.call-start = ((), (), s32[]{:S(2)}) async-start(), calls=%async_computation.5 | async-start | bytes 3932160 | tf_op jit(solution)/shard_map/while/body/eval_jaxpr/reduce_scatter | solution.py:38
  474.1 12.7 collective-permute-start
  499.1 28.7 %all-gather.5.cloned.1.call-start = ((), (), s32[]{:S(2)}) async-start(), calls=%async_computation.6 | async-start | bytes 1966080 | tf_op jit(solution)/shard_map/while/body/eval_jaxpr/all_gather | solution.py:42
  509.8 109.7 %reduce-scatter.5.cloned.1.call-start = ((), (), s32[]{:S(2)}) async-start(), calls=%async_computation.7 | async-start | bytes 3932160 | tf_op jit(solution)/shard_map/while/body/eval_jaxpr/reduce_scatter | solution.py:46
  621.0 20.2 %collective-permute-start.1 = (f32[2,128,768]{2,1,0:T(8,128)S(1)}, f32[2,128,768]{2,1,0:T(8,128)S(1)}, u32[]{:S(2)}, u32[]{:S(2)}) collective-permute-start(f32[2,128,768]{2,1,0:T(8,128)S(1)} %fusion.400), channel_id=1, source_target_pairs={{0,24},{8,0},{16,8},{24,16},{1,25},{9,1},{17,9},{25,17},{2,26},{10... | collective-permute-start | bytes 2359304 | tf_op jit(solution)/shard_map/while/body/eval_jaxpr/ppermute | solution.py:15
  642.2 31.5 %all-gather.5.cloned.1.call-start = ((), (), s32[]{:S(2)}) async-start(), calls=%async_computation.6 | async-start | bytes 1966080 | tf_op jit(solution)/shard_map/while/body/eval_jaxpr/all_gather | solution.py:42
  652.9 112.4 %reduce-scatter.5.cloned.1.call-start = ((), (), s32[]{:S(2)}) async-start(), calls=%async_computation.7 | async-start | bytes 3932160 | tf_op jit(solution)/shard_map/while/body/eval_jaxpr/reduce_scatter | solution.py:46
  766.8 20.2 %collective-permute-start.1 = (f32[2,128,768]{2,1,0:T(8,128)S(1)}, f32[2,128,768]{2,1,0:T(8,128)S(1)}, u32[]{:S(2)}, u32[]{:S(2)}) collective-permute-start(f32[2,128,768]{2,1,0:T(8,128)S(1)} %fusion.400), channel_id=1, source_target_pairs={{0,24},{8,0},{16,8},{24,16},{1,25},{9,1},{17,9},{25,17},{2,26},{10... | collective-permute-start | bytes 2359304 | tf_op jit(solution)/shard_map/while/body/eval_jaxpr/ppermute | solution.py:15
  788.2 31.5 %all-gather.5.cloned.1.call-start = ((), (), s32[]{:S(2)}) async-start(), calls=%async_computation.6 | async-start | bytes 1966080 | tf_op jit(solution)/shard_map/while/body/eval_jaxpr/all_gather | solution.py:42
  798.9 112.5 %reduce-scatter.5.cloned.1.call-start = ((), (), s32[]{:S(2)}) async-start(), calls=%async_computation.7 | async-start | bytes 3932160 | tf_op jit(solution)/shard_map/while/body/eval_jaxpr/reduce_scatter | solution.py:46
  912.8 20.2 %collective-permute-start.1 = (f32[2,128,768]{2,1,0:T(8,128)S(1)}, f32[2,128,768]{2,1,0:T(8,128)S(1)}, u32[]{:S(2)}, u32[]{:S(2)}) collective-permute-start(f32[2,128,768]{2,1,0:T(8,128)S(1)} %fusion.400), channel_id=1, source_target_pairs={{0,24},{8,0},{16,8},{24,16},{1,25},{9,1},{17,9},{25,17},{2,26},{10... | collective-permute-start | bytes 2359304 | tf_op jit(solution)/shard_map/while/body/eval_jaxpr/ppermute | solution.py:15
  934.3 31.5 %all-gather.5.cloned.1.call-start = ((), (), s32[]{:S(2)}) async-start(), calls=%async_computation.6 | async-start | bytes 1966080 | tf_op jit(solution)/shard_map/while/body/eval_jaxpr/all_gather | solution.py:42
  945.0 112.5 %reduce-scatter.5.cloned.1.call-start = ((), (), s32[]{:S(2)}) async-start(), calls=%async_computation.7 | async-start | bytes 3932160 | tf_op jit(solution)/shard_map/while/body/eval_jaxpr/reduce_scatter | solution.py:46
  1058.9 20.2 %collective-permute-start.1 = (f32[2,128,768]{2,1,0:T(8,128)S(1)}, f32[2,128,768]{2,1,0:T(8,128)S(1)}, u32[]{:S(2)}, u32[]{:S(2)}) collective-permute-start(f32[2,128,768]{2,1,0:T(8,128)S(1)} %fusion.400), channel_id=1, source_target_pairs={{0,24},{8,0},{16,8},{24,16},{1,25},{9,1},{17,9},{25,17},{2,26},{10... | collective-permute-start | bytes 2359304 | tf_op jit(solution)/shard_map/while/body/eval_jaxpr/ppermute | solution.py:15
  1080.2 31.5 %all-gather.5.cloned.1.call-start = ((), (), s32[]{:S(2)}) async-start(), calls=%async_computation.6 | async-start | bytes 1966080 | tf_op jit(solution)/shard_map/while/body/eval_jaxpr/all_gather | solution.py:42
  1090.9 112.4 %reduce-scatter.5.cloned.1.call-start = ((), (), s32[]{:S(2)}) async-start(), calls=%async_computation.7 | async-start | bytes 3932160 | tf_op jit(solution)/shard_map/while/body/eval_jaxpr/reduce_scatter | solution.py:46
  1204.8 20.2 %collective-permute-start.1 = (f32[2,128,768]{2,1,0:T(8,128)S(1)}, f32[2,128,768]{2,1,0:T(8,128)S(1)}, u32[]{:S(2)}, u32[]{:S(2)}) collective-permute-start(f32[2,128,768]{2,1,0:T(8,128)S(1)} %fusion.400), channel_id=1, source_target_pairs={{0,24},{8,0},{16,8},{24,16},{1,25},{9,1},{17,9},{25,17},{2,26},{10... | collective-permute-start | bytes 2359304 | tf_op jit(solution)/shard_map/while/body/eval_jaxpr/ppermute | solution.py:15
  1229.3 82.2 %all-reduce.11.cloned.1.call-start = ((), (), s32[]{:S(2)}) async-start(), calls=%async_computation.3 | async-start | bytes 3145728 | tf_op jit(solution)/shard_map/psum | solution.py:428
  1229.8 308.3 %all-reduce.9.cloned.1.call-start = ((), (), s32[]{:S(2)}) async-start(), calls=%async_computation.2 | async-start | bytes 13565952 | tf_op jit(solution)/shard_map/psum | solution.py:413
  (222 other events, 3439.7 us)
Sparse Core Ops, SparseCore 0:
  24.0 22.3 all-gather.2
  53.9 44.2 reduce-scatter.2
  121.5 17.8 all-gather.2
  146.9 44.2 reduce-scatter.2
  214.5 17.8 all-gather.2
  239.9 44.2 reduce-scatter.2
  307.4 17.8 all-gather.2
  332.9 44.2 reduce-scatter.2
  400.4 17.8 all-gather.2
  425.8 44.2 reduce-scatter.2
  509.9 17.8 all-gather.4
  561.6 57.8 reduce-scatter.4
  653.1 20.6 all-gather.4
  707.4 57.9 reduce-scatter.4
  799.0 20.5 all-gather.4
  853.1 58.2 reduce-scatter.4
  945.1 20.6 all-gather.4
  999.6 57.8 reduce-scatter.4
  1091.0 20.6 all-gather.4
  1145.3 57.9 reduce-scatter.4
Sparse Core Ops, SparseCore 1:
  1232.7 71.5 all-reduce.10
  1310.5 227.7 all-reduce.8
where the time goes:
time: 1580 us; the launch traced here: 1560 us
  waiting for transfers between devices  1000 us (63%)
  other arithmetic  154 us (10%)
  local copies, waits for them, and re-layouts  116 us (7%)
  matrix products  105 us (7%)
  loops' own time  76.6 us (5%)
  blocking collectives  62.9 us (4%)
  starting transfers between devices  25.4 us (2%)
  between operations  16.8 us (1%)
    reduce_scatter x5, waiting for transfers between devices, input_total(): lax.psum_scatter(partial_value, 'mp', scatter_dimension=1, tiled=True)  288 us
    psum x1, waiting for transfers between devices, on_device(): lax.psum(grad_qkv.astype(jnp.bfloat16), ('section', 'dp'))  224 us
    reduce_scatter x5, waiting for transfers between devices, branch_total(): lax.psum_scatter(partial_value, 'mp', scatter_dimension=1, tiled=True)  194 us
    ppermute x10, waiting for transfers between devices, shifted(): lax.ppermute(array, axis, [(i, (i + by) % peers) for i in range(peers)])  115 us
    all_gather x5, waiting for transfers between devices, spread_rows(): return lax.all_gather(shard, 'mp', axis=1, tiled=True)  94.4 us
    all_gather x5, waiting for transfers between devices, grad_rows(): return lax.all_gather(shard.astype(jnp.bfloat16), 'mp', axis=1, tiled=True)  87 us
    another operation x5, loops' own time, switch_back(): lax.switch(block_pos, back_fns, hidden, grad_full, grad_state, active)  41.1 us
    psum x1, blocking collectives, on_device(): lax.psum((gain_acc, bias_acc, replica_rows), ('section', 'dp', 'mp'))  39.5 us
  transfers between devices with their start and end apart: 32, of which 31 were waited for; matrix products, arithmetic and copies ran while one was open for 5% of the time, Pallas kernels for 0%

commit v1 on v0

v1 whole, which is shorter than its diff:
```python
import functools
import math

import jax
import jax.numpy as jnp
from jax import lax
from jax.experimental import pallas as pl
from jax.experimental.pallas import tpu as pltpu
from jax.sharding import PartitionSpec as P

HEAD = 64
TAPS = 7
MARGIN = TAPS // 2
EPSILON = 1e-05
SECTIONS = 4
GROUP = 4
PAD = 8
TILE = 32
LANES = 256

F32 = jnp.float32
BF16 = jnp.bfloat16
MESH = pl.DeviceIdType.MESH


def dot(left, right):
    return jnp.dot(left, right, preferred_element_type=F32)


def dot_lanes(left, right):
    return lax.dot_general(left, right, (((1,), (1,)), ((), ())), preferred_element_type=F32)


def dot_rows(left, right):
    return lax.dot_general(left, right, (((0,), (0,)), ((), ())), preferred_element_type=F32)


def round_up(value, step):
    return (value + step - 1) // step * step


def normalise(summed):
    centre = summed - jnp.mean(summed, axis=-1, keepdims=True)
    variance = jnp.mean(centre * centre, axis=-1, keepdims=True)
    inverse = lax.rsqrt(variance + EPSILON)
    return centre * inverse, inverse


def norm_pull(grad_out, normed, inverse, gain_row):
    scaled = grad_out * gain_row
    first = jnp.mean(scaled, axis=-1, keepdims=True)
    second = jnp.mean(scaled * normed, axis=-1, keepdims=True)
    return inverse * (scaled - first - normed * second)


def gelu_parts(before):
    cdf = 0.5 * (1.0 + lax.erf(before * math.sqrt(0.5)))
    slope = cdf + before * jnp.exp(-0.5 * before * before) * (1.0 / math.sqrt(2.0 * math.pi))
    return before * cdf, slope


def two_terms(values):
    high = values.astype(BF16)
    return high, (values - high.astype(F32)).astype(BF16)


def fold(rows):
    count, width = rows.shape
    return jnp.sum(rows.reshape(count // 8, 8, width), axis=0)


def whole_sum(values):
    return jnp.sum(values, axis=(0, 1), keepdims=True)


class Layout:
    def __init__(self, dp, seq, width, heads_width, hidden, marked):
        self.dp, self.seq, self.width = dp, seq, width
        self.heads_width, self.hidden = heads_width, hidden
        self.marked = marked
        self.part = seq // GROUP
        self.chunk = 2 * self.part
        unit = 16 * dp
        conv_rows = round_up(3 * heads_width + 16, max(unit, 128))
        self.conv_at, at = 0, conv_rows
        self.up_at, at = at, at + width
        self.down_at, at = at, at + hidden
        self.attn_at, at = at, at + 4 * heads_width
        self.rows = at
        self.kernel_at = self.conv_at + 3 * heads_width
        self.pieces = {
            "conv": self.cut(self.conv_at, conv_rows, 1),
            "up": self.cut(self.up_at, width, 2),
            "down": self.cut(self.down_at, hidden, 2),
            "attn": self.cut(self.attn_at, 4 * heads_width, 2),
        }
        self.bits = dp.bit_length() - 1
        assert dp == 1 << self.bits and dp <= 8
        self.misc_rows = 16
        self.sets = 3 if dp <= 2 else 2

    def cut(self, start, rows, count):
        step = rows // count
        assert step * count == rows and step % (16 * self.dp) == 0
        return [(start + i * step, step) for i in range(count)]


def main_kernel(
    lay,
    x_in,
    qkv_in,
    ao_in,
    cin_in,
    co_in,
    up_in,
    down_in,
    gain,
    bias,
    tap_weight,
    tap_on,
    where,
    cotangent,
    used,
    final,
    up1_grad,
    down1_grad,
    layer_rows,
    input_rows,
    misc_out,
    wqkv,
    wao,
    wcin,
    wco,
    wup,
    wdown,
    hid,
    dfull,
    normed,
    inverse,
    qkv,
    probs,
    mix,
    dmix,
    dqkv,
    dkv,
    units,
    slope,
    dbefore,
    value,
    sig,
    gated,
    conv,
    dconv,
    dgates,
    hits,
    mh,
    mnorm,
    mslope,
    munits,
    mdz,
    partial,
    cs,
    cr,
    ys,
    yr,
    ms,
    mr,
    mys,
    myr,
    grads,
    xr,
    za,
    zb,
    factors,
    misc,
    misc_in,
    load_sem,
    send_sem,
    recv_sem,
):
    section, replica, member = (
        lax.axis_index("section"),
        lax.axis_index("dp"),
        lax.axis_index("mp"),
    )
    low = lax.rem(member, 2)
    high = lax.div(member, 2)
    part, chunk, width = lay.part, lay.chunk, lay.width
    hw, marked = lay.heads_width, lay.marked
    local_heads = hw // HEAD
    scale = HEAD ** (-0.5)
    side = (section, replica, member + 1 - 2 * low)
    across = (section, replica, lax.rem(member + 2, GROUP))
    is_end = (section == 0) | (section == SECTIONS - 1)
    is_inner = jnp.logical_not(is_end)
    inner_of = jnp.where(section == 0, 1, SECTIONS - 2)
    end_of = jnp.where(section == 1, 0, SECTIONS - 1)
    other_inner = SECTIONS - 1 - section
    counter = [0]
    closing = []
    leaving = {}

    def section_peer(by):
        return (lax.rem(section + by, SECTIONS), replica, member)

    def replica_peer(by):
        return (section, lax.rem(replica + by, lay.dp), member)

    def replica_bit(bit):
        on = lax.rem(lax.div(replica, 1 << bit), 2)
        return (section, replica + (1 - 2 * on) * (1 << bit), member), on

    def slots(count=1):
        at = counter[0]
        counter[0] += count
        return at

    def remote(src, dst, target, slot):
        return pltpu.make_async_remote_copy(
            src_ref=src,
            dst_ref=dst,
            send_sem=send_sem.at[slot],
            recv_sem=recv_sem.at[slot],
            device_id=target,
            device_id_type=MESH,
        )

    def send(src, dst, target, slot=None):
        copy = remote(src, dst, target, slots() if slot is None else slot)
        copy.start()
        closing.append(copy.wait_send)
        return copy

    def send_slot(name, ref, e, t, dst, target, slot=None):
        copy = remote(ref.at[e % lay.sets, t], dst.at[e % lay.sets, t], target, slots() if slot is None else slot)
        copy.start()
        leaving[name, e % lay.sets, t] = copy.wait_send
        return copy

    def reuse(name, e, t):
        wait = leaving.pop((name, e % lay.sets, t), None)
        if wait is not None:
            wait()

    barrier = pltpu.get_barrier_semaphore()
    peers = (
        [side, across]
        + [section_peer(by) for by in range(1, SECTIONS)]
        + [replica_peer(by) for by in range(1, lay.dp)]
    )
    for peer in peers:
        pl.semaphore_signal(barrier, inc=1, device_id=peer, device_id_type=MESH)

    loads = {}
    for at, (name, src, dst) in enumerate(
        [
            ("x", x_in.at[section], hid.at[0, pl.ds(pl.multiple_of(member * part, part), part)]),
            ("qkv", qkv_in, wqkv),
            ("ao", ao_in, wao),
            ("up", up_in, wup),
            ("down", down_in, wdown),
            ("cin", cin_in, wcin),
            ("co", co_in, wco),
        ]
    ):
        copy = pltpu.make_async_copy(src, dst, load_sem.at[at])
        copy.start()
        loads[name] = copy

    misc[...] = jnp.zeros_like(misc)
    lane = lax.broadcasted_iota(jnp.int32, (1, hw), 1)
    head_lanes = [(lane >= HEAD * i) & (lane < HEAD * (i + 1)) for i in range(local_heads)]
    head_low = [jnp.where(on, 1.0, 0.0).astype(BF16) for on in head_lanes]

    def block(at, size):
        return pl.ds(pl.multiple_of(at, size), size)

    def own_rows(t):
        return block(chunk * t + part * low, part)

    def other_rows(t):
        return block(chunk * t + part * (1 - low), part)

    def tiles(count, body, init=0):
        return lax.fori_loop(0, count, body, init)

    def exchange_send(e, t):
        reuse("cs", e, t)
        reuse("ys", e, t)
        at = e % lay.sets

        def body(i, carry):
            rows = block(i * TILE, TILE)
            cs[at, t, rows] = partial[block(part * (1 - low) + i * TILE, TILE)].astype(BF16)
            return carry

        tiles(part // TILE, body)
        copy = send_slot("cs", cs, e, t, cr, side)

        def body(i, carry):
            rows = block(i * TILE, TILE)
            ys[at, t, rows] = partial[block(part * low + i * TILE, TILE)].astype(BF16)
            return carry

        tiles(part // TILE, body)
        return copy

    def sums_across(e, t, core_copy, start=True):
        core_copy.wait_recv()
        at = e % lay.sets

        def body(i, carry):
            rows = block(i * TILE, TILE)
            ys[at, t, rows] = (ys[at, t, rows].astype(F32) + cr[at, t, rows].astype(F32)).astype(BF16)
            return carry

        tiles(part // TILE, body)
        if start:
            return send_slot("ys", ys, e, t, yr, across)

    def total_tile(e, t, rows):
        return ys[e % lay.sets, t, rows].astype(F32) + yr[e % lay.sets, t, rows].astype(F32)

    def send_half(e):
        slot = slots()
        at = e % lay.sets
        out = remote(ys.at[at, 1 - high], yr.at[at, 1 - high], across, slot)
        out.start()
        leaving["ys", at, 0] = out.wait_send
        return remote(ys.at[at, high], yr.at[at, high], across, slot)

    def add_stat(column, amount):
        cell = (lax.broadcasted_iota(jnp.int32, (8, width), 0) == replica) & (
            lax.broadcasted_iota(jnp.int32, (8, width), 1) == column
        )
        misc[8:16] += jnp.where(cell, amount, 0.0)

    def run_exchange(e, work, finish, during=None):
        core, y = [None, None], [None, None]
        for t in range(2):
            work(t)
            core[t] = exchange_send(e, t)
            if t == 1:
                y[0] = sums_across(e, 0, core[0])
        y[1] = sums_across(e, 1, core[1])
        if during is not None:
            during()
        last = []
        for t in range(2):
            y[t].wait_recv()
            last.append(finish(t))
        return last

    def forward_finish(e, k, keep_normed):
        def finish(t):
            at = chunk * t + part * low

            def body(i, carry):
                rows = block(i * TILE, TILE)
                place = block(at + i * TILE, TILE)
                stream = hid[k, place].astype(F32)
                branch = total_tile(e, t, rows)
                norm, inv = normalise(stream + branch)
                if keep_normed:
                    normed[k, t, rows] = norm
                    inverse[k, t, rows] = inv
                hid[k + 1, place] = (norm * gain[k : k + 1] + bias[k : k + 1]).astype(BF16)
                return (carry[0] + fold(stream * stream), carry[1] + fold(branch * branch))

            zero = jnp.zeros((8, width), F32)
            squares = tiles(part // TILE, body, (zero, zero))

            @pl.when(high == t)
            def _():
                add_stat(k, whole_sum(squares[0]) * used[0:1, 0:1])
                add_stat(4 + k, whole_sum(squares[1]) * used[0:1, 0:1])

            rows = own_rows(t)
            return send(hid.at[k + 1, rows], hid.at[k + 1, rows], side)

        return finish

    def norm_back_rows(k, t, grad_tile):
        at = chunk * t + part * low

        def body(i, carry):
            rows = block(i * TILE, TILE)
            dy = grad_tile(rows, block(at + i * TILE, TILE))
            norm = normed[k, t, rows]
            result = norm_pull(dy, norm, inverse[k, t, rows], gain[k : k + 1])
            normed[k, t, rows] = result
            dfull[k, block(at + i * TILE, TILE)] = result.astype(BF16)
            return (carry[0] + fold(dy * norm), carry[1] + fold(dy))

        zero = jnp.zeros((8, width), F32)
        terms = tiles(part // TILE, body, (zero, zero))

        @pl.when(high == t)
        def _():
            misc[k : k + 1] += jnp.sum(terms[0], axis=0, keepdims=True)
            misc[4 + k : 5 + k] += jnp.sum(terms[1], axis=0, keepdims=True)

        rows = own_rows(t)
        return send(dfull.at[k, rows], dfull.at[k, rows], side)

    def marked_total(e, values):
        ms[e] = values.astype(BF16)
        core = send(ms.at[e], mr.at[e], side)
        core.wait_recv()
        mys[e] = (ms[e].astype(F32) + mr[e].astype(F32)).astype(BF16)
        y = send(mys.at[e], myr.at[e], across)
        y.wait_recv()
        return mys[e].astype(F32) + myr[e].astype(F32)

    def reduce_piece(start, rows):
        xr_at, z_at = reduce_piece.xr_at, reduce_piece.z_at
        reduce_piece.xr_at += rows - rows // lay.dp
        reduce_piece.z_at += rows // lay.dp
        first, size = start, rows
        steps = []
        for bit in reversed(range(lay.bits)):
            half = size // 2
            peer, on = replica_bit(bit)
            keep = first + on * half
            give = first + (1 - on) * half
            copy = send(
                grads.at[pl.ds(pl.multiple_of(give, 16), half)],
                xr.at[pl.ds(xr_at, half)],
                peer,
            )
            yield
            copy.wait_recv()
            step = math.gcd(half, 64)

            def body(i, carry, keep=keep, xr_at=xr_at, step=step):
                here = pl.ds(pl.multiple_of(keep + i * step, 16), step)
                there = pl.ds(pl.multiple_of(xr_at + i * step, 16), step)
                grads[here] = (grads[here].astype(F32) + xr[there].astype(F32)).astype(BF16)
                return carry

            tiles(half // step, body)
            xr_at += half
            steps.append((first, size, keep, give, half, peer))
            first, size = keep, half
        mine = pl.ds(pl.multiple_of(first, 16), size)
        z_rows = pl.ds(z_at, size)
        step = math.gcd(size, 64)
        slot_a, slot_b, slot_c = slots(), slots(), slots()

        def z_copy(kind):
            if kind == "a":
                return remote(
                    grads.at[mine], za.at[z_rows], (inner_of, replica, member), slot_a
                )
            if kind == "b":
                return remote(
                    grads.at[mine], zb.at[z_rows], (other_inner, replica, member), slot_b
                )
            return remote(final.at[mine], final.at[mine], (end_of, replica, member), slot_c)

        @pl.when(is_end)
        def _():
            z_copy("a").start()

        yield

        @pl.when(is_inner)
        def _():
            z_copy("a").wait_recv()

            def body(i, carry):
                here = pl.ds(pl.multiple_of(first + i * step, 16), step)
                there = pl.ds(pl.multiple_of(z_at + i * step, 16), step)
                grads[here] = (grads[here].astype(F32) + za[there].astype(F32)).astype(BF16)
                return carry

            tiles(size // step, body)
            z_copy("b").start()

        yield

        @pl.when(is_inner)
        def _():
            z_copy("b").wait_recv()

            def body(i, carry):
                here = pl.ds(pl.multiple_of(first + i * step, 16), step)
                there = pl.ds(pl.multiple_of(z_at + i * step, 16), step)
                final[here] = (grads[here].astype(F32) + zb[there].astype(F32)).astype(BF16)
                return carry

            tiles(size // step, body)
            z_copy("c").start()

        yield

        @pl.when(is_end)
        def _():
            z_copy("c").wait_recv()

        for first, size, keep, give, half, peer in reversed(steps):
            here = pl.ds(pl.multiple_of(keep, 16), half)
            there = pl.ds(pl.multiple_of(give, 16), half)
            slot = slots()
            out = remote(final.at[here], final.at[here], peer, slot)
            out.start()
            closing.append(out.wait_send)
            yield
            remote(final.at[there], final.at[there], peer, slot).wait_recv()

        def close():
            @pl.when(is_end)
            def _():
                z_copy("a").wait_send()

            @pl.when(is_inner)
            def _():
                z_copy("b").wait_send()
                z_copy("c").wait_send()

        closing.append(close)

    reduce_piece.xr_at = 0
    reduce_piece.z_at = 0
    running = []

    def launch(name):
        for start, rows in lay.pieces[name]:
            piece = reduce_piece(start, rows)
            next(piece)
            running.append(piece)

    def pump(count=1):
        for _ in range(count):
            for piece in list(running):
                try:
                    next(piece)
                except StopIteration:
                    running.remove(piece)

    pl.semaphore_wait(barrier, len(peers))
    loads["x"].wait()
    mine = block(member * part, part)
    to_side = send(hid.at[0, mine], hid.at[0, mine], side)
    to_across = send(hid.at[0, mine], hid.at[0, mine], across)
    hits[...] = jnp.where(
        lax.broadcasted_iota(jnp.int32, hits.shape, 0) == where[0:1, 0 : hits.shape[1]], 1.0, 0.0
    ).astype(BF16)
    loads["qkv"].wait()

    def project(at):
        rows = block(at, part)
        for j in range(3):
            qkv[j, rows] = dot(hid[0, rows], wqkv[j]).astype(BF16)

    project(member * part)
    to_side.wait_recv()
    project(side[2] * part)
    to_across.wait_recv()
    theirs = block(across[2] * part, part)
    onward = send(hid.at[0, theirs], hid.at[0, theirs], side)
    project(across[2] * part)
    onward.wait_recv()
    project(lax.rem(side[2] + 2, GROUP) * part)
    loads["ao"].wait()

    def attention_work(t):
        rows = pl.ds(chunk * t, chunk)
        mixture = jnp.zeros((chunk, hw), F32)
        for i in range(local_heads):
            scores = dot_lanes(qkv[0, rows] * head_low[i], qkv[1]) * scale
            top = jnp.max(scores, axis=-1, keepdims=True)
            powers = jnp.exp(scores - top)
            chances = powers * (1.0 / jnp.sum(powers, axis=-1, keepdims=True))
            probs[i, rows] = chances
            mixture = mixture + jnp.where(head_lanes[i], dot(chances.astype(BF16), qkv[2]), 0.0)
        mix[rows] = mixture.astype(BF16)
        partial[...] = dot(mix[rows], wao[...])

    gathered = run_exchange(0, attention_work, forward_finish(0, 0, True))

    loads["up"].wait()
    loads["down"].wait()

    def ffn_forward(layer, src, rows, keep):
        def body(i, carry):
            lanes = block(i * LANES, LANES)
            unit, slope_here = gelu_parts(dot(src[rows], wup[layer, :, lanes]))
            units[rows, lanes] = unit.astype(BF16)
            if keep:
                slope[rows, lanes] = slope_here
            return carry

        tiles(lay.hidden // LANES, body)
        partial[...] = dot(units[rows], wdown[layer])

    def ffn0_work(t):
        gathered[t].wait_recv()
        ffn_forward(0, hid.at[1], pl.ds(chunk * t, chunk), True)

    gathered = run_exchange(1, ffn0_work, forward_finish(1, 1, True))

    loads["cin"].wait()
    loads["co"].wait()
    edge = jnp.zeros((PAD, hw), F32)
    for buffer in (gated, dconv):
        buffer[0:PAD] = edge
        buffer[PAD + lay.seq : 2 * PAD + lay.seq] = edge
    for t in range(2):
        gathered[t].wait_recv()
        rows = pl.ds(chunk * t, chunk)
        value_here = dot(hid[2, rows], wcin[0])
        sig_here = jax.nn.sigmoid(dot(hid[2, rows], wcin[1]))
        value[rows] = value_here
        sig[rows] = sig_here
        gated[pl.ds(PAD + chunk * t, chunk)] = value_here * sig_here
    tap_tile = 64

    def taps(i, carry):
        total = jnp.zeros((tap_tile, hw), F32)
        window = gated[pl.ds(pl.multiple_of(i * tap_tile, 8), tap_tile + 2 * PAD)]
        for j in range(TAPS):
            at = PAD - MARGIN + j
            total = total + tap_weight[j : j + 1] * window[at : at + tap_tile]
        conv[block(i * tap_tile, tap_tile)] = total.astype(BF16)
        return carry

    tiles(lay.seq // tap_tile, taps)

    spots = hits[...]
    conv_marked = dot_rows(spots, conv[...]).astype(BF16)
    stream = dot_rows(spots, hid[2])
    branch = marked_total(0, dot(conv_marked, wco[...]))
    norm2, inv2 = normalise(stream + branch)
    mnorm[0] = norm2
    mh[...] = (norm2 * gain[2:3] + bias[2:3]).astype(BF16)

    def marked_up(i, carry):
        lanes = block(i * LANES, LANES)
        unit, slope_here = gelu_parts(dot(mh[...], wup[1, :, lanes]))
        munits[:, lanes] = unit.astype(BF16)
        mslope[:, lanes] = slope_here
        return carry

    tiles(lay.hidden // LANES, marked_up)
    branch = marked_total(1, dot(munits[...], wdown[1]))
    norm3, inv3 = normalise(mh[...].astype(F32) + branch)
    once = jnp.where(member == 0, 1.0, 0.0).astype(F32)
    dy = cotangent[...].astype(F32)
    misc[3:4] += once * jnp.sum(dy * norm3, axis=0, keepdims=True)
    misc[7:8] += once * jnp.sum(dy, axis=0, keepdims=True)
    dz3 = norm_pull(dy, norm3, inv3, gain[3:4])
    mdz[0] = dz3
    df3 = dz3.astype(BF16)

    per_section = lay.dp * marked
    here = pl.ds(pl.multiple_of(section * per_section + replica * marked, 16), marked)
    factors[0, here] = mh[...]
    factors[1, here] = df3
    factor_copies = [
        send(factors.at[low, here], factors.at[low, here], replica_peer(by))
        for by in range(1, lay.dp)
    ]

    def marked_down(i, carry):
        lanes = block(i * LANES, LANES)
        grad_units = dot_lanes(factors[1, here], wdown[1, lanes])
        munits[:, lanes] = (grad_units * mslope[:, lanes]).astype(BF16)
        return carry

    tiles(lay.hidden // LANES, marked_down)
    dy = mdz[0] + marked_total(2, dot_lanes(munits[...], wup[1]))
    for copy in factor_copies:
        copy.wait_recv()
    ours = pl.ds(pl.multiple_of(section * per_section, 16), per_section)
    factor_copies = [
        send(factors.at[low, ours], factors.at[low, ours], section_peer(by))
        for by in range(1, SECTIONS)
    ]
    norm2 = mnorm[0]
    misc[2:3] += once * jnp.sum(dy * norm2, axis=0, keepdims=True)
    misc[6:7] += once * jnp.sum(dy, axis=0, keepdims=True)
    dz2 = norm_pull(dy, norm2, inv2, gain[2:3])
    dz2_terms = two_terms(dz2)
    mdz[1] = dz2
    df2 = dz2.astype(BF16)

    def spread(rows, terms):
        where_rows = hits[rows]
        return dot(where_rows, terms[0]) + dot(where_rows, terms[1])

    dconv_terms = two_terms(dot_lanes(df2, wco[...]))
    dconv[pl.ds(PAD, lay.seq)] = spread(pl.ds(0, lay.seq), dconv_terms)

    def taps_back(i, carry):
        total = jnp.zeros((tap_tile, hw), F32)
        place = pl.ds(pl.multiple_of(i * tap_tile, 8), tap_tile + 2 * PAD)
        window = dconv[place]
        around = gated[place]
        middle = window[PAD : PAD + tap_tile]
        sums = []
        for j in range(TAPS):
            at = PAD + MARGIN - j
            total = total + tap_weight[j : j + 1] * window[at : at + tap_tile]
            at = PAD - MARGIN + j
            sums.append(jnp.sum(around[at : at + tap_tile] * middle, axis=0, keepdims=True))
        rows = block(i * tap_tile, tap_tile)
        s = sig[rows]
        by_value = total * s
        dgates[0, rows] = by_value.astype(BF16)
        dgates[1, rows] = (by_value * value[rows] * (1.0 - s)).astype(BF16)
        sums.append(jnp.zeros((1, hw), F32))
        return carry + jnp.concatenate(sums, axis=0)

    kernel_rows = tiles(lay.seq // tap_tile, taps_back, jnp.zeros((8, hw), F32)) * tap_on[...]
    grads[pl.ds(lay.kernel_at, lay.up_at - lay.kernel_at)] = jnp.zeros(
        (lay.up_at - lay.kernel_at, width), BF16
    )
    grads[pl.ds(lay.kernel_at, 16), 0:hw] = jnp.concatenate(
        [kernel_rows, jnp.zeros((8, hw), F32)], axis=0
    ).astype(BF16)
    for j in range(2):
        grads[pl.ds(lay.conv_at + j * hw, hw)] = dot_rows(dgates[j], hid[2]).astype(BF16)
    grads[pl.ds(lay.conv_at + 2 * hw, hw)] = dot_rows(conv_marked, df2).astype(BF16)
    launch("conv")

    def conv_back_work(t):
        rows = pl.ds(chunk * t, chunk)
        partial[...] = dot_lanes(dgates[0, rows], wcin[0]) + dot_lanes(dgates[1, rows], wcin[1])

    def conv_back_finish(t):
        def grad_tile(rows, place):
            return total_tile(2, t, rows) + spread(place, dz2_terms)

        return norm_back_rows(1, t, grad_tile)

    gathered = run_exchange(2, conv_back_work, conv_back_finish)

    def ffn0_back_work(t):
        gathered[t].wait_recv()
        rows = pl.ds(chunk * t, chunk)

        def body(i, carry):
            lanes = block(i * LANES, LANES)
            grad_units = dot_lanes(dfull[1, rows], wdown[0, lanes])
            dbefore[rows, lanes] = (grad_units * slope[rows, lanes]).astype(BF16)
            return carry

        tiles(lay.hidden // LANES, body)
        partial[...] = dot_lanes(dbefore[rows], wup[0])

    def ffn0_back_finish(t):
        return norm_back_rows(
            0, t, lambda rows, place: normed[1, t, rows] + total_tile(3, t, rows)
        )

    def weight_rows(start, left, right, count):
        def body(i, carry):
            lanes = block(i * LANES, LANES)
            grads[pl.ds(pl.multiple_of(start + i * LANES, 16), LANES)] = dot_rows(
                left[:, lanes], right[...]
            ).astype(BF16)
            return carry

        tiles(count // LANES, body)

    def ffn0_weights():
        pump()
        weight_rows(lay.up_at, hid.at[1], dbefore, width)
        launch("up")
        pump()
        weight_rows(lay.down_at, units0, dfull.at[1], lay.hidden)
        launch("down")

    units0 = units
    gathered = run_exchange(3, ffn0_back_work, ffn0_back_finish, ffn0_weights)

    dkv[...] = jnp.zeros_like(dkv)
    for t in range(2):
        gathered[t].wait_recv()
        rows = pl.ds(chunk * t, chunk)
        dmix[rows] = dot_lanes(dfull[0, rows], wao[...]).astype(BF16)
        grad_queries = jnp.zeros((chunk, hw), F32)
        for i in range(local_heads):
            chances = probs[i, rows]
            grad_chances = dot_lanes(dmix[rows] * head_low[i], qkv[2])
            grad_scores = chances * (
                grad_chances - jnp.sum(grad_chances * chances, axis=-1, keepdims=True)
            )
            grad_scores = grad_scores.astype(BF16)
            on = head_lanes[i]
            grad_queries = grad_queries + jnp.where(on, dot(grad_scores, qkv[1]), 0.0)
            dkv[0] += jnp.where(on, dot_rows(grad_scores, qkv[0, rows]), 0.0)
            dkv[1] += jnp.where(on, dot_rows(chances.astype(BF16), dmix[rows]), 0.0)
        dqkv[0, rows] = (grad_queries * scale).astype(BF16)
        pump()
    dqkv[1] = (dkv[0] * scale).astype(BF16)
    dqkv[2] = dkv[1].astype(BF16)

    def attention_back_work(t):
        rows = pl.ds(chunk * t, chunk)
        partial[...] = (
            dot_lanes(dqkv[0, rows], wqkv[0])
            + dot_lanes(dqkv[1, rows], wqkv[1])
            + dot_lanes(dqkv[2, rows], wqkv[2])
        )

    core = []
    for t in range(2):
        attention_back_work(t)
        core.append(exchange_send(4, t))
    for t in range(2):
        sums_across(4, t, core[t], start=False)
    last = send_half(4)
    for j in range(3):
        grads[pl.ds(lay.attn_at + j * hw, hw)] = dot_rows(dqkv[j], hid[0]).astype(BF16)
    grads[pl.ds(lay.attn_at + 3 * hw, hw)] = dot_rows(mix[...], dfull[0]).astype(BF16)
    launch("attn")
    pump()
    last.wait_recv()

    def input_body(i, carry):
        rows = block(i * TILE, TILE)
        total = total_tile(4, high, rows)
        input_rows[section, rows] = (normed[0, high, rows] + total).astype(BF16)
        return carry

    tiles(part // TILE, input_body)
    end_copies = [
        send(input_rows.at[section], input_rows.at[section], section_peer(by))
        for by in range(1, SECTIONS)
    ]
    pump()

    def conv_work(t):
        partial[...] = dot(conv[pl.ds(chunk * t, chunk)], wco[...])

    gathered = run_exchange(5, conv_work, forward_finish(5, 2, False), pump)
    core = []
    for t in range(2):
        gathered[t].wait_recv()
        ffn_forward(1, hid.at[3], pl.ds(chunk * t, chunk), False)
        core.append(exchange_send(6, t))
        pump()
    for t in range(2):
        sums_across(6, t, core[t], start=False)
    last = send_half(6)
    pump()

    for copy in factor_copies:
        copy.wait_recv()
    shared = slots()
    send(factors.at[low], factors.at[low], side, shared)
    remote(factors.at[1 - low], factors.at[1 - low], side, shared).wait_recv()
    group_rows = GROUP * marked
    for group in range(SECTIONS * per_section // group_rows):
        rows = pl.ds(group * group_rows, group_rows)

        def recompute(j, carry):
            lanes = block(j * LANES, LANES)
            unit, slope_here = gelu_parts(dot(factors[0, rows], wup[1, :, lanes]))
            units[0:group_rows, lanes] = unit.astype(BF16)
            grad_units = dot_lanes(factors[1, rows], wdown[1, lanes])
            dbefore[0:group_rows, lanes] = (grad_units * slope_here).astype(BF16)
            return carry

        tiles(lay.hidden // LANES, recompute)

        def last_weights(i, carry):
            lanes = block(i * LANES, LANES)
            by_up = dot_rows(factors[0, rows, lanes], dbefore[0:group_rows])
            by_down = dot_rows(units[0:group_rows, lanes], factors[1, rows])
            if group == 0:
                up1_grad[lanes] = by_up
                down1_grad[lanes] = by_down
            else:
                up1_grad[lanes] += by_up
                down1_grad[lanes] += by_down
            return carry

        tiles(width // LANES, last_weights)
        pump()
    last.wait_recv()

    def layer_body(i, carry):
        rows = block(i * TILE, TILE)
        stream = hid[3, block(member * part + i * TILE, TILE)].astype(F32)
        branch = total_tile(6, high, rows)
        norm, _ = normalise(stream + branch)
        result = (norm * gain[3:4] + bias[3:4]) * used[0:1, 0:1]
        layer_rows[section, rows] = result.astype(BF16)
        return (carry[0] + fold(stream * stream), carry[1] + fold(branch * branch))

    zero = jnp.zeros((8, width), F32)
    squares = tiles(part // TILE, layer_body, (zero, zero))
    add_stat(3, whole_sum(squares[0]) * used[0:1, 0:1])
    add_stat(7, whole_sum(squares[1]) * used[0:1, 0:1])
    end_copies += [
        send(layer_rows.at[section], layer_rows.at[section], section_peer(by))
        for by in range(1, SECTIONS)
    ]

    hops = [side, across] + [replica_bit(bit)[0] for bit in range(lay.bits)]
    for at, peer in enumerate(hops):
        misc_in[2 * at] = misc[...]
        copy = send(misc_in.at[2 * at], misc_in.at[2 * at + 1], peer)
        pump()
        copy.wait_recv()
        misc[...] = misc_in[2 * at] + misc_in[2 * at + 1]
    at = 2 * len(hops)
    slot_a, slot_b, slot_c = slots(), slots(), slots()
    to_inner = remote(misc_in.at[at], misc_in.at[at + 1], (inner_of, replica, member), slot_a)
    to_other = remote(misc_in.at[at + 2], misc_in.at[at + 3], (other_inner, replica, member), slot_b)
    to_end = remote(misc_out, misc_out, (end_of, replica, member), slot_c)

    @pl.when(is_end)
    def _():
        misc_in[at] = misc[...]
        to_inner.start()

    pump()

    @pl.when(is_inner)
    def _():
        to_inner.wait_recv()
        misc_in[at + 2] = misc[...] + misc_in[at + 1]
        to_other.start()

    pump()

    @pl.when(is_inner)
    def _():
        to_other.wait_recv()
        misc_out[...] = misc_in[at + 2] + misc_in[at + 3]
        to_end.start()

    pump(8)

    @pl.when(is_end)
    def _():
        to_end.wait_recv()
        to_inner.wait_send()

    @pl.when(is_inner)
    def _():
        to_other.wait_send()
        to_end.wait_send()

    for copy in end_copies:
        copy.wait_recv()
    for wait in closing + list(leaving.values()):
        wait()


def on_device(
    inputs,
    attn_qkv,
    attn_out,
    conv_in,
    conv_kernel,
    conv_out,
    ffn_up,
    ffn_down,
    norm_gain,
    norm_bias,
    kernel_half,
    batch_plan,
    masked_positions,
    out_grad,
):
    section = lax.axis_index("section")
    replica = lax.axis_index("dp")
    dp = lax.axis_size("dp")
    slot_count, part, width = inputs.shape
    micro_count = batch_plan.shape[1]
    count = masked_positions.shape[1]
    marked = round_up(count, 16)
    assert slot_count == SECTIONS == lax.axis_size("section") and lax.axis_size("mp") == GROUP
    hw = attn_out.shape[0]
    hidden = ffn_up.shape[2]
    lay = Layout(dp, part * GROUP, width, hw, hidden, marked)
    assert hidden == width and width % LANES == 0 and hw % HEAD == 0

    slot_ids = jnp.arange(slot_count)
    paired = jnp.any(batch_plan[:, :, 1][:, :, None] == slot_ids[None, None, :], axis=1)
    used_all = ((slot_ids[None, :] < micro_count) | paired).astype(F32)
    used = used_all[replica, section]
    tap_mask = (jnp.abs(jnp.arange(8) - MARGIN) <= kernel_half[0]) & (jnp.arange(8) < TAPS)
    tap_on = jnp.broadcast_to(tap_mask.astype(F32)[:, None], (8, hw))
    tap_weight = jnp.pad(conv_kernel.astype(F32), ((0, 1), (0, 0))) * tap_on
    where = lax.dynamic_index_in_dim(masked_positions, section, 0, keepdims=True)
    where = jnp.pad(where, ((0, 7), (0, 128 - count)), constant_values=-1)
    cotangent = lax.dynamic_index_in_dim(out_grad, section, 0, keepdims=False)
    cotangent = jnp.pad(cotangent, ((0, marked - count), (0, 0))) * used.astype(BF16)
    used_rows = jnp.full((8, 128), used, F32)

    seq, chunk = lay.seq, lay.chunk
    any_spec = pl.BlockSpec(memory_space=pl.ANY)
    vmem_spec = pl.BlockSpec(memory_space=pltpu.VMEM)
    hops = 2 + lay.bits
    all_marked = SECTIONS * dp * marked
    z_rows = lay.rows // dp
    scratch = [
        pltpu.VMEM(attn_qkv.shape, BF16),
        pltpu.VMEM(attn_out.shape, BF16),
        pltpu.VMEM(conv_in.shape, BF16),
        pltpu.VMEM(conv_out.shape, BF16),
        pltpu.VMEM(ffn_up.shape, BF16),
        pltpu.VMEM(ffn_down.shape, BF16),
        pltpu.VMEM((4, seq, width), BF16),
        pltpu.VMEM((2, seq, width), BF16),
        pltpu.VMEM((2, 2, part, width), F32),
        pltpu.VMEM((2, 2, part, 1), F32),
        pltpu.VMEM((3, seq, hw), BF16),
        pltpu.VMEM((hw // HEAD, seq, seq), F32),
        pltpu.VMEM((seq, hw), BF16),
        pltpu.VMEM((seq, hw), BF16),
        pltpu.VMEM((3, seq, hw), BF16),
        pltpu.VMEM((2, seq, hw), F32),
        pltpu.VMEM((seq, hidden), BF16),
        pltpu.VMEM((seq, hidden), F32),
        pltpu.VMEM((seq, hidden), BF16),
        pltpu.VMEM((seq, hw), F32),
        pltpu.VMEM((seq, hw), F32),
        pltpu.VMEM((seq + 2 * PAD, hw), F32),
        pltpu.VMEM((seq, hw), BF16),
        pltpu.VMEM((seq + 2 * PAD, hw), F32),
        pltpu.VMEM((2, seq, hw), BF16),
        pltpu.VMEM((seq, marked), BF16),
        pltpu.VMEM((marked, width), BF16),
        pltpu.VMEM((1, marked, width), F32),
        pltpu.VMEM((marked, hidden), F32),
        pltpu.VMEM((marked, hidden), BF16),
        pltpu.VMEM((2, marked, width), F32),
        pltpu.VMEM((chunk, width), F32),
        pltpu.VMEM((lay.sets, 2, part, width), BF16),
        pltpu.VMEM((lay.sets, 2, part, width), BF16),
        pltpu.VMEM((lay.sets, 2, part, width), BF16),
        pltpu.VMEM((lay.sets, 2, part, width), BF16),
        pltpu.VMEM((3, marked, width), BF16),
        pltpu.VMEM((3, marked, width), BF16),
        pltpu.VMEM((3, marked, width), BF16),
        pltpu.VMEM((3, marked, width), BF16),
        pltpu.VMEM((lay.rows, width), BF16),
        pltpu.VMEM((max(lay.rows - z_rows, 16), width), BF16),
        pltpu.VMEM((z_rows, width), BF16),
        pltpu.VMEM((z_rows, width), BF16),
        pltpu.VMEM((2, all_marked, width), BF16),
        pltpu.VMEM((lay.misc_rows, width), F32),
        pltpu.VMEM((2 * hops + 4, lay.misc_rows, width), F32),
        pltpu.SemaphoreType.DMA((8,)),
        pltpu.SemaphoreType.DMA((160,)),
        pltpu.SemaphoreType.DMA((160,)),
    ]
    final, up1_grad, down1_grad, layer_rows, input_rows, misc = pl.pallas_call(
        functools.partial(main_kernel, lay),
        out_shape=(
            jax.ShapeDtypeStruct((lay.rows, width), BF16),
            jax.ShapeDtypeStruct((width, hidden), F32),
            jax.ShapeDtypeStruct((hidden, width), F32),
            jax.ShapeDtypeStruct((slot_count, part, width), BF16),
            jax.ShapeDtypeStruct((slot_count, part, width), BF16),
            jax.ShapeDtypeStruct((lay.misc_rows, width), F32),
        ),
        in_specs=[any_spec] * 7 + [vmem_spec] * 7,
        out_specs=(vmem_spec,) * 6,
        scratch_shapes=scratch,
        compiler_params=pltpu.CompilerParams(
            collective_id=0, has_side_effects=True, vmem_limit_bytes=62 * 2**20
        ),
        name="layers",
    )(
        inputs,
        attn_qkv,
        attn_out,
        conv_in,
        conv_out,
        ffn_up,
        ffn_down,
        norm_gain,
        norm_bias,
        tap_weight,
        tap_on,
        where,
        cotangent,
        used_rows,
    )
    conv_grads = final[lay.conv_at : lay.conv_at + 3 * hw].astype(F32)
    attn_grads = final[lay.attn_at : lay.attn_at + 4 * hw].astype(F32)
    grad_qkv = attn_grads[: 3 * hw].reshape(3, hw, width).transpose(0, 2, 1)
    grad_cin = conv_grads[: 2 * hw].reshape(2, hw, width).transpose(0, 2, 1)
    grad_kernel = final[lay.kernel_at : lay.kernel_at + TAPS, :hw].astype(F32)
    grad_up = jnp.stack([final[lay.up_at : lay.up_at + width].astype(F32), up1_grad])
    grad_down = jnp.stack([final[lay.down_at : lay.down_at + hidden].astype(F32), down1_grad])
    counts = jnp.sum(used_all, axis=1) * (seq * width)
    stream_rms = jnp.sqrt(misc[8 : 8 + dp, 0:8] / counts[:, None])
    return (
        layer_rows,
        input_rows.astype(F32),
        grad_qkv,
        attn_grads[3 * hw :],
        grad_cin,
        grad_kernel,
        conv_grads[2 * hw :],
        grad_up,
        grad_down,
        misc[0:4],
        misc[4:8],
        stream_rms,
    )


def solution(mesh):
    return jax.shard_map(
        on_device,
        mesh=mesh,
        in_specs=(
            P("dp", "mp", None),
            P(None, None, "mp"),
            P("mp", None),
            P(None, None, "mp"),
            P(None, "mp"),
            P("mp", None),
            P(None, None, "mp"),
            P(None, "mp", None),
            P(),
            P(),
            P(),
            P(),
            P("dp", None),
            P("dp", None, None),
        ),
        out_specs=(
            P("dp", "mp", None),
            P("dp", "mp", None),
            P(None, None, "mp"),
            P("mp", None),
            P(None, None, "mp"),
            P(None, "mp"),
            P("mp", None),
            P(None, None, "mp"),
            P(None, "mp", None),
            P(),
            P(),
            P(),
        ),
        check_vma=False,
    )
```

time: 1580 us -> 263 us (0.17); the launches traced: 1560 us -> 262 us
  waiting for transfers between devices: 1000 us -> 0 us
  Pallas kernels: 0 us -> 230 us
  other arithmetic: 154 us -> 13.6 us
  matrix products: 105 us -> 0 us
  local copies, waits for them, and re-layouts: 116 us -> 16.8 us
  loops' own time: 76.6 us -> 0 us
  blocking collectives: 62.9 us -> 0 us
  starting transfers between devices: 25.4 us -> 0 us
    reduce_scatter x10 -> x0, waiting for transfers between devices: 482 us -> none  [the longest x5 288 us: input_total(): lax.psum_scatter(partial_value, 'mp', scatter_dimension=1, tiled=True)]
    pallas_call x0 -> x1, Pallas kernels: none -> 230 us  [on_device(): pl.pallas_call(functools.partial(main_kernel, lay), out_shape=(jax.ShapeD...]
    psum x2 -> x0, waiting for transfers between devices: 224 us -> none  [the longest x1 224 us: on_device(): lax.psum(grad_qkv.astype(jnp.bfloat16), ('section', 'dp'))]
    all_gather x10 -> x0, waiting for transfers between devices: 181 us -> none  [the longest x5 94.4 us: spread_rows(): return lax.all_gather(shard, 'mp', axis=1, tiled=True)]
    ppermute x10 -> x0, waiting for transfers between devices: 115 us -> none  [shifted(): lax.ppermute(array, axis, [(i, (i + by) % peers) for i in range(peers)])]
    dot_general x45 -> x0, matrix products: 105 us -> none  [the longest x10 21.7 us: conv_parts(): jnp.einsum('bld,kdc->kblc', hidden, conv_in, preferred_element_type=jnp.f...]
    another operation x12 -> x0, loops' own time: 76.6 us -> none  [the longest x5 41.1 us: switch_back(): lax.switch(block_pos, back_fns, hidden, grad_full, grad_state, active)]
    psum x2 -> x0, blocking collectives: 62.9 us -> none  [the longest x1 39.5 us: on_device(): lax.psum((gain_acc, bias_acc, replica_rows), ('section', 'dp', 'mp'))]
  transfers between devices with their start and end apart: 32 -> 0, of which waited for: 31 -> 0; matrix products, arithmetic and copies ran while one was open for 5% -> 0% of each run, Pallas kernels for 0% -> 0%
where the time goes in v1:
time: 263 us; the launch traced here: 262 us
  Pallas kernels  230 us (87%)
  local copies, waits for them, and re-layouts  16.8 us (6%)
  other arithmetic  13.6 us (5%)
    pallas_call x1, Pallas kernels, on_device(): pl.pallas_call(functools.partial(main_kernel, lay), out_shape=(jax.ShapeD...  230 us
    unnamed x16, local copies, waits for them, and re-layouts  6.32 us

profile of v1, /device:TPU:0, one launch (start us, length us, event | category | flops | bytes accessed | tf_op | source)
XLA Modules:
  0.0 262.3 jit_solution(4029402729031696461)
XLA Ops:
  0.6 0.0 copy-start
  0.7 0.0 copy-start.4
  1.4 0.7 constant_dynamic-slice_fusion.1
  2.1 0.9 slice_reduce_fusion
  3.0 0.1 compare_reduce_fusion
  3.1 0.1 fusion
  3.3 0.6 dynamic_slice.13
  4.5 1.2 broadcast_in_dim.5.used
  5.8 0.6 pad.17.where
  6.4 1.4 convert_multiply_fusion.tap_weight
  7.7 0.7 broadcast_in_dim.4.tap_on
  8.4 0.0 copy-done
  8.4 0.2 constant_dynamic-slice_fusion
  8.7 0.7 pad_multiply_fusion.cotangent
  9.3 2.2 copy.33.cin_in
  11.5 0.0 copy-done.4
  11.6 1.4 copy.32.qkv_in
  13.0 229.7 %layers.1 = (bf16[2944,768]{1,0:T(8,128)(2,1)}, f32[768,768]{1,0:T(8,128)}, f32[768,768]{1,0:T(8,128)}, bf16[4,128,768]{2,1,0:T(8,128)(2,1)}, bf16[4,128,768]{2,1,0:T(8,128)(2,1)}, /*index=5*/f32[16,768]{1,0:T(8,128)}) custom-call(bf16[4,128,768]{2,1,0:T(8,128)(2,1)} %x_in.1, bf16[3,768,192]{2,1,0:T(8,128)(2,1)} %copy.32.qkv_in, bf16[192,768]{1,0:T(8,128)(2,1)} %ao_in.1, ...), custom_call_target="tpu_custom_call" | custom-call | tf_op jit(solution)/shard_map/layers/pallas_call | solution.py:1055
  242.7 1.3 divide_sqrt_fusion
  244.0 1.4 fusion.1
  245.4 1.3 slice_convert_fusion.2
  246.7 2.4 convert_element_type.35
  249.1 1.4 slice_convert_fusion.1
  250.6 0.9 slice.55
  251.4 1.1 slice.54
  252.5 0.6 bitcast_convert_fusion
  253.1 1.1 copy-done.2
  254.2 0.7 copy-done.3
  254.9 4.3 %pad_maximum_fusion = (f32[2,768,768]{2,1,0:T(8,128)}, f32[2,768,768]{2,1,0:T(8,128)}) fusion(f32[1,768,768]{2,1,0:T(8,128)S(1)} %bitcast.20, f32[1,768,768]{2,1,0:T(8,128)S(1)} %get-tuple-element.25, f32[1,768,768]{2,1,0:T(8,128)S(1)} %bitcast.21, f32[1,768,768]{2,1,0:T(8,128)S(1)} %get-tuple-element.24), kind=kLoop, calls=%fused_computation | loop fusion | flops 2359296 | bytes 18874368 | tf_op jit(solution)/shard_map/stack | solution.py:1093
  259.2 0.9 slice.53
  260.1 1.3 slice.52
  261.4 0.9 copy.39
  (11 shorter events, 0.1 us)
Async XLA Ops:
  0.6 7.7 %copy-start = (bf16[4,77,768]{2,0,1:T(4,128)(2,1)S(1)}, bf16[4,77,768]{2,0,1:T(4,128)(2,1)}, u32[]{:S(2)}) copy-start(bf16[4,77,768]{2,0,1:T(4,128)(2,1)} %param.27) | copy-start | bytes 1419268
  0.7 10.9 %copy-start.4 = (bf16[3,768,192]{1,2,0:T(8,128)(2,1)S(1)}, bf16[3,768,192]{1,2,0:T(8,128)(2,1)}, u32[]{:S(2)}) copy-start(bf16[3,768,192]{1,2,0:T(8,128)(2,1)} %param.15) | copy-start | bytes 2654212
  249.1 3.4 %copy-start.1 = (bf16[2944,768]{1,0:T(8,128)(2,1)S(1)}, bf16[2944,768]{1,0:T(8,128)(2,1)}, u32[]{:S(2)}) copy-start(bf16[2944,768]{1,0:T(8,128)(2,1)} %get-tuple-element.20) | copy-start | bytes 13565956
  252.5 1.7 copy-start.2
  252.5 2.4 copy-start.3
  259.2 2.2 copy-start.5

commit v2 on v1

--- a/solution.py
+++ b/solution.py
@@ -74,8 +74,8 @@
 
 
 class Layout:
-    def __init__(self, dp, seq, width, heads_width, hidden, marked):
-        self.dp, self.seq, self.width = dp, seq, width
+    def __init__(self, dp, micro, seq, width, heads_width, hidden, marked):
+        self.dp, self.micro, self.seq, self.width = dp, micro, seq, width
         self.heads_width, self.hidden = heads_width, hidden
         self.marked = marked
         self.part = seq // GROUP
@@ -87,6 +87,9 @@
         self.down_at, at = at, at + hidden
         self.attn_at, at = at, at + 4 * heads_width
         self.rows = at
+        self.up1_at, at = at, at + width
+        self.down1_at, at = at, at + hidden
+        self.all_rows = at
         self.kernel_at = self.conv_at + 3 * heads_width
         self.pieces = {
             "conv": self.cut(self.conv_at, conv_rows, 1),
@@ -94,6 +97,12 @@
             "down": self.cut(self.down_at, hidden, 2),
             "attn": self.cut(self.attn_at, 4 * heads_width, 2),
         }
+        self.stores = [
+            (self.conv_at, self.up_at),
+            (self.up_at, width + hidden),
+            (self.attn_at, 4 * heads_width),
+            (self.up1_at, width + hidden),
+        ]
         self.bits = dp.bit_length() - 1
         assert dp == 1 << self.bits and dp <= 8
         self.misc_rows = 16
@@ -116,17 +125,19 @@
     down_in,
     gain,
     bias,
+    taps_in,
+    positions,
+    cotangent,
+    half_size,
+    plan,
+    final_out,
+    layer_rows,
+    input_rows,
+    misc_out,
+    final,
     tap_weight,
     tap_on,
     where,
-    cotangent,
-    used,
-    final,
-    up1_grad,
-    down1_grad,
-    layer_rows,
-    input_rows,
-    misc_out,
     wqkv,
     wao,
     wcin,
@@ -172,9 +183,11 @@
     za,
     zb,
     factors,
+    sums,
     misc,
     misc_in,
     load_sem,
+    store_sem,
     send_sem,
     recv_sem,
 ):
@@ -268,6 +281,17 @@
         loads[name] = copy
 
     misc[...] = jnp.zeros_like(misc)
+    holds = section < lay.micro
+    for i in range(lay.micro):
+        holds = holds | (plan[replica, i, 1] == section)
+    used = jnp.where(holds, 1.0, 0.0).astype(F32)
+    tap_row = lax.broadcasted_iota(jnp.int32, (TAPS, hw), 0)
+    tap_mask = jnp.where(jnp.abs(tap_row - MARGIN) <= half_size[0], 1.0, 0.0)
+    tap_on[...] = jnp.zeros_like(tap_on)
+    tap_on[0:TAPS] = tap_mask
+    tap_weight[0:TAPS] = taps_in[...].astype(F32) * tap_mask
+    where[...] = jnp.full(where.shape, -1, jnp.int32)
+    where[0:1, 0 : positions.shape[1]] = positions[pl.ds(section, 1)]
     lane = lax.broadcasted_iota(jnp.int32, (1, hw), 1)
     head_lanes = [(lane >= HEAD * i) & (lane < HEAD * (i + 1)) for i in range(local_heads)]
     head_low = [jnp.where(on, 1.0, 0.0).astype(BF16) for on in head_lanes]
@@ -372,8 +396,8 @@
 
             @pl.when(high == t)
             def _():
-                add_stat(k, whole_sum(squares[0]) * used[0:1, 0:1])
-                add_stat(4 + k, whole_sum(squares[1]) * used[0:1, 0:1])
+                add_stat(k, whole_sum(squares[0]) * used)
+                add_stat(4 + k, whole_sum(squares[1]) * used)
 
             rows = own_rows(t)
             return send(hid.at[k + 1, rows], hid.at[k + 1, rows], side)
@@ -538,6 +562,15 @@
                 except StopIteration:
                     running.remove(piece)
 
+    def final_store(at):
+        rows = pl.ds(*lay.stores[at])
+        return pltpu.make_async_copy(final.at[rows], final_out.at[rows], store_sem.at[at])
+
+    stored = [0]
+
+    def store_final(at):
+        final_store(at).start()
+
     pl.semaphore_wait(barrier, len(peers))
     loads["x"].wait()
     mine = block(member * part, part)
@@ -551,7 +584,7 @@
     def project(at):
         rows = block(at, part)
         for j in range(3):
-            qkv[j, rows] = dot(hid[0, rows], wqkv[j]).astype(BF16)
+            qkv[j, rows] = dot_lanes(hid[0, rows], wqkv[j]).astype(BF16)
 
     project(member * part)
     to_side.wait_recv()
@@ -609,8 +642,8 @@
     for t in range(2):
         gathered[t].wait_recv()
         rows = pl.ds(chunk * t, chunk)
-        value_here = dot(hid[2, rows], wcin[0])
-        sig_here = jax.nn.sigmoid(dot(hid[2, rows], wcin[1]))
+        value_here = dot_lanes(hid[2, rows], wcin[0])
+        sig_here = jax.nn.sigmoid(dot_lanes(hid[2, rows], wcin[1]))
         value[rows] = value_here
         sig[rows] = sig_here
         gated[pl.ds(PAD + chunk * t, chunk)] = value_here * sig_here
@@ -646,7 +679,7 @@
     branch = marked_total(1, dot(munits[...], wdown[1]))
     norm3, inv3 = normalise(mh[...].astype(F32) + branch)
     once = jnp.where(member == 0, 1.0, 0.0).astype(F32)
-    dy = cotangent[...].astype(F32)
+    dy = cotangent[...].astype(F32) * used
     misc[3:4] += once * jnp.sum(dy * norm3, axis=0, keepdims=True)
     misc[7:8] += once * jnp.sum(dy, axis=0, keepdims=True)
     dz3 = norm_pull(dy, norm3, inv3, gain[3:4])
@@ -726,7 +759,7 @@
 
     def conv_back_work(t):
         rows = pl.ds(chunk * t, chunk)
-        partial[...] = dot_lanes(dgates[0, rows], wcin[0]) + dot_lanes(dgates[1, rows], wcin[1])
+        partial[...] = dot(dgates[0, rows], wcin[0]) + dot(dgates[1, rows], wcin[1])
 
     def conv_back_finish(t):
         def grad_tile(rows, place):
@@ -800,9 +833,9 @@
     def attention_back_work(t):
         rows = pl.ds(chunk * t, chunk)
         partial[...] = (
-            dot_lanes(dqkv[0, rows], wqkv[0])
-            + dot_lanes(dqkv[1, rows], wqkv[1])
-            + dot_lanes(dqkv[2, rows], wqkv[2])
+            dot(dqkv[0, rows], wqkv[0])
+            + dot(dqkv[1, rows], wqkv[1])
+            + dot(dqkv[2, rows], wqkv[2])
         )
 
     core = []
@@ -853,7 +886,8 @@
     send(factors.at[low], factors.at[low], side, shared)
     remote(factors.at[1 - low], factors.at[1 - low], side, shared).wait_recv()
     group_rows = GROUP * marked
-    for group in range(SECTIONS * per_section // group_rows):
+    groups = SECTIONS * per_section // group_rows
+    for group in range(groups):
         rows = pl.ds(group * group_rows, group_rows)
 
         def recompute(j, carry):
@@ -870,12 +904,16 @@
             lanes = block(i * LANES, LANES)
             by_up = dot_rows(factors[0, rows, lanes], dbefore[0:group_rows])
             by_down = dot_rows(units[0:group_rows, lanes], factors[1, rows])
-            if group == 0:
-                up1_grad[lanes] = by_up
-                down1_grad[lanes] = by_down
+            if group > 0:
+                by_up = by_up + sums[0, lanes]
+                by_down = by_down + sums[1, lanes]
+            if group < groups - 1:
+                sums[0, lanes] = by_up
+                sums[1, lanes] = by_down
             else:
-                up1_grad[lanes] += by_up
-                down1_grad[lanes] += by_down
+                at = pl.multiple_of(i * LANES, LANES)
+                final[pl.ds(lay.up1_at + at, LANES)] = by_up.astype(BF16)
+                final[pl.ds(lay.down1_at + at, LANES)] = by_down.astype(BF16)
             return carry
 
         tiles(width // LANES, last_weights)
@@ -887,14 +925,14 @@
         stream = hid[3, block(member * part + i * TILE, TILE)].astype(F32)
         branch = total_tile(6, high, rows)
         norm, _ = normalise(stream + branch)
-        result = (norm * gain[3:4] + bias[3:4]) * used[0:1, 0:1]
+        result = (norm * gain[3:4] + bias[3:4]) * used
         layer_rows[section, rows] = result.astype(BF16)
         return (carry[0] + fold(stream * stream), carry[1] + fold(branch * branch))
 
     zero = jnp.zeros((8, width), F32)
     squares = tiles(part // TILE, layer_body, (zero, zero))
-    add_stat(3, whole_sum(squares[0]) * used[0:1, 0:1])
-    add_stat(7, whole_sum(squares[1]) * used[0:1, 0:1])
+    add_stat(3, whole_sum(squares[0]) * used)
+    add_stat(7, whole_sum(squares[1]) * used)
     end_copies += [
         send(layer_rows.at[section], layer_rows.at[section], section_peer(by))
         for by in range(1, SECTIONS)
@@ -946,10 +984,109 @@
         to_other.wait_send()
         to_end.wait_send()
 
+    for at, (start, rows) in enumerate(lay.stores):
+        if at >= stored[0]:
+            store_final(at)
     for copy in end_copies:
         copy.wait_recv()
+    for at in range(len(lay.stores)):
+        final_store(at).wait()
     for wait in closing + list(leaving.values()):
         wait()
+
+
+def widen_kernel(
+    lay,
+    final,
+    input_rows,
+    misc,
+    plan,
+    input_grad,
+    qkv,
+    out,
+    cin,
+    cout,
+    up,
+    down,
+    kernel,
+    gains,
+    biases,
+    rms,
+    narrow,
+    wide,
+    narrow_input,
+    wide_input,
+    load_sem,
+    store_sem,
+):
+    hw, width, hidden = lay.heads_width, lay.width, lay.hidden
+    blocks = []
+
+    def cover(start, rows, target, step):
+        for at in range(0, rows, step):
+            blocks.append((start + at, step, target.at[pl.ds(at, step)]))
+
+    for layer, (up_at, down_at) in enumerate(
+        ((lay.up_at, lay.down_at), (lay.up1_at, lay.down1_at))
+    ):
+        cover(up_at, width, up.at[layer], width // 2)
+        cover(down_at, hidden, down.at[layer], hidden // 2)
+    for j in range(3):
+        cover(lay.attn_at + j * hw, hw, qkv.at[j], hw)
+    cover(lay.attn_at + 3 * hw, hw, out, hw)
+    for j in range(2):
+        cover(lay.conv_at + j * hw, hw, cin.at[j], hw)
+    cover(lay.conv_at + 2 * hw, hw, cout, hw)
+
+    def load(at):
+        start, rows, _ = blocks[at]
+        here = pl.ds(start, rows)
+        return pltpu.make_async_copy(final.at[here], narrow.at[here], load_sem.at[at])
+
+    def store(at):
+        start, rows, target = blocks[at]
+        return pltpu.make_async_copy(wide.at[pl.ds(start, rows)], target, store_sem.at[at])
+
+    extra = len(blocks)
+    tap_rows = pltpu.make_async_copy(
+        final.at[pl.ds(lay.kernel_at, 16)], narrow.at[pl.ds(lay.kernel_at, 16)], load_sem.at[extra]
+    )
+    inputs_in = pltpu.make_async_copy(input_rows, narrow_input, load_sem.at[extra + 1])
+    inputs_out = pltpu.make_async_copy(wide_input, input_grad, store_sem.at[extra])
+    for at in range(len(blocks)):
+        load(at).start()
+    inputs_in.start()
+    tap_rows.start()
+    gains[...] = misc[0:4]
+    biases[...] = misc[4:8]
+    row = lax.broadcasted_iota(jnp.int32, rms.shape, 0)
+    counts = jnp.zeros(rms.shape, F32)
+    for r in range(rms.shape[0]):
+        total = jnp.float32(lay.micro)
+        for i in range(lay.micro):
+            total = total + jnp.where(plan[r, i, 1] >= 0, 1.0, 0.0).astype(F32)
+        counts = jnp.where(row == r, total, counts)
+    rms[...] = jnp.sqrt(misc[8 : 8 + rms.shape[0], 0:8] / (counts * (lay.seq * width)))
+    for at, (start, rows, _) in enumerate(blocks):
+        load(at).wait()
+
+        def body(i, carry, start=start):
+            here = pl.ds(pl.multiple_of(start + i * 32, 16), 32)
+            wide[here] = narrow[here].astype(F32)
+            return carry
+
+        lax.fori_loop(0, rows // 32, body, 0)
+        store(at).start()
+    inputs_in.wait()
+    for slot in range(input_rows.shape[0]):
+        wide_input[slot] = narrow_input[slot].astype(F32)
+    inputs_out.start()
+    tap_rows.wait()
+    taps = narrow[pl.ds(lay.kernel_at, 16)].astype(F32)
+    kernel[...] = taps[0:TAPS, 0:hw]
+    for at in range(len(blocks)):
+        store(at).wait()
+    inputs_out.wait()
 
 
 def on_device(
@@ -978,21 +1115,11 @@
     assert slot_count == SECTIONS == lax.axis_size("section") and lax.axis_size("mp") == GROUP
     hw = attn_out.shape[0]
     hidden = ffn_up.shape[2]
-    lay = Layout(dp, part * GROUP, width, hw, hidden, marked)
+    lay = Layout(dp, micro_count, part * GROUP, width, hw, hidden, marked)
     assert hidden == width and width % LANES == 0 and hw % HEAD == 0
 
-    slot_ids = jnp.arange(slot_count)
-    paired = jnp.any(batch_plan[:, :, 1][:, :, None] == slot_ids[None, None, :], axis=1)
-    used_all = ((slot_ids[None, :] < micro_count) | paired).astype(F32)
-    used = used_all[replica, section]
-    tap_mask = (jnp.abs(jnp.arange(8) - MARGIN) <= kernel_half[0]) & (jnp.arange(8) < TAPS)
-    tap_on = jnp.broadcast_to(tap_mask.astype(F32)[:, None], (8, hw))
-    tap_weight = jnp.pad(conv_kernel.astype(F32), ((0, 1), (0, 0))) * tap_on
-    where = lax.dynamic_index_in_dim(masked_positions, section, 0, keepdims=True)
-    where = jnp.pad(where, ((0, 7), (0, 128 - count)), constant_values=-1)
     cotangent = lax.dynamic_index_in_dim(out_grad, section, 0, keepdims=False)
-    cotangent = jnp.pad(cotangent, ((0, marked - count), (0, 0))) * used.astype(BF16)
-    used_rows = jnp.full((8, 128), used, F32)
+    cotangent = jnp.pad(cotangent, ((0, marked - count), (0, 0)))
 
     seq, chunk = lay.seq, lay.chunk
     any_spec = pl.BlockSpec(memory_space=pl.ANY)
@@ -1001,9 +1128,13 @@
     all_marked = SECTIONS * dp * marked
     z_rows = lay.rows // dp
     scratch = [
-        pltpu.VMEM(attn_qkv.shape, BF16),
+        pltpu.VMEM((lay.all_rows, width), BF16),
+        pltpu.VMEM((8, hw), F32),
+        pltpu.VMEM((8, hw), F32),
+        pltpu.VMEM((8, marked), jnp.int32),
+        pltpu.VMEM((3, hw, width), BF16),
         pltpu.VMEM(attn_out.shape, BF16),
-        pltpu.VMEM(conv_in.shape, BF16),
+        pltpu.VMEM((2, hw, width), BF16),
         pltpu.VMEM(conv_out.shape, BF16),
         pltpu.VMEM(ffn_up.shape, BF16),
         pltpu.VMEM(ffn_down.shape, BF16),
@@ -1046,67 +1177,89 @@
         pltpu.VMEM((z_rows, width), BF16),
         pltpu.VMEM((z_rows, width), BF16),
         pltpu.VMEM((2, all_marked, width), BF16),
+        pltpu.VMEM((2, width, hidden), F32),
         pltpu.VMEM((lay.misc_rows, width), F32),
         pltpu.VMEM((2 * hops + 4, lay.misc_rows, width), F32),
         pltpu.SemaphoreType.DMA((8,)),
+        pltpu.SemaphoreType.DMA((len(lay.stores),)),
         pltpu.SemaphoreType.DMA((160,)),
         pltpu.SemaphoreType.DMA((160,)),
     ]
-    final, up1_grad, down1_grad, layer_rows, input_rows, misc = pl.pallas_call(
+    smem_spec = pl.BlockSpec(memory_space=pltpu.SMEM)
+    final, layer_rows, input_rows, misc = pl.pallas_call(
         functools.partial(main_kernel, lay),
         out_shape=(
-            jax.ShapeDtypeStruct((lay.rows, width), BF16),
-            jax.ShapeDtypeStruct((width, hidden), F32),
-            jax.ShapeDtypeStruct((hidden, width), F32),
+            jax.ShapeDtypeStruct((lay.all_rows, width), BF16),
             jax.ShapeDtypeStruct((slot_count, part, width), BF16),
             jax.ShapeDtypeStruct((slot_count, part, width), BF16),
             jax.ShapeDtypeStruct((lay.misc_rows, width), F32),
         ),
-        in_specs=[any_spec] * 7 + [vmem_spec] * 7,
-        out_specs=(vmem_spec,) * 6,
+        in_specs=[any_spec] * 7 + [vmem_spec] * 5 + [smem_spec] * 2,
+        out_specs=(any_spec,) + (vmem_spec,) * 3,
         scratch_shapes=scratch,
         compiler_params=pltpu.CompilerParams(
-            collective_id=0, has_side_effects=True, vmem_limit_bytes=62 * 2**20
+            collective_id=0, has_side_effects=True, vmem_limit_bytes=63 * 2**20
         ),
         name="layers",
     )(
         inputs,
-        attn_qkv,
+        jnp.swapaxes(attn_qkv, 1, 2),
         attn_out,
-        conv_in,
+        jnp.swapaxes(conv_in, 1, 2),
         conv_out,
         ffn_up,
         ffn_down,
         norm_gain,
         norm_bias,
-        tap_weight,
-        tap_on,
-        where,
+        conv_kernel,
+        masked_positions,
         cotangent,
-        used_rows,
+        kernel_half,
+        batch_plan,
     )
-    conv_grads = final[lay.conv_at : lay.conv_at + 3 * hw].astype(F32)
-    attn_grads = final[lay.attn_at : lay.attn_at + 4 * hw].astype(F32)
-    grad_qkv = attn_grads[: 3 * hw].reshape(3, hw, width).transpose(0, 2, 1)
-    grad_cin = conv_grads[: 2 * hw].reshape(2, hw, width).transpose(0, 2, 1)
-    grad_kernel = final[lay.kernel_at : lay.kernel_at + TAPS, :hw].astype(F32)
-    grad_up = jnp.stack([final[lay.up_at : lay.up_at + width].astype(F32), up1_grad])
-    grad_down = jnp.stack([final[lay.down_at : lay.down_at + hidden].astype(F32), down1_grad])
-    counts = jnp.sum(used_all, axis=1) * (seq * width)
-    stream_rms = jnp.sqrt(misc[8 : 8 + dp, 0:8] / counts[:, None])
+    shapes = [
+        (slot_count, part, width),
+        (3, hw, width),
+        (hw, width),
+        (2, hw, width),
+        (hw, width),
+        (2, width, hidden),
+        (2, hidden, width),
+        (TAPS, hw),
+        (4, width),
+        (4, width),
+        (dp, 8),
+    ]
+    widened = pl.pallas_call(
+        functools.partial(widen_kernel, lay),
+        out_shape=tuple(jax.ShapeDtypeStruct(shape, F32) for shape in shapes),
+        in_specs=[any_spec] * 2 + [vmem_spec] + [smem_spec],
+        out_specs=(any_spec,) * 7 + (vmem_spec,) * 4,
+        scratch_shapes=[
+            pltpu.VMEM((lay.all_rows, width), BF16),
+            pltpu.VMEM((lay.all_rows, width), F32),
+            pltpu.VMEM((slot_count, part, width), BF16),
+            pltpu.VMEM((slot_count, part, width), F32),
+            pltpu.SemaphoreType.DMA((32,)),
+            pltpu.SemaphoreType.DMA((32,)),
+        ],
+        compiler_params=pltpu.CompilerParams(vmem_limit_bytes=48 * 2**20),
+        name="widen",
+    )(final, input_rows, misc, batch_plan)
+    (input_grad, qkv, out, cin, cout, up, down, kernel, gains, biases, rms) = widened
     return (
         layer_rows,
-        input_rows.astype(F32),
-        grad_qkv,
-        attn_grads[3 * hw :],
-        grad_cin,
-        grad_kernel,
-        conv_grads[2 * hw :],
-        grad_up,
-        grad_down,
-        misc[0:4],
-        misc[4:8],
-        stream_rms,
+        input_grad,
+        jnp.swapaxes(qkv, 1, 2),
+        out,
+        jnp.swapaxes(cin, 1, 2),
+        kernel,
+        cout,
+        up,
+        down,
+        gains,
+        biases,
+        rms,
     )
 
 

time: 263 us -> 244 us (0.928)
  other arithmetic: 13.6 us -> 0 us
  local copies, waits for them, and re-layouts: 16.8 us -> 4.07 us
  Pallas kernels: 230 us -> 238 us
    pallas_call x0 -> x1, Pallas kernels: none -> 8.64 us  [on_device(): pl.pallas_call(functools.partial(widen_kernel, lay), out_shape=tuple((jax...]
    slice x6 -> x0, local copies, waits for them, and re-layouts: 6.43 us -> none  [the longest x1 1.42 us: on_device(): misc[4:8]]
    convert_element_type x5 -> x0, other arithmetic: 5.13 us -> none  [the longest x1 2.41 us: on_device(): input_rows.astype(F32)]
    another operation x2 -> x0, other arithmetic: 4.94 us -> none  [the longest x1 4.34 us: on_device(): jnp.stack([final[lay.up_at:lay.up_at + width].astype(F32), up1_grad])]
    unnamed x16 -> x12, local copies, waits for them, and re-layouts: 6.32 us -> 3.17 us
where the time goes in v2:
time: 244 us; the launch traced here: 243 us
  Pallas kernels  238 us (98%)
  local copies, waits for them, and re-layouts  4.07 us (2%)
    pallas_call x1, Pallas kernels, on_device(): pl.pallas_call(functools.partial(main_kernel, lay), out_shape=(jax.ShapeD...  229 us
    pallas_call x1, Pallas kernels, on_device(): pl.pallas_call(functools.partial(widen_kernel, lay), out_shape=tuple((jax...  8.64 us

profile of v2, /device:TPU:0, one launch (start us, length us, event | category | flops | bytes accessed | tf_op | source)
XLA Modules:
  0.0 243.4 jit_solution(11459468280666389274)
XLA Ops:
  0.6 0.0 copy-start
  1.4 0.3 copy-done
  1.7 0.2 constant_dynamic-slice_fusion
  2.0 0.7 pad.4.cotangent
  2.6 0.0 copy-start.3
  2.6 229.2 %layers.1 = (bf16[4480,768]{1,0:T(8,128)(2,1)}, bf16[4,128,768]{2,1,0:T(8,128)(2,1)}, bf16[4,128,768]{2,1,0:T(8,128)(2,1)}, f32[16,768]{1,0:T(8,128)}) custom-call(bf16[4,128,768]{2,1,0:T(8,128)(2,1)} %x_in.1, bf16[3,192,768]{2,1,0:T(8,128)(2,1)} %bitcast.7, bf16[192,768]{1,0:T(8,128)(2,1)} %ao_in.1, bf16[2,192,768]{2,1,0:T(8,128)(2,1)} %bitcast.8, ...), custom_call_target="tpu_custom_call" | custom-call | tf_op jit(solution)/shard_map/layers/pallas_call | solution.py:1189
  231.9 0.0 copy-done.3
  231.9 0.0 copy-start.1
  231.9 1.1 copy-done.1
  233.0 0.0 copy-start.2
  233.0 0.8 copy-done.2
  233.8 0.0 copy-start.4
  233.8 8.6 %widen.1 = (f32[4,128,768]{2,1,0:T(8,128)}, f32[3,192,768]{2,1,0:T(8,128)}, f32[192,768]{1,0:T(8,128)}, f32[2,192,768]{2,1,0:T(8,128)}, f32[192,768]{1,0:T(8,128...) custom-call(bf16[4480,768]{1,0:T(8,128)(2,1)} %get-tuple-element.28., ...), custom_call_target="tpu_custom_call" | custom-call | tf_op jit(solution)/shard_map/widen/pallas_call | solution.py:1233
  242.5 0.0 copy-done.4
  242.5 0.9 copy.32
  (1 shorter events, 0.0 us)
Async XLA Ops:
  0.6 1.0 copy-start
  2.6 229.2 %copy-start.3 = (s32[2,2,2]{2,1,0:T(2,128)S(1)}, s32[2,2,2]{2,1,0:T(2,128)}, u32[]{:S(2)}) copy-start(s32[2,2,2]{2,1,0:T(2,128)} %plan.3) | copy-start | bytes 100
  231.9 1.1 copy-start.1
  233.0 0.8 copy-start.2
  233.8 8.7 %copy-start.4 = (bf16[4,128,768]{2,1,0:T(8,128)(2,1)S(1)}, bf16[4,128,768]{2,1,0:T(8,128)(2,1)}, u32[]{:S(2)}) copy-start(bf16[4,128,768]{2,1,0:T(8,128)(2,1)} %get-tuple-element.54) | copy-start | bytes 2359300

commit v3 on v2

--- a/solution.py
+++ b/solution.py
@@ -16,7 +16,19 @@
 GROUP = 4
 PAD = 8
 TILE = 32
+SETS = (0, 1, 0, 1, 2, 2, 3)
 LANES = 256
+
+C_CUT, U_CUT, D_CUT, A_CUT = (2, 1, 2), (1, 1, 2, 2), (2, 2, 2), (2, 2, 1, 1)
+TAIL = (
+    "main", "fa", "lo", "lo", "c0", "fa", "main", "c0", "fa", "fa", "c2", "c1", "lo", "main", "c0",
+    "c2", "pw", "pw", "pw", "c0", "c2", "c1", "lo", "main", "main", "ms", "main", "c0", "c2", "c1",
+    "ms", "u1", "main", "u2", "c2", "ms", "u1", "lo", "main", "c1", "u3", "u0", "u2", "d0", "ms",
+    "u1", "w1", "u3", "a0", "lo", "d1", "u0", "d2", "d0", "ms", "w1", "u2", "a0", "d1", "d2", "ms",
+    "w1", "a1", "a3", "u3", "a3", "a2", "a0", "a3", "c1", "u0", "a2", "d0", "u2", "u1", "a1", "ig",
+    "d1", "u3", "d2", "u0", "ms", "d0", "a0", "a3", "d1", "d2", "a2", "a1", "a2", "a0", "a3", "a1",
+    "ig", "a2", "ig", "a1", "ig",
+)
 
 F32 = jnp.float32
 BF16 = jnp.bfloat16
@@ -91,12 +103,29 @@
         self.down1_at, at = at, at + hidden
         self.all_rows = at
         self.kernel_at = self.conv_at + 3 * heads_width
-        self.pieces = {
-            "conv": self.cut(self.conv_at, conv_rows, 1),
-            "up": self.cut(self.up_at, width, 2),
-            "down": self.cut(self.down_at, hidden, 2),
-            "attn": self.cut(self.attn_at, 4 * heads_width, 2),
-        }
+        half, step = width // 2, width // 6
+        self.pieces, self.groups = {}, {}
+
+        def cut(name, start, stride, sizes):
+            at = start
+            self.groups[name] = []
+            for i, size in enumerate(sizes):
+                size = step * size // 2
+                key = name + str(i)
+                self.pieces[key] = (at, stride or size, size, stride > 0)
+                self.groups[name].append(key)
+                at += size if stride else 2 * size
+
+        cut("c", self.conv_at, 0, C_CUT)
+        cut("u", self.up_at, half, U_CUT)
+        cut("d", self.down_at, half, D_CUT)
+        cut("a", self.attn_at, 0, A_CUT)
+        self.xr_rows = self.z_rows = 0
+        for _, _, size, paired in self.pieces.values():
+            least = size // (dp // 2)
+            assert least * (dp // 2) == size and least % 16 == 0
+            self.xr_rows += size - least + (0 if paired else size)
+            self.z_rows += least
         self.stores = [
             (self.conv_at, self.up_at),
             (self.up_at, width + hidden),
@@ -106,12 +135,6 @@
         self.bits = dp.bit_length() - 1
         assert dp == 1 << self.bits and dp <= 8
         self.misc_rows = 16
-        self.sets = 3 if dp <= 2 else 2
-
-    def cut(self, start, rows, count):
-        step = rows // count
-        assert step * count == rows and step % (16 * self.dp) == 0
-        return [(start + i * step, step) for i in range(count)]
 
 
 def main_kernel(
@@ -157,6 +180,7 @@
     units,
     slope,
     dbefore,
+    last_units,
     value,
     sig,
     gated,
@@ -183,7 +207,10 @@
     za,
     zb,
     factors,
-    sums,
+    pair,
+    punits,
+    pslope,
+    pdbefore,
     misc,
     misc_in,
     load_sem,
@@ -245,13 +272,13 @@
         return copy
 
     def send_slot(name, ref, e, t, dst, target, slot=None):
-        copy = remote(ref.at[e % lay.sets, t], dst.at[e % lay.sets, t], target, slots() if slot is None else slot)
+        copy = remote(ref.at[SETS[e], t], dst.at[SETS[e], t], target, slots() if slot is None else slot)
         copy.start()
-        leaving[name, e % lay.sets, t] = copy.wait_send
+        leaving[name, SETS[e], t] = copy.wait_send
         return copy
 
     def reuse(name, e, t):
-        wait = leaving.pop((name, e % lay.sets, t), None)
+        wait = leaving.pop((name, SETS[e], t), None)
         if wait is not None:
             wait()
 
@@ -311,7 +338,7 @@
     def exchange_send(e, t):
         reuse("cs", e, t)
         reuse("ys", e, t)
-        at = e % lay.sets
+        at = SETS[e]
 
         def body(i, carry):
             rows = block(i * TILE, TILE)
@@ -331,7 +358,7 @@
 
     def sums_across(e, t, core_copy, start=True):
         core_copy.wait_recv()
-        at = e % lay.sets
+        at = SETS[e]
 
         def body(i, carry):
             rows = block(i * TILE, TILE)
@@ -343,11 +370,11 @@
             return send_slot("ys", ys, e, t, yr, across)
 
     def total_tile(e, t, rows):
-        return ys[e % lay.sets, t, rows].astype(F32) + yr[e % lay.sets, t, rows].astype(F32)
+        return ys[SETS[e], t, rows].astype(F32) + yr[SETS[e], t, rows].astype(F32)
 
     def send_half(e):
         slot = slots()
-        at = e % lay.sets
+        at = SETS[e]
         out = remote(ys.at[at, 1 - high], yr.at[at, 1 - high], across, slot)
         out.start()
         leaving["ys", at, 0] = out.wait_send
@@ -359,21 +386,33 @@
         )
         misc[8:16] += jnp.where(cell, amount, 0.0)
 
-    def run_exchange(e, work, finish, during=None):
-        core, y = [None, None], [None, None]
+    core_copies, y_copies, gathered = {}, {}, {}
+
+    def begin(e, t, work):
+        work(t)
+        core_copies[e, t] = exchange_send(e, t)
+
+    def cross(e, t):
+        y_copies[e, t] = sums_across(e, t, core_copies[e, t])
+
+    def end(e, t, finish):
+        y_copies[e, t].wait_recv()
+        gathered[e, t] = finish(t)
+
+    pair_peer, pair_on = replica_bit(lay.bits - 1)
+    pair_copies = {}
+    halfway = lay.hidden // 2
+    half_lanes = pl.ds(pl.multiple_of(pair_on * halfway, 128), halfway)
+
+    def to_pair(which, t, src):
+        rows = own_rows(t)
+        pair_copies[which, t] = send(src.at[rows], pair.at[which, rows], pair_peer)
+
+    def pass_on(which):
         for t in range(2):
-            work(t)
-            core[t] = exchange_send(e, t)
-            if t == 1:
-                y[0] = sums_across(e, 0, core[0])
-        y[1] = sums_across(e, 1, core[1])
-        if during is not None:
-            during()
-        last = []
-        for t in range(2):
-            y[t].wait_recv()
-            last.append(finish(t))
-        return last
+            pair_copies[which, t].wait_recv()
+            rows = own_rows(t)
+            pair_copies[which, t] = send(pair.at[which, rows], pair.at[which, rows], side)
 
     def forward_finish(e, k, keep_normed):
         def finish(t):
@@ -400,7 +439,10 @@
                 add_stat(4 + k, whole_sum(squares[1]) * used)
 
             rows = own_rows(t)
-            return send(hid.at[k + 1, rows], hid.at[k + 1, rows], side)
+            copy = send(hid.at[k + 1, rows], hid.at[k + 1, rows], side)
+            if k == 0:
+                to_pair(0, t, hid.at[1])
+            return copy
 
         return finish
 
@@ -425,47 +467,56 @@
             misc[4 + k : 5 + k] += jnp.sum(terms[1], axis=0, keepdims=True)
 
         rows = own_rows(t)
-        return send(dfull.at[k, rows], dfull.at[k, rows], side)
-
-    def marked_total(e, values):
+        copy = send(dfull.at[k, rows], dfull.at[k, rows], side)
+        if k == 1:
+            to_pair(1, t, dfull.at[1])
+        return copy
+
+    def marked_total(e, values, during=None):
         ms[e] = values.astype(BF16)
         core = send(ms.at[e], mr.at[e], side)
         core.wait_recv()
         mys[e] = (ms[e].astype(F32) + mr[e].astype(F32)).astype(BF16)
         y = send(mys.at[e], myr.at[e], across)
+        if during is not None:
+            during()
         y.wait_recv()
         return mys[e].astype(F32) + myr[e].astype(F32)
 
-    def reduce_piece(start, rows):
-        xr_at, z_at = reduce_piece.xr_at, reduce_piece.z_at
-        reduce_piece.xr_at += rows - rows // lay.dp
-        reduce_piece.z_at += rows // lay.dp
-        first, size = start, rows
+    def reduce_piece(base, stride, size, paired):
         steps = []
-        for bit in reversed(range(lay.bits)):
-            half = size // 2
+        first, bit = base, lay.bits - 1
+        while bit >= 0:
             peer, on = replica_bit(bit)
-            keep = first + on * half
-            give = first + (1 - on) * half
-            copy = send(
-                grads.at[pl.ds(pl.multiple_of(give, 16), half)],
-                xr.at[pl.ds(xr_at, half)],
-                peer,
-            )
-            yield
-            copy.wait_recv()
-            step = math.gcd(half, 64)
-
-            def body(i, carry, keep=keep, xr_at=xr_at, step=step):
-                here = pl.ds(pl.multiple_of(keep + i * step, 16), step)
-                there = pl.ds(pl.multiple_of(xr_at + i * step, 16), step)
-                grads[here] = (grads[here].astype(F32) + xr[there].astype(F32)).astype(BF16)
-                return carry
-
-            tiles(half // step, body)
-            xr_at += half
-            steps.append((first, size, keep, give, half, peer))
-            first, size = keep, half
+            keep = first + on * stride
+            give = first + (1 - on) * stride
+            if not paired:
+                xr_at = reduce_piece.xr_at
+                reduce_piece.xr_at += size
+                copy = send(
+                    grads.at[pl.ds(pl.multiple_of(give, 16), size)],
+                    xr.at[pl.ds(xr_at, size)],
+                    peer,
+                )
+                yield
+                copy.wait_recv()
+                step = math.gcd(size, 64)
+
+                def body(i, carry, keep=keep, xr_at=xr_at, step=step):
+                    here = pl.ds(pl.multiple_of(keep + i * step, 16), step)
+                    there = pl.ds(pl.multiple_of(xr_at + i * step, 16), step)
+                    grads[here] = (grads[here].astype(F32) + xr[there].astype(F32)).astype(BF16)
+                    return carry
+
+                tiles(size // step, body)
+            steps.append((keep, give, size, peer))
+            paired = False
+            first, bit = keep, bit - 1
+            if bit >= 0:
+                size = size // 2
+                stride = size
+        z_at = reduce_piece.z_at
+        reduce_piece.z_at += size
         mine = pl.ds(pl.multiple_of(first, 16), size)
         z_rows = pl.ds(z_at, size)
         step = math.gcd(size, 64)
@@ -482,6 +533,14 @@
                 )
             return remote(final.at[mine], final.at[mine], (end_of, replica, member), slot_c)
 
+        steps.reverse()
+        gather_slots = [slots() for _ in steps]
+
+        def gather(at, arriving=False):
+            keep, give, half, peer = steps[at]
+            rows = pl.ds(pl.multiple_of(give if arriving else keep, 16), half)
+            return remote(final.at[rows], final.at[rows], peer, gather_slots[at])
+
         @pl.when(is_end)
         def _():
             z_copy("a").start()
@@ -515,22 +574,22 @@
 
             tiles(size // step, body)
             z_copy("c").start()
+            gather(0).start()
 
         yield
 
         @pl.when(is_end)
         def _():
             z_copy("c").wait_recv()
-
-        for first, size, keep, give, half, peer in reversed(steps):
-            here = pl.ds(pl.multiple_of(keep, 16), half)
-            there = pl.ds(pl.multiple_of(give, 16), half)
-            slot = slots()
-            out = remote(final.at[here], final.at[here], peer, slot)
-            out.start()
-            closing.append(out.wait_send)
-            yield
-            remote(final.at[there], final.at[there], peer, slot).wait_recv()
+            gather(0).start()
+
+        yield
+        for at in range(len(steps)):
+            if at > 0:
+                gather(at).start()
+                yield
+            gather(at, True).wait_recv()
+            closing.append(gather(at).wait_send)
 
         def close():
             @pl.when(is_end)
@@ -546,27 +605,62 @@
 
     reduce_piece.xr_at = 0
     reduce_piece.z_at = 0
-    running = []
-
-    def launch(name):
-        for start, rows in lay.pieces[name]:
-            piece = reduce_piece(start, rows)
-            next(piece)
-            running.append(piece)
-
-    def pump(count=1):
-        for _ in range(count):
-            for piece in list(running):
+    running = {}
+    summed = set()
+
+    def launch(*names):
+        for name in names:
+            spec = lay.pieces.get(name)
+            running[name] = reduce_piece(*spec)
+            next(running[name])
+
+    def start(name, task):
+        running[name] = task
+        next(task)
+
+    def pump(*names):
+        for name in names:
+            if name in running:
                 try:
-                    next(piece)
+                    next(running[name])
                 except StopIteration:
-                    running.remove(piece)
+                    del running[name]
+
+    def line_gather(view):
+        right, left = [slots() for _ in range(3)], [slots() for _ in range(3)]
+
+        def hop(k, to_right, at):
+            origin = at - k if to_right else at + k
+            target = (section + (1 if to_right else -1), replica, member)
+            return remote(view(origin), view(origin), target, (right if to_right else left)[k])
+
+        def sends(k, action):
+            @pl.when((section >= k) & (section < SECTIONS - 1))
+            def _():
+                getattr(hop(k, True, section), action)()
+
+            @pl.when((section + k < SECTIONS) & (section > 0))
+            def _():
+                getattr(hop(k, False, section), action)()
+
+        def arrivals(k):
+            @pl.when(section > k)
+            def _():
+                hop(k, True, section - 1).wait_recv()
+
+            @pl.when(section + k < SECTIONS - 1)
+            def _():
+                hop(k, False, section + 1).wait_recv()
+
+        for k in range(SECTIONS - 1):
+            sends(k, "start")
+            closing.append(functools.partial(sends, k, "wait_send"))
+            yield
+            arrivals(k)
 
     def final_store(at):
         rows = pl.ds(*lay.stores[at])
         return pltpu.make_async_copy(final.at[rows], final_out.at[rows], store_sem.at[at])
-
-    stored = [0]
 
     def store_final(at):
         final_store(at).start()
@@ -601,6 +695,8 @@
         rows = pl.ds(chunk * t, chunk)
         mixture = jnp.zeros((chunk, hw), F32)
         for i in range(local_heads):
+            if t == 1 and i == 1:
+                cross(0, 0)
             scores = dot_lanes(qkv[0, rows] * head_low[i], qkv[1]) * scale
             top = jnp.max(scores, axis=-1, keepdims=True)
             powers = jnp.exp(scores - top)
@@ -610,28 +706,36 @@
         mix[rows] = mixture.astype(BF16)
         partial[...] = dot(mix[rows], wao[...])
 
-    gathered = run_exchange(0, attention_work, forward_finish(0, 0, True))
-
+    begin(0, 0, attention_work)
+    begin(0, 1, attention_work)
+    cross(0, 1)
     loads["up"].wait()
     loads["down"].wait()
 
-    def ffn_forward(layer, src, rows, keep):
+    def ffn_forward(layer, src, rows, units_here, slope_here=None):
         def body(i, carry):
             lanes = block(i * LANES, LANES)
-            unit, slope_here = gelu_parts(dot(src[rows], wup[layer, :, lanes]))
-            units[rows, lanes] = unit.astype(BF16)
-            if keep:
-                slope[rows, lanes] = slope_here
+            unit, steep = gelu_parts(dot(src[rows], wup[layer, :, lanes]))
+            units_here[:, lanes] = unit.astype(BF16)
+            if slope_here is not None:
+                slope_here[:, lanes] = steep
             return carry
 
         tiles(lay.hidden // LANES, body)
-        partial[...] = dot(units[rows], wdown[layer])
+        partial[...] = dot(units_here[...], wdown[layer])
 
     def ffn0_work(t):
-        gathered[t].wait_recv()
-        ffn_forward(0, hid.at[1], pl.ds(chunk * t, chunk), True)
-
-    gathered = run_exchange(1, ffn0_work, forward_finish(1, 1, True))
+        gathered[0, t].wait_recv()
+        rows = pl.ds(chunk * t, chunk)
+        ffn_forward(0, hid.at[1], rows, units.at[rows], slope.at[rows])
+
+    attention_finish = forward_finish(0, 0, True)
+    end(0, 0, attention_finish)
+    begin(1, 0, ffn0_work)
+    end(0, 1, attention_finish)
+    cross(1, 0)
+    begin(1, 1, ffn0_work)
+    cross(1, 1)
 
     loads["cin"].wait()
     loads["co"].wait()
@@ -639,14 +743,22 @@
     for buffer in (gated, dconv):
         buffer[0:PAD] = edge
         buffer[PAD + lay.seq : 2 * PAD + lay.seq] = edge
-    for t in range(2):
-        gathered[t].wait_recv()
+
+    def conv_gates(t):
+        gathered[1, t].wait_recv()
         rows = pl.ds(chunk * t, chunk)
         value_here = dot_lanes(hid[2, rows], wcin[0])
         sig_here = jax.nn.sigmoid(dot_lanes(hid[2, rows], wcin[1]))
         value[rows] = value_here
         sig[rows] = sig_here
         gated[pl.ds(PAD + chunk * t, chunk)] = value_here * sig_here
+
+    ffn0_finish = forward_finish(1, 1, True)
+    pass_on(0)
+    end(1, 0, ffn0_finish)
+    conv_gates(0)
+    end(1, 1, ffn0_finish)
+    conv_gates(1)
     tap_tile = 64
 
     def taps(i, carry):
@@ -663,7 +775,62 @@
     spots = hits[...]
     conv_marked = dot_rows(spots, conv[...]).astype(BF16)
     stream = dot_rows(spots, hid[2])
-    branch = marked_total(0, dot(conv_marked, wco[...]))
+
+    def pair_up(t):
+        pair_copies[0, t].wait_recv()
+        rows = pl.ds(chunk * t, chunk)
+        unit, slope_here = gelu_parts(dot(pair[0, rows], wup[0, :, half_lanes]))
+        punits[rows] = unit.astype(BF16)
+        pslope[rows] = slope_here
+
+
+    def conv_work(t):
+        partial[...] = dot(conv[pl.ds(chunk * t, chunk)], wco[...])
+
+    def ffn1_work(t):
+        gathered[5, t].wait_recv()
+        ffn_forward(1, hid.at[3], pl.ds(chunk * t, chunk), last_units)
+
+    def layer_output():
+        last_finish = forward_finish(5, 2, False)
+        begin(5, 0, conv_work)
+        begin(5, 1, conv_work)
+        cross(5, 0)
+        yield
+        cross(5, 1)
+        yield
+        end(5, 0, last_finish)
+        yield
+        end(5, 1, last_finish)
+        yield
+        begin(6, 0, ffn1_work)
+        yield
+        begin(6, 1, ffn1_work)
+        for t in range(2):
+            sums_across(6, t, core_copies[6, t], start=False)
+        last = send_half(6)
+        yield
+        last.wait_recv()
+
+        def layer_body(i, carry):
+            rows = block(i * TILE, TILE)
+            stream = hid[3, block(member * part + i * TILE, TILE)].astype(F32)
+            branch = total_tile(6, high, rows)
+            norm, _ = normalise(stream + branch)
+            result = (norm * gain[3:4] + bias[3:4]) * used
+            layer_rows[section, rows] = result.astype(BF16)
+            return (carry[0] + fold(stream * stream), carry[1] + fold(branch * branch))
+
+        zero = jnp.zeros((8, width), F32)
+        squares = tiles(part // TILE, layer_body, (zero, zero))
+        add_stat(3, whole_sum(squares[0]) * used)
+        add_stat(7, whole_sum(squares[1]) * used)
+        summed.add("rows")
+        yield from line_gather(lambda at: layer_rows.at[at])
+
+    branch = marked_total(
+        0, dot(conv_marked, wco[...]), lambda: start("lo", layer_output())
+    )
     norm2, inv2 = normalise(stream + branch)
     mnorm[0] = norm2
     mh[...] = (norm2 * gain[2:3] + bias[2:3]).astype(BF16)
@@ -676,7 +843,12 @@
         return carry
 
     tiles(lay.hidden // LANES, marked_up)
-    branch = marked_total(1, dot(munits[...], wdown[1]))
+
+    def beside_units():
+        pump("lo")
+        pair_up(0)
+
+    branch = marked_total(1, dot(munits[...], wdown[1]), beside_units)
     norm3, inv3 = normalise(mh[...].astype(F32) + branch)
     once = jnp.where(member == 0, 1.0, 0.0).astype(F32)
     dy = cotangent[...].astype(F32) * used
@@ -690,10 +862,24 @@
     here = pl.ds(pl.multiple_of(section * per_section + replica * marked, 16), marked)
     factors[0, here] = mh[...]
     factors[1, here] = df3
-    factor_copies = [
-        send(factors.at[low, here], factors.at[low, here], replica_peer(by))
-        for by in range(1, lay.dp)
-    ]
+
+    def spread_factors():
+        copies = [
+            send(factors.at[low, here], factors.at[low, here], replica_peer(by))
+            for by in range(1, lay.dp)
+        ]
+        yield
+        for copy in copies:
+            copy.wait_recv()
+        yield from line_gather(
+            lambda at: factors.at[low, pl.ds(pl.multiple_of(at * per_section, 16), per_section)]
+        )
+        slot = slots()
+        send(factors.at[low], factors.at[low], side, slot)
+        yield
+        remote(factors.at[1 - low], factors.at[1 - low], side, slot).wait_recv()
+
+    start("fa", spread_factors())
 
     def marked_down(i, carry):
         lanes = block(i * LANES, LANES)
@@ -702,20 +888,18 @@
         return carry
 
     tiles(lay.hidden // LANES, marked_down)
-    dy = mdz[0] + marked_total(2, dot_lanes(munits[...], wup[1]))
-    for copy in factor_copies:
-        copy.wait_recv()
-    ours = pl.ds(pl.multiple_of(section * per_section, 16), per_section)
-    factor_copies = [
-        send(factors.at[low, ours], factors.at[low, ours], section_peer(by))
-        for by in range(1, SECTIONS)
-    ]
+    def beside_down():
+        pump("lo")
+        pump("lo")
+        pair_up(1)
+
+    dy = mdz[0] + marked_total(2, dot_lanes(munits[...], wup[1]), beside_down)
+    pump("fa")
     norm2 = mnorm[0]
     misc[2:3] += once * jnp.sum(dy * norm2, axis=0, keepdims=True)
     misc[6:7] += once * jnp.sum(dy, axis=0, keepdims=True)
     dz2 = norm_pull(dy, norm2, inv2, gain[2:3])
     dz2_terms = two_terms(dz2)
-    mdz[1] = dz2
     df2 = dz2.astype(BF16)
 
     def spread(rows, terms):
@@ -752,10 +936,6 @@
     grads[pl.ds(lay.kernel_at, 16), 0:hw] = jnp.concatenate(
         [kernel_rows, jnp.zeros((8, hw), F32)], axis=0
     ).astype(BF16)
-    for j in range(2):
-        grads[pl.ds(lay.conv_at + j * hw, hw)] = dot_rows(dgates[j], hid[2]).astype(BF16)
-    grads[pl.ds(lay.conv_at + 2 * hw, hw)] = dot_rows(conv_marked, df2).astype(BF16)
-    launch("conv")
 
     def conv_back_work(t):
         rows = pl.ds(chunk * t, chunk)
@@ -767,10 +947,8 @@
 
         return norm_back_rows(1, t, grad_tile)
 
-    gathered = run_exchange(2, conv_back_work, conv_back_finish)
-
     def ffn0_back_work(t):
-        gathered[t].wait_recv()
+        gathered[2, t].wait_recv()
         rows = pl.ds(chunk * t, chunk)
 
         def body(i, carry):
@@ -787,30 +965,42 @@
             0, t, lambda rows, place: normed[1, t, rows] + total_tile(3, t, rows)
         )
 
-    def weight_rows(start, left, right, count):
-        def body(i, carry):
-            lanes = block(i * LANES, LANES)
-            grads[pl.ds(pl.multiple_of(start + i * LANES, 16), LANES)] = dot_rows(
-                left[:, lanes], right[...]
-            ).astype(BF16)
-            return carry
-
-        tiles(count // LANES, body)
-
-    def ffn0_weights():
-        pump()
-        weight_rows(lay.up_at, hid.at[1], dbefore, width)
-        launch("up")
-        pump()
-        weight_rows(lay.down_at, units0, dfull.at[1], lay.hidden)
-        launch("down")
-
-    units0 = units
-    gathered = run_exchange(3, ffn0_back_work, ffn0_back_finish, ffn0_weights)
-
-    dkv[...] = jnp.zeros_like(dkv)
-    for t in range(2):
-        gathered[t].wait_recv()
+    up_rows = pl.ds(pl.multiple_of(lay.up_at + pair_on * halfway, 16), halfway)
+    down_rows = pl.ds(pl.multiple_of(lay.down_at + pair_on * halfway, 16), halfway)
+
+    def own_weights():
+        left = dbefore[:, half_lanes]
+        for q in range(2):
+            lanes = pl.ds(q * halfway, halfway)
+            grads[up_rows, lanes] = dot_rows(hid[1, :, lanes], left).astype(BF16)
+        grads[down_rows] = dot_rows(units[:, half_lanes], dfull[1]).astype(BF16)
+
+    def pair_weights():
+        for t in range(2):
+            pair_copies[1, t].wait_recv()
+            rows = pl.ds(chunk * t, chunk)
+            grad_units = dot_lanes(pair[1, rows], wdown[0, half_lanes])
+            pdbefore[rows] = (grad_units * pslope[rows]).astype(BF16)
+        left = pdbefore[...]
+        for q in range(2):
+            lanes = pl.ds(q * halfway, halfway)
+            total = grads[up_rows, lanes].astype(F32) + dot_rows(pair[0, :, lanes], left)
+            grads[up_rows, lanes] = total.astype(BF16)
+        launch(*lay.groups["u"])
+        total = grads[down_rows].astype(F32) + dot_rows(punits[...], pair[1])
+        grads[down_rows] = total.astype(BF16)
+        launch(*lay.groups["d"])
+
+    def attention_back_work(t):
+        rows = pl.ds(chunk * t, chunk)
+        partial[...] = (
+            dot(dqkv[0, rows], wqkv[0])
+            + dot(dqkv[1, rows], wqkv[1])
+            + dot(dqkv[2, rows], wqkv[2])
+        )
+
+    def attention_back_rows(t):
+        gathered[3, t].wait_recv()
         rows = pl.ds(chunk * t, chunk)
         dmix[rows] = dot_lanes(dfull[0, rows], wao[...]).astype(BF16)
         grad_queries = jnp.zeros((chunk, hw), F32)
@@ -826,31 +1016,55 @@
             dkv[0] += jnp.where(on, dot_rows(grad_scores, qkv[0, rows]), 0.0)
             dkv[1] += jnp.where(on, dot_rows(chances.astype(BF16), dmix[rows]), 0.0)
         dqkv[0, rows] = (grad_queries * scale).astype(BF16)
-        pump()
-    dqkv[1] = (dkv[0] * scale).astype(BF16)
-    dqkv[2] = dkv[1].astype(BF16)
-
-    def attention_back_work(t):
-        rows = pl.ds(chunk * t, chunk)
-        partial[...] = (
-            dot(dqkv[0, rows], wqkv[0])
-            + dot(dqkv[1, rows], wqkv[1])
-            + dot(dqkv[2, rows], wqkv[2])
-        )
-
-    core = []
-    for t in range(2):
-        attention_back_work(t)
-        core.append(exchange_send(4, t))
-    for t in range(2):
-        sums_across(4, t, core[t], start=False)
-    last = send_half(4)
-    for j in range(3):
-        grads[pl.ds(lay.attn_at + j * hw, hw)] = dot_rows(dqkv[j], hid[0]).astype(BF16)
-    grads[pl.ds(lay.attn_at + 3 * hw, hw)] = dot_rows(mix[...], dfull[0]).astype(BF16)
-    launch("attn")
-    pump()
-    last.wait_recv()
+
+    waits = {}
+
+    def backward():
+        begin(2, 0, conv_back_work)
+        begin(2, 1, conv_back_work)
+        cross(2, 0)
+        cross(2, 1)
+        for j in range(2):
+            grads[pl.ds(lay.conv_at + j * hw, hw)] = dot_rows(dgates[j], hid[2]).astype(BF16)
+        grads[pl.ds(lay.conv_at + 2 * hw, hw)] = dot_rows(conv_marked, df2).astype(BF16)
+        launch(*lay.groups["c"])
+        yield
+        end(2, 0, conv_back_finish)
+        begin(3, 0, ffn0_back_work)
+        yield
+        end(2, 1, conv_back_finish)
+        cross(3, 0)
+        begin(3, 1, ffn0_back_work)
+        cross(3, 1)
+        yield
+        end(3, 0, ffn0_back_finish)
+        yield
+        end(3, 1, ffn0_back_finish)
+        summed.add("norms")
+        yield
+        dkv[...] = jnp.zeros_like(dkv)
+        attention_back_rows(0)
+        yield
+        attention_back_rows(1)
+        dqkv[1] = (dkv[0] * scale).astype(BF16)
+        dqkv[2] = dkv[1].astype(BF16)
+        for t in range(2):
+            begin(4, t, attention_back_work)
+        for t in range(2):
+            sums_across(4, t, core_copies[4, t], start=False)
+        waits["input"] = send_half(4)
+        yield
+        for j in range(3):
+            grads[pl.ds(lay.attn_at + j * hw, hw)] = dot_rows(dqkv[j], hid[0]).astype(BF16)
+        grads[pl.ds(lay.attn_at + 3 * hw, hw)] = dot_rows(mix[...], dfull[0]).astype(BF16)
+        launch(*lay.groups["a"])
+
+    def feed_forward_weights():
+        own_weights()
+        yield
+        pass_on(1)
+        yield
+        pair_weights()
 
     def input_body(i, carry):
         rows = block(i * TILE, TILE)
@@ -858,137 +1072,127 @@
         input_rows[section, rows] = (normed[0, high, rows] + total).astype(BF16)
         return carry
 
-    tiles(part // TILE, input_body)
-    end_copies = [
-        send(input_rows.at[section], input_rows.at[section], section_peer(by))
-        for by in range(1, SECTIONS)
-    ]
-    pump()
-
-    def conv_work(t):
-        partial[...] = dot(conv[pl.ds(chunk * t, chunk)], wco[...])
-
-    gathered = run_exchange(5, conv_work, forward_finish(5, 2, False), pump)
-    core = []
-    for t in range(2):
-        gathered[t].wait_recv()
-        ffn_forward(1, hid.at[3], pl.ds(chunk * t, chunk), False)
-        core.append(exchange_send(6, t))
-        pump()
-    for t in range(2):
-        sums_across(6, t, core[t], start=False)
-    last = send_half(6)
-    pump()
-
-    for copy in factor_copies:
-        copy.wait_recv()
-    shared = slots()
-    send(factors.at[low], factors.at[low], side, shared)
-    remote(factors.at[1 - low], factors.at[1 - low], side, shared).wait_recv()
+    def input_gradient():
+        waits["input"].wait_recv()
+        tiles(part // TILE, input_body)
+        yield from line_gather(lambda at: input_rows.at[at])
+
     group_rows = GROUP * marked
     groups = SECTIONS * per_section // group_rows
-    for group in range(groups):
-        rows = pl.ds(group * group_rows, group_rows)
-
-        def recompute(j, carry):
-            lanes = block(j * LANES, LANES)
-            unit, slope_here = gelu_parts(dot(factors[0, rows], wup[1, :, lanes]))
-            units[0:group_rows, lanes] = unit.astype(BF16)
-            grad_units = dot_lanes(factors[1, rows], wdown[1, lanes])
-            dbefore[0:group_rows, lanes] = (grad_units * slope_here).astype(BF16)
-            return carry
-
-        tiles(lay.hidden // LANES, recompute)
-
-        def last_weights(i, carry):
-            lanes = block(i * LANES, LANES)
-            by_up = dot_rows(factors[0, rows, lanes], dbefore[0:group_rows])
-            by_down = dot_rows(units[0:group_rows, lanes], factors[1, rows])
-            if group > 0:
-                by_up = by_up + sums[0, lanes]
-                by_down = by_down + sums[1, lanes]
-            if group < groups - 1:
-                sums[0, lanes] = by_up
-                sums[1, lanes] = by_down
-            else:
-                at = pl.multiple_of(i * LANES, LANES)
-                final[pl.ds(lay.up1_at + at, LANES)] = by_up.astype(BF16)
-                final[pl.ds(lay.down1_at + at, LANES)] = by_down.astype(BF16)
-            return carry
-
-        tiles(width // LANES, last_weights)
-        pump()
-    last.wait_recv()
-
-    def layer_body(i, carry):
-        rows = block(i * TILE, TILE)
-        stream = hid[3, block(member * part + i * TILE, TILE)].astype(F32)
-        branch = total_tile(6, high, rows)
-        norm, _ = normalise(stream + branch)
-        result = (norm * gain[3:4] + bias[3:4]) * used
-        layer_rows[section, rows] = result.astype(BF16)
-        return (carry[0] + fold(stream * stream), carry[1] + fold(branch * branch))
-
-    zero = jnp.zeros((8, width), F32)
-    squares = tiles(part // TILE, layer_body, (zero, zero))
-    add_stat(3, whole_sum(squares[0]) * used)
-    add_stat(7, whole_sum(squares[1]) * used)
-    end_copies += [
-        send(layer_rows.at[section], layer_rows.at[section], section_peer(by))
-        for by in range(1, SECTIONS)
-    ]
-
-    hops = [side, across] + [replica_bit(bit)[0] for bit in range(lay.bits)]
-    for at, peer in enumerate(hops):
-        misc_in[2 * at] = misc[...]
-        copy = send(misc_in.at[2 * at], misc_in.at[2 * at + 1], peer)
-        pump()
-        copy.wait_recv()
-        misc[...] = misc_in[2 * at] + misc_in[2 * at + 1]
-    at = 2 * len(hops)
-    slot_a, slot_b, slot_c = slots(), slots(), slots()
-    to_inner = remote(misc_in.at[at], misc_in.at[at + 1], (inner_of, replica, member), slot_a)
-    to_other = remote(misc_in.at[at + 2], misc_in.at[at + 3], (other_inner, replica, member), slot_b)
-    to_end = remote(misc_out, misc_out, (end_of, replica, member), slot_c)
-
-    @pl.when(is_end)
-    def _():
-        misc_in[at] = misc[...]
-        to_inner.start()
-
-    pump()
-
-    @pl.when(is_inner)
-    def _():
-        to_inner.wait_recv()
-        misc_in[at + 2] = misc[...] + misc_in[at + 1]
-        to_other.start()
-
-    pump()
-
-    @pl.when(is_inner)
-    def _():
-        to_other.wait_recv()
-        misc_out[...] = misc_in[at + 2] + misc_in[at + 3]
-        to_end.start()
-
-    pump(8)
-
-    @pl.when(is_end)
-    def _():
-        to_end.wait_recv()
-        to_inner.wait_send()
-
-    @pl.when(is_inner)
-    def _():
-        to_other.wait_send()
-        to_end.wait_send()
-
-    for at, (start, rows) in enumerate(lay.stores):
-        if at >= stored[0]:
-            store_final(at)
-    for copy in end_copies:
-        copy.wait_recv()
+
+    def last_block():
+        assert not {"main", "pw", "fa"} & set(running)
+        for group in range(groups):
+            rows = pl.ds(group * group_rows, group_rows)
+
+            def recompute(j, carry, rows=rows):
+                lanes = block(j * LANES, LANES)
+                unit, slope_here = gelu_parts(dot(factors[0, rows], wup[1, :, lanes]))
+                units[0:group_rows, lanes] = unit.astype(BF16)
+                grad_units = dot_lanes(factors[1, rows], wdown[1, lanes])
+                dbefore[0:group_rows, lanes] = (grad_units * slope_here).astype(BF16)
+                return carry
+
+            tiles(lay.hidden // LANES, recompute)
+
+            def last_weights(i, carry, rows=rows, group=group):
+                lanes = block(i * LANES, LANES)
+                by_up = dot_rows(factors[0, rows, lanes], dbefore[0:group_rows])
+                by_down = dot_rows(units[0:group_rows, lanes], factors[1, rows])
+                wide, rest = probs.shape[2], width - probs.shape[2]
+                held = [
+                    (
+                        probs.at[i, pl.ds(j * LANES, LANES)],
+                        slope.at[pl.ds(j * LANES, LANES), block(i * rest, rest)],
+                    )
+                    for j in range(2)
+                ]
+                if group > 0:
+                    by_up = by_up + jnp.concatenate([held[0][0][...], held[0][1][...]], axis=1)
+                    by_down = by_down + jnp.concatenate([held[1][0][...], held[1][1][...]], axis=1)
+                if group < groups - 1:
+                    for (left, right), total in zip(held, (by_up, by_down)):
+                        left[...] = total[:, :wide]
+                        right[...] = total[:, wide:]
+                else:
+                    at = pl.multiple_of(i * LANES, LANES)
+                    final[pl.ds(lay.up1_at + at, LANES)] = by_up.astype(BF16)
+                    final[pl.ds(lay.down1_at + at, LANES)] = by_down.astype(BF16)
+                return carry
+
+            tiles(width // LANES, last_weights)
+            yield
+        store_final(3)
+
+    def small_sums():
+        assert summed >= {"norms", "rows"}
+        hops = [side, across] + [replica_bit(bit)[0] for bit in range(lay.bits)]
+        for at, peer in enumerate(hops):
+            misc_in[2 * at] = misc[...]
+            copy = send(misc_in.at[2 * at], misc_in.at[2 * at + 1], peer)
+            yield
+            copy.wait_recv()
+            misc[...] = misc_in[2 * at] + misc_in[2 * at + 1]
+        at = 2 * len(hops)
+        slot_a, slot_b, slot_c = slots(), slots(), slots()
+        to_inner = remote(misc_in.at[at], misc_in.at[at + 1], (inner_of, replica, member), slot_a)
+        to_other = remote(
+            misc_in.at[at + 2], misc_in.at[at + 3], (other_inner, replica, member), slot_b
+        )
+        to_end = remote(misc_out, misc_out, (end_of, replica, member), slot_c)
+
+        @pl.when(is_end)
+        def _():
+            misc_in[at] = misc[...]
+            to_inner.start()
+
+        yield
+
+        @pl.when(is_inner)
+        def _():
+            to_inner.wait_recv()
+            misc_in[at + 2] = misc[...] + misc_in[at + 1]
+            to_other.start()
+
+        yield
+
+        @pl.when(is_inner)
+        def _():
+            to_other.wait_recv()
+            misc_out[...] = misc_in[at + 2] + misc_in[at + 3]
+            to_end.start()
+
+        yield
+
+        @pl.when(is_end)
+        def _():
+            to_end.wait_recv()
+            to_inner.wait_send()
+
+        @pl.when(is_inner)
+        def _():
+            to_other.wait_send()
+            to_end.wait_send()
+
+    later = {
+        "main": backward,
+        "pw": feed_forward_weights,
+        "ig": input_gradient,
+        "w1": last_block,
+        "ms": small_sums,
+    }
+    for name in TAIL:
+        if name in later:
+            start(name, later.pop(name)())
+        elif name.startswith("s"):
+            store_final(int(name[1]))
+        else:
+            pump(name)
+    assert not later
+    while running:
+        pump(*list(running))
+    for at in range(3):
+        store_final(at)
     for at in range(len(lay.stores)):
         final_store(at).wait()
     for wait in closing + list(leaving.values()):
@@ -1067,12 +1271,23 @@
             total = total + jnp.where(plan[r, i, 1] >= 0, 1.0, 0.0).astype(F32)
         counts = jnp.where(row == r, total, counts)
     rms[...] = jnp.sqrt(misc[8 : 8 + rms.shape[0], 0:8] / (counts * (lay.seq * width)))
+    half = width // 2
+    for at in range(2):
+        load(at).wait()
     for at, (start, rows, _) in enumerate(blocks):
-        load(at).wait()
-
-        def body(i, carry, start=start):
+        if at >= 2:
+            load(at).wait()
+
+        def body(i, carry, start=start, at=at):
             here = pl.ds(pl.multiple_of(start + i * 32, 16), 32)
-            wide[here] = narrow[here].astype(F32)
+            if at >= 2:
+                wide[here] = narrow[here].astype(F32)
+            else:
+                for q in range(2):
+                    there = pl.ds(pl.multiple_of(lay.up_at + q * half + i * 32, 16), 32)
+                    wide[here, q * half : (q + 1) * half] = narrow[
+                        there, at * half : (at + 1) * half
+                    ].astype(F32)
             return carry
 
         lax.fori_loop(0, rows // 32, body, 0)
@@ -1126,7 +1341,6 @@
     vmem_spec = pl.BlockSpec(memory_space=pltpu.VMEM)
     hops = 2 + lay.bits
     all_marked = SECTIONS * dp * marked
-    z_rows = lay.rows // dp
     scratch = [
         pltpu.VMEM((lay.all_rows, width), BF16),
         pltpu.VMEM((8, hw), F32),
@@ -1151,6 +1365,7 @@
         pltpu.VMEM((seq, hidden), BF16),
         pltpu.VMEM((seq, hidden), F32),
         pltpu.VMEM((seq, hidden), BF16),
+        pltpu.VMEM((chunk, hidden), BF16),
         pltpu.VMEM((seq, hw), F32),
         pltpu.VMEM((seq, hw), F32),
         pltpu.VMEM((seq + 2 * PAD, hw), F32),
@@ -1162,22 +1377,25 @@
         pltpu.VMEM((1, marked, width), F32),
         pltpu.VMEM((marked, hidden), F32),
         pltpu.VMEM((marked, hidden), BF16),
-        pltpu.VMEM((2, marked, width), F32),
+        pltpu.VMEM((1, marked, width), F32),
         pltpu.VMEM((chunk, width), F32),
-        pltpu.VMEM((lay.sets, 2, part, width), BF16),
-        pltpu.VMEM((lay.sets, 2, part, width), BF16),
-        pltpu.VMEM((lay.sets, 2, part, width), BF16),
-        pltpu.VMEM((lay.sets, 2, part, width), BF16),
+        pltpu.VMEM((4, 2, part, width), BF16),
+        pltpu.VMEM((4, 2, part, width), BF16),
+        pltpu.VMEM((4, 2, part, width), BF16),
+        pltpu.VMEM((4, 2, part, width), BF16),
         pltpu.VMEM((3, marked, width), BF16),
         pltpu.VMEM((3, marked, width), BF16),
         pltpu.VMEM((3, marked, width), BF16),
         pltpu.VMEM((3, marked, width), BF16),
         pltpu.VMEM((lay.rows, width), BF16),
-        pltpu.VMEM((max(lay.rows - z_rows, 16), width), BF16),
-        pltpu.VMEM((z_rows, width), BF16),
-        pltpu.VMEM((z_rows, width), BF16),
+        pltpu.VMEM((lay.xr_rows, width), BF16),
+        pltpu.VMEM((lay.z_rows, width), BF16),
+        pltpu.VMEM((lay.z_rows, width), BF16),
         pltpu.VMEM((2, all_marked, width), BF16),
-        pltpu.VMEM((2, width, hidden), F32),
+        pltpu.VMEM((2, seq, width), BF16),
+        pltpu.VMEM((seq, hidden // 2), BF16),
+        pltpu.VMEM((seq, hidden // 2), F32),
+        pltpu.VMEM((seq, hidden // 2), BF16),
         pltpu.VMEM((lay.misc_rows, width), F32),
         pltpu.VMEM((2 * hops + 4, lay.misc_rows, width), F32),
         pltpu.SemaphoreType.DMA((8,)),

time: 244 us -> 184 us (0.75)
  Pallas kernels: 238 us -> 179 us
    pallas_call x1, Pallas kernels: 229 us -> 170 us  [on_device(): pl.pallas_call(functools.partial(main_kernel, lay), out_shape=(jax.ShapeD...]
where the time goes in v3:
time: 184 us
  Pallas kernels  179 us (97%)
  local copies, waits for them, and re-layouts  4.07 us (2%)
    pallas_call x1, Pallas kernels, on_device(): pl.pallas_call(functools.partial(main_kernel, lay), out_shape=(jax.ShapeD...  170 us
    pallas_call x1, Pallas kernels, on_device(): pl.pallas_call(functools.partial(widen_kernel, lay), out_shape=tuple((jax...  8.6 us

profile of v3, /device:TPU:0, one launch (start us, length us, event | category | flops | bytes accessed | tf_op | source)
XLA Modules:
  0.0 184.1 jit_solution(17861361635247375637)
XLA Ops:
  0.6 0.0 copy-start
  1.4 0.3 copy-done
  1.7 0.2 constant_dynamic-slice_fusion
  2.0 0.7 pad.4.cotangent
  2.6 0.0 copy-start.3
  2.6 170.0 %layers.1 = (bf16[4480,768]{1,0:T(8,128)(2,1)}, bf16[4,128,768]{2,1,0:T(8,128)(2,1)}, bf16[4,128,768]{2,1,0:T(8,128)(2,1)}, f32[16,768]{1,0:T(8,128)}) custom-call(bf16[4,128,768]{2,1,0:T(8,128)(2,1)} %x_in.1, bf16[3,192,768]{2,1,0:T(8,128)(2,1)} %bitcast.7, bf16[192,768]{1,0:T(8,128)(2,1)} %ao_in.1, bf16[2,192,768]{2,1,0:T(8,128)(2,1)} %bitcast.8, ...), custom_call_target="tpu_custom_call" | custom-call | tf_op jit(solution)/shard_map/layers/pallas_call | solution.py:1407
  172.7 0.0 copy-done.3
  172.7 0.0 copy-start.1
  172.7 1.1 copy-done.1
  173.8 0.0 copy-start.2
  173.8 0.8 copy-done.2
  174.6 0.0 copy-start.4
  174.6 8.6 %widen.1 = (f32[4,128,768]{2,1,0:T(8,128)}, f32[3,192,768]{2,1,0:T(8,128)}, f32[192,768]{1,0:T(8,128)}, f32[2,192,768]{2,1,0:T(8,128)}, f32[192,768]{1,0:T(8,128...) custom-call(bf16[4480,768]{1,0:T(8,128)(2,1)} %get-tuple-element.28., ...), custom_call_target="tpu_custom_call" | custom-call | tf_op jit(solution)/shard_map/widen/pallas_call | solution.py:1451
  183.2 0.0 copy-done.4
  183.2 0.9 copy.32
  (1 shorter events, 0.0 us)
Async XLA Ops:
  0.6 1.0 copy-start
  2.6 170.1 %copy-start.3 = (s32[2,2,2]{2,1,0:T(2,128)S(1)}, s32[2,2,2]{2,1,0:T(2,128)}, u32[]{:S(2)}) copy-start(s32[2,2,2]{2,1,0:T(2,128)} %plan.3) | copy-start | bytes 100
  172.7 1.1 copy-start.1
  173.8 0.8 copy-start.2
  174.6 8.6 %copy-start.4 = (bf16[4,128,768]{2,1,0:T(8,128)(2,1)S(1)}, bf16[4,128,768]{2,1,0:T(8,128)(2,1)}, u32[]{:S(2)}) copy-start(bf16[4,128,768]{2,1,0:T(8,128)(2,1)} %get-tuple-element.54) | copy-start | bytes 2359300

commit v4 on v3

--- a/solution.py
+++ b/solution.py
@@ -16,18 +16,20 @@
 GROUP = 4
 PAD = 8
 TILE = 32
+VMEM_BYTES = 55 * 2**20 + 2**17
 SETS = (0, 1, 0, 1, 2, 2, 3)
 LANES = 256
 
+KEEP = 12
 C_CUT, U_CUT, D_CUT, A_CUT = (2, 1, 2), (1, 1, 2, 2), (2, 2, 2), (2, 2, 1, 1)
 TAIL = (
-    "main", "fa", "lo", "lo", "c0", "fa", "main", "c0", "fa", "fa", "c2", "c1", "lo", "main", "c0",
-    "c2", "pw", "pw", "pw", "c0", "c2", "c1", "lo", "main", "main", "ms", "main", "c0", "c2", "c1",
-    "ms", "u1", "main", "u2", "c2", "ms", "u1", "lo", "main", "c1", "u3", "u0", "u2", "d0", "ms",
-    "u1", "w1", "u3", "a0", "lo", "d1", "u0", "d2", "d0", "ms", "w1", "u2", "a0", "d1", "d2", "ms",
-    "w1", "a1", "a3", "u3", "a3", "a2", "a0", "a3", "c1", "u0", "a2", "d0", "u2", "u1", "a1", "ig",
-    "d1", "u3", "d2", "u0", "ms", "d0", "a0", "a3", "d1", "d2", "a2", "a1", "a2", "a0", "a3", "a1",
-    "ig", "a2", "ig", "a1", "ig",
+    "main", "fa", "lo", "lo", "c0", "fa", "main", "c1", "lo", "c0", "main", "fa", "fa", "c1", "lo",
+    "c2", "pw", "main", "c0", "pw", "pw", "c1", "c2", "main", "ms", "u0", "main", "u1", "lo", "ms",
+    "c0", "main", "u2", "c1", "ms", "u0", "c2", "u1", "u3", "u2", "d0", "main", "d1", "u3", "c0",
+    "lo", "d0", "d2", "d1", "ig", "c1", "a0", "ms", "u0", "c2", "a0", "d2", "ms", "u1", "a1", "a2",
+    "u2", "a3", "a1", "a2", "a0", "a3", "ms", "w1", "u3", "a1", "a2", "a3", "u0", "w1", "d0", "u1",
+    "d1", "u2", "c2", "ig", "u3", "w1", "d2", "d0", "a0", "d1", "ms", "a1", "a2", "a3", "d2", "a0",
+    "ig", "ig", "a1", "a2", "a3",
 )
 
 F32 = jnp.float32
@@ -126,15 +128,11 @@
             assert least * (dp // 2) == size and least % 16 == 0
             self.xr_rows += size - least + (0 if paired else size)
             self.z_rows += least
-        self.stores = [
-            (self.conv_at, self.up_at),
-            (self.up_at, width + hidden),
-            (self.attn_at, 4 * heads_width),
-            (self.up1_at, width + hidden),
-        ]
         self.bits = dp.bit_length() - 1
         assert dp == 1 << self.bits and dp <= 8
         self.misc_rows = 16
+        self.arrivals = 127 + (2 * len(self.pieces) + 1) * (self.bits - 1) + dp - 2
+        self.departures = self.arrivals * 4 // 7
 
 
 def main_kernel(
@@ -146,21 +144,24 @@
     co_in,
     up_in,
     down_in,
-    gain,
-    bias,
+    gain_in,
+    bias_in,
     taps_in,
     positions,
-    cotangent,
+    out_grads_in,
     half_size,
     plan,
-    final_out,
+    final,
     layer_rows,
     input_rows,
     misc_out,
-    final,
     tap_weight,
     tap_on,
     where,
+    gain,
+    bias,
+    cotangent,
+    out_grads,
     wqkv,
     wao,
     wcin,
@@ -192,7 +193,6 @@
     mnorm,
     mslope,
     munits,
-    mdz,
     partial,
     cs,
     cr,
@@ -214,7 +214,6 @@
     misc,
     misc_in,
     load_sem,
-    store_sem,
     send_sem,
     recv_sem,
 ):
@@ -236,7 +235,7 @@
     inner_of = jnp.where(section == 0, 1, SECTIONS - 2)
     end_of = jnp.where(section == 1, 0, SECTIONS - 1)
     other_inner = SECTIONS - 1 - section
-    counter = [0]
+    counter = [0, 0]
     closing = []
     leaving = {}
 
@@ -250,37 +249,52 @@
         on = lax.rem(lax.div(replica, 1 << bit), 2)
         return (section, replica + (1 - 2 * on) * (1 << bit), member), on
 
-    def slots(count=1):
+    free, departures = [], {}
+
+    def slots():
         at = counter[0]
-        counter[0] += count
+        counter[0] += 1
+        if not free:
+            free.append(counter[1])
+            counter[1] += 1
+        departures[at] = free.pop()
         return at
+
+    def settle(keep=0):
+        while len(closing) > keep:
+            wait, done = closing.pop(0)
+            wait()
+            free.extend(departures[slot] for slot in done)
 
     def remote(src, dst, target, slot):
         return pltpu.make_async_remote_copy(
             src_ref=src,
             dst_ref=dst,
-            send_sem=send_sem.at[slot],
+            send_sem=send_sem.at[departures[slot]],
             recv_sem=recv_sem.at[slot],
             device_id=target,
             device_id_type=MESH,
         )
 
     def send(src, dst, target, slot=None):
-        copy = remote(src, dst, target, slots() if slot is None else slot)
+        slot = slots() if slot is None else slot
+        copy = remote(src, dst, target, slot)
         copy.start()
-        closing.append(copy.wait_send)
+        closing.append((copy.wait_send, (slot,)))
         return copy
 
-    def send_slot(name, ref, e, t, dst, target, slot=None):
-        copy = remote(ref.at[SETS[e], t], dst.at[SETS[e], t], target, slots() if slot is None else slot)
+    def send_slot(name, ref, e, t, dst, target):
+        slot = slots()
+        copy = remote(ref.at[SETS[e], t], dst.at[SETS[e], t], target, slot)
         copy.start()
-        leaving[name, SETS[e], t] = copy.wait_send
+        leaving[name, SETS[e], t] = copy.wait_send, (slot,)
         return copy
 
     def reuse(name, e, t):
-        wait = leaving.pop((name, SETS[e], t), None)
-        if wait is not None:
-            wait()
+        entry = leaving.pop((name, SETS[e], t), None)
+        if entry is not None:
+            closing.insert(0, entry)
+            settle(len(closing) - 1)
 
     barrier = pltpu.get_barrier_semaphore()
     peers = (
@@ -297,6 +311,9 @@
             ("x", x_in.at[section], hid.at[0, pl.ds(pl.multiple_of(member * part, part), part)]),
             ("qkv", qkv_in, wqkv),
             ("ao", ao_in, wao),
+            ("gain", gain_in, gain),
+            ("out_grads", out_grads_in, out_grads),
+            ("bias", bias_in, bias),
             ("up", up_in, wup),
             ("down", down_in, wdown),
             ("cin", cin_in, wcin),
@@ -377,7 +394,7 @@
         at = SETS[e]
         out = remote(ys.at[at, 1 - high], yr.at[at, 1 - high], across, slot)
         out.start()
-        leaving["ys", at, 0] = out.wait_send
+        leaving["ys", at, 0] = out.wait_send, (slot,)
         return remote(ys.at[at, high], yr.at[at, high], across, slot)
 
     def add_stat(column, amount):
@@ -520,7 +537,7 @@
         mine = pl.ds(pl.multiple_of(first, 16), size)
         z_rows = pl.ds(z_at, size)
         step = math.gcd(size, 64)
-        slot_a, slot_b, slot_c = slots(), slots(), slots()
+        slot_a, slot_b = slots(), slots()
 
         def z_copy(kind):
             if kind == "a":
@@ -531,7 +548,7 @@
                 return remote(
                     grads.at[mine], zb.at[z_rows], (other_inner, replica, member), slot_b
                 )
-            return remote(final.at[mine], final.at[mine], (end_of, replica, member), slot_c)
+            return remote(final.at[mine], final.at[mine], (end_of, replica, member), slot_a)
 
         steps.reverse()
         gather_slots = [slots() for _ in steps]
@@ -589,7 +606,7 @@
                 gather(at).start()
                 yield
             gather(at, True).wait_recv()
-            closing.append(gather(at).wait_send)
+            closing.append((gather(at).wait_send, (gather_slots[at],)))
 
         def close():
             @pl.when(is_end)
@@ -601,7 +618,7 @@
                 z_copy("b").wait_send()
                 z_copy("c").wait_send()
 
-        closing.append(close)
+        closing.append((close, (slot_a, slot_b)))
 
     reduce_piece.xr_at = 0
     reduce_piece.z_at = 0
@@ -619,6 +636,7 @@
         next(task)
 
     def pump(*names):
+        settle(KEEP)
         for name in names:
             if name in running:
                 try:
@@ -654,22 +672,15 @@
 
         for k in range(SECTIONS - 1):
             sends(k, "start")
-            closing.append(functools.partial(sends, k, "wait_send"))
+            closing.append((functools.partial(sends, k, "wait_send"), (right[k], left[k])))
             yield
             arrivals(k)
 
-    def final_store(at):
-        rows = pl.ds(*lay.stores[at])
-        return pltpu.make_async_copy(final.at[rows], final_out.at[rows], store_sem.at[at])
-
-    def store_final(at):
-        final_store(at).start()
-
     pl.semaphore_wait(barrier, len(peers))
+    mine = block(member * part, part)
+    to_across = send(x_in.at[section], hid.at[0, mine], across)
+    to_side = send(x_in.at[section], hid.at[0, mine], side)
     loads["x"].wait()
-    mine = block(member * part, part)
-    to_side = send(hid.at[0, mine], hid.at[0, mine], side)
-    to_across = send(hid.at[0, mine], hid.at[0, mine], across)
     hits[...] = jnp.where(
         lax.broadcasted_iota(jnp.int32, hits.shape, 0) == where[0:1, 0 : hits.shape[1]], 1.0, 0.0
     ).astype(BF16)
@@ -729,6 +740,8 @@
         rows = pl.ds(chunk * t, chunk)
         ffn_forward(0, hid.at[1], rows, units.at[rows], slope.at[rows])
 
+    for name in ("gain", "bias"):
+        loads[name].wait()
     attention_finish = forward_finish(0, 0, True)
     end(0, 0, attention_finish)
     begin(1, 0, ffn0_work)
@@ -835,6 +848,14 @@
     mnorm[0] = norm2
     mh[...] = (norm2 * gain[2:3] + bias[2:3]).astype(BF16)
 
+    def pick_cotangent():
+        loads["out_grads"].wait()
+        count = out_grads.shape[0]
+        slot = lax.broadcasted_iota(jnp.int32, (1, out_grads.shape[1], 1), 1)
+        mine = jnp.where(slot == section, used, 0.0)
+        cotangent[...] = jnp.zeros_like(cotangent)
+        cotangent[0:count] = jnp.sum(out_grads[...].astype(F32) * mine, axis=1)
+
     def marked_up(i, carry):
         lanes = block(i * LANES, LANES)
         unit, slope_here = gelu_parts(dot(mh[...], wup[1, :, lanes]))
@@ -846,16 +867,17 @@
 
     def beside_units():
         pump("lo")
+        pick_cotangent()
         pair_up(0)
 
     branch = marked_total(1, dot(munits[...], wdown[1]), beside_units)
     norm3, inv3 = normalise(mh[...].astype(F32) + branch)
     once = jnp.where(member == 0, 1.0, 0.0).astype(F32)
-    dy = cotangent[...].astype(F32) * used
+    dy = cotangent[...]
     misc[3:4] += once * jnp.sum(dy * norm3, axis=0, keepdims=True)
     misc[7:8] += once * jnp.sum(dy, axis=0, keepdims=True)
     dz3 = norm_pull(dy, norm3, inv3, gain[3:4])
-    mdz[0] = dz3
+    cotangent[...] = dz3
     df3 = dz3.astype(BF16)
 
     per_section = lay.dp * marked
@@ -871,9 +893,10 @@
         yield
         for copy in copies:
             copy.wait_recv()
-        yield from line_gather(
-            lambda at: factors.at[low, pl.ds(pl.multiple_of(at * per_section, 16), per_section)]
-        )
+        def of_section(at):
+            return factors.at[low, pl.ds(pl.multiple_of(at * per_section, 16), per_section)]
+
+        yield from line_gather(of_section)
         slot = slots()
         send(factors.at[low], factors.at[low], side, slot)
         yield
@@ -893,7 +916,7 @@
         pump("lo")
         pair_up(1)
 
-    dy = mdz[0] + marked_total(2, dot_lanes(munits[...], wup[1]), beside_down)
+    dy = cotangent[...] + marked_total(2, dot_lanes(munits[...], wup[1]), beside_down)
     pump("fa")
     norm2 = mnorm[0]
     misc[2:3] += once * jnp.sum(dy * norm2, axis=0, keepdims=True)
@@ -929,17 +952,23 @@
         sums.append(jnp.zeros((1, hw), F32))
         return carry + jnp.concatenate(sums, axis=0)
 
-    kernel_rows = tiles(lay.seq // tap_tile, taps_back, jnp.zeros((8, hw), F32)) * tap_on[...]
+    def conv_back_work(t):
+        rows = pl.ds(chunk * t, chunk)
+        partial[...] = dot(dgates[0, rows], wcin[0]) + dot(dgates[1, rows], wcin[1])
+
+    half_tiles = chunk // tap_tile
+    kernel_rows = lax.fori_loop(0, half_tiles, taps_back, jnp.zeros((8, hw), F32))
+    begin(2, 0, conv_back_work)
+    kernel_rows = lax.fori_loop(half_tiles, 2 * half_tiles, taps_back, kernel_rows)
+    cross(2, 0)
+    begin(2, 1, conv_back_work)
+    kernel_rows = kernel_rows * tap_on[...]
     grads[pl.ds(lay.kernel_at, lay.up_at - lay.kernel_at)] = jnp.zeros(
         (lay.up_at - lay.kernel_at, width), BF16
     )
     grads[pl.ds(lay.kernel_at, 16), 0:hw] = jnp.concatenate(
         [kernel_rows, jnp.zeros((8, hw), F32)], axis=0
     ).astype(BF16)
-
-    def conv_back_work(t):
-        rows = pl.ds(chunk * t, chunk)
-        partial[...] = dot(dgates[0, rows], wcin[0]) + dot(dgates[1, rows], wcin[1])
 
     def conv_back_finish(t):
         def grad_tile(rows, place):
@@ -1020,9 +1049,6 @@
     waits = {}
 
     def backward():
-        begin(2, 0, conv_back_work)
-        begin(2, 1, conv_back_work)
-        cross(2, 0)
         cross(2, 1)
         for j in range(2):
             grads[pl.ds(lay.conv_at + j * hw, hw)] = dot_rows(dgates[j], hid[2]).astype(BF16)
@@ -1122,7 +1148,6 @@
 
             tiles(width // LANES, last_weights)
             yield
-        store_final(3)
 
     def small_sums():
         assert summed >= {"norms", "rows"}
@@ -1134,12 +1159,12 @@
             copy.wait_recv()
             misc[...] = misc_in[2 * at] + misc_in[2 * at + 1]
         at = 2 * len(hops)
-        slot_a, slot_b, slot_c = slots(), slots(), slots()
+        slot_a, slot_b = slots(), slots()
         to_inner = remote(misc_in.at[at], misc_in.at[at + 1], (inner_of, replica, member), slot_a)
         to_other = remote(
             misc_in.at[at + 2], misc_in.at[at + 3], (other_inner, replica, member), slot_b
         )
-        to_end = remote(misc_out, misc_out, (end_of, replica, member), slot_c)
+        to_end = remote(misc_out, misc_out, (end_of, replica, member), slot_a)
 
         @pl.when(is_end)
         def _():
@@ -1184,27 +1209,24 @@
     for name in TAIL:
         if name in later:
             start(name, later.pop(name)())
-        elif name.startswith("s"):
-            store_final(int(name[1]))
         else:
             pump(name)
     assert not later
     while running:
         pump(*list(running))
-    for at in range(3):
-        store_final(at)
-    for at in range(len(lay.stores)):
-        final_store(at).wait()
-    for wait in closing + list(leaving.values()):
-        wait()
+    closing.extend(leaving.values())
+    settle()
+    assert counter[0] <= lay.arrivals and counter[1] <= lay.departures
 
 
 def widen_kernel(
     lay,
     final,
     input_rows,
+    layer_rows,
     misc,
     plan,
+    layer_out,
     input_grad,
     qkv,
     out,
@@ -1216,11 +1238,8 @@
     gains,
     biases,
     rms,
-    narrow,
     wide,
-    narrow_input,
     wide_input,
-    load_sem,
     store_sem,
 ):
     hw, width, hidden = lay.heads_width, lay.width, lay.hidden
@@ -1242,25 +1261,14 @@
         cover(lay.conv_at + j * hw, hw, cin.at[j], hw)
     cover(lay.conv_at + 2 * hw, hw, cout, hw)
 
-    def load(at):
-        start, rows, _ = blocks[at]
-        here = pl.ds(start, rows)
-        return pltpu.make_async_copy(final.at[here], narrow.at[here], load_sem.at[at])
-
     def store(at):
         start, rows, target = blocks[at]
         return pltpu.make_async_copy(wide.at[pl.ds(start, rows)], target, store_sem.at[at])
 
     extra = len(blocks)
-    tap_rows = pltpu.make_async_copy(
-        final.at[pl.ds(lay.kernel_at, 16)], narrow.at[pl.ds(lay.kernel_at, 16)], load_sem.at[extra]
-    )
-    inputs_in = pltpu.make_async_copy(input_rows, narrow_input, load_sem.at[extra + 1])
     inputs_out = pltpu.make_async_copy(wide_input, input_grad, store_sem.at[extra])
-    for at in range(len(blocks)):
-        load(at).start()
-    inputs_in.start()
-    tap_rows.start()
+    layer_done = pltpu.make_async_copy(layer_rows, layer_out, store_sem.at[extra + 1])
+    layer_done.start()
     gains[...] = misc[0:4]
     biases[...] = misc[4:8]
     row = lax.broadcasted_iota(jnp.int32, rms.shape, 0)
@@ -1272,36 +1280,30 @@
         counts = jnp.where(row == r, total, counts)
     rms[...] = jnp.sqrt(misc[8 : 8 + rms.shape[0], 0:8] / (counts * (lay.seq * width)))
     half = width // 2
-    for at in range(2):
-        load(at).wait()
     for at, (start, rows, _) in enumerate(blocks):
-        if at >= 2:
-            load(at).wait()
-
         def body(i, carry, start=start, at=at):
             here = pl.ds(pl.multiple_of(start + i * 32, 16), 32)
             if at >= 2:
-                wide[here] = narrow[here].astype(F32)
+                wide[here] = final[here].astype(F32)
             else:
                 for q in range(2):
                     there = pl.ds(pl.multiple_of(lay.up_at + q * half + i * 32, 16), 32)
-                    wide[here, q * half : (q + 1) * half] = narrow[
+                    wide[here, q * half : (q + 1) * half] = final[
                         there, at * half : (at + 1) * half
                     ].astype(F32)
             return carry
 
         lax.fori_loop(0, rows // 32, body, 0)
         store(at).start()
-    inputs_in.wait()
     for slot in range(input_rows.shape[0]):
-        wide_input[slot] = narrow_input[slot].astype(F32)
+        wide_input[slot] = input_rows[slot].astype(F32)
     inputs_out.start()
-    tap_rows.wait()
-    taps = narrow[pl.ds(lay.kernel_at, 16)].astype(F32)
+    taps = final[pl.ds(lay.kernel_at, 16)].astype(F32)
     kernel[...] = taps[0:TAPS, 0:hw]
     for at in range(len(blocks)):
         store(at).wait()
     inputs_out.wait()
+    layer_done.wait()
 
 
 def on_device(
@@ -1333,19 +1335,19 @@
     lay = Layout(dp, micro_count, part * GROUP, width, hw, hidden, marked)
     assert hidden == width and width % LANES == 0 and hw % HEAD == 0
 
-    cotangent = lax.dynamic_index_in_dim(out_grad, section, 0, keepdims=False)
-    cotangent = jnp.pad(cotangent, ((0, marked - count), (0, 0)))
-
     seq, chunk = lay.seq, lay.chunk
     any_spec = pl.BlockSpec(memory_space=pl.ANY)
     vmem_spec = pl.BlockSpec(memory_space=pltpu.VMEM)
     hops = 2 + lay.bits
     all_marked = SECTIONS * dp * marked
     scratch = [
-        pltpu.VMEM((lay.all_rows, width), BF16),
         pltpu.VMEM((8, hw), F32),
         pltpu.VMEM((8, hw), F32),
         pltpu.VMEM((8, marked), jnp.int32),
+        pltpu.VMEM(norm_gain.shape, F32),
+        pltpu.VMEM(norm_bias.shape, F32),
+        pltpu.VMEM((marked, width), F32),
+        pltpu.VMEM((count, slot_count, width), BF16),
         pltpu.VMEM((3, hw, width), BF16),
         pltpu.VMEM(attn_out.shape, BF16),
         pltpu.VMEM((2, hw, width), BF16),
@@ -1377,7 +1379,6 @@
         pltpu.VMEM((1, marked, width), F32),
         pltpu.VMEM((marked, hidden), F32),
         pltpu.VMEM((marked, hidden), BF16),
-        pltpu.VMEM((1, marked, width), F32),
         pltpu.VMEM((chunk, width), F32),
         pltpu.VMEM((4, 2, part, width), BF16),
         pltpu.VMEM((4, 2, part, width), BF16),
@@ -1398,25 +1399,24 @@
         pltpu.VMEM((seq, hidden // 2), BF16),
         pltpu.VMEM((lay.misc_rows, width), F32),
         pltpu.VMEM((2 * hops + 4, lay.misc_rows, width), F32),
-        pltpu.SemaphoreType.DMA((8,)),
-        pltpu.SemaphoreType.DMA((len(lay.stores),)),
-        pltpu.SemaphoreType.DMA((160,)),
-        pltpu.SemaphoreType.DMA((160,)),
+        pltpu.SemaphoreType.DMA((10,)),
+        pltpu.SemaphoreType.DMA((lay.departures,)),
+        pltpu.SemaphoreType.DMA((lay.arrivals,)),
     ]
     smem_spec = pl.BlockSpec(memory_space=pltpu.SMEM)
     final, layer_rows, input_rows, misc = pl.pallas_call(
         functools.partial(main_kernel, lay),
         out_shape=(
-            jax.ShapeDtypeStruct((lay.all_rows, width), BF16),
-            jax.ShapeDtypeStruct((slot_count, part, width), BF16),
-            jax.ShapeDtypeStruct((slot_count, part, width), BF16),
-            jax.ShapeDtypeStruct((lay.misc_rows, width), F32),
+            pltpu.VMEM((lay.all_rows, width), BF16),
+            pltpu.VMEM((slot_count, part, width), BF16),
+            pltpu.VMEM((slot_count, part, width), BF16),
+            pltpu.VMEM((lay.misc_rows, width), F32),
         ),
-        in_specs=[any_spec] * 7 + [vmem_spec] * 5 + [smem_spec] * 2,
-        out_specs=(any_spec,) + (vmem_spec,) * 3,
+        in_specs=[any_spec] * 9 + [vmem_spec] * 2 + [any_spec] + [smem_spec] * 2,
+        out_specs=(vmem_spec,) * 4,
         scratch_shapes=scratch,
         compiler_params=pltpu.CompilerParams(
-            collective_id=0, has_side_effects=True, vmem_limit_bytes=63 * 2**20
+            collective_id=0, has_side_effects=True, vmem_limit_bytes=VMEM_BYTES
         ),
         name="layers",
     )(
@@ -1431,7 +1431,7 @@
         norm_bias,
         conv_kernel,
         masked_positions,
-        cotangent,
+        jnp.swapaxes(out_grad, 0, 1),
         kernel_half,
         batch_plan,
     )
@@ -1450,23 +1450,27 @@
     ]
     widened = pl.pallas_call(
         functools.partial(widen_kernel, lay),
-        out_shape=tuple(jax.ShapeDtypeStruct(shape, F32) for shape in shapes),
-        in_specs=[any_spec] * 2 + [vmem_spec] + [smem_spec],
-        out_specs=(any_spec,) * 7 + (vmem_spec,) * 4,
+        out_shape=(jax.ShapeDtypeStruct(shapes[0], BF16),)
+        + tuple(jax.ShapeDtypeStruct(shape, F32) for shape in shapes),
+        in_specs=[vmem_spec] * 4 + [smem_spec],
+        out_specs=(any_spec,) * 8 + (vmem_spec,) * 4,
         scratch_shapes=[
-            pltpu.VMEM((lay.all_rows, width), BF16),
             pltpu.VMEM((lay.all_rows, width), F32),
-            pltpu.VMEM((slot_count, part, width), BF16),
             pltpu.VMEM((slot_count, part, width), F32),
-            pltpu.SemaphoreType.DMA((32,)),
-            pltpu.SemaphoreType.DMA((32,)),
+            pltpu.SemaphoreType.DMA((17,)),
         ],
-        compiler_params=pltpu.CompilerParams(vmem_limit_bytes=48 * 2**20),
+        compiler_params=pltpu.CompilerParams(vmem_limit_bytes=VMEM_BYTES),
         name="widen",
-    )(final, input_rows, misc, batch_plan)
-    (input_grad, qkv, out, cin, cout, up, down, kernel, gains, biases, rms) = widened
+    )(
+        *[
+            pltpu.with_memory_space_constraint(result, pltpu.VMEM)
+            for result in (final, input_rows, layer_rows, misc)
+        ],
+        batch_plan,
+    )
+    (layer_out, input_grad, qkv, out, cin, cout, up, down, kernel, gains, biases, rms) = widened
     return (
-        layer_rows,
+        layer_out,
         input_grad,
         jnp.swapaxes(qkv, 1, 2),
         out,

time: 184 us -> 175 us (0.951)
  Pallas kernels: 179 us -> 173 us
  local copies, waits for them, and re-layouts: 4.07 us -> 0 us
    pallas_call x2, Pallas kernels: 179 us -> 173 us  [the longest x1 166 us: on_device(): pl.pallas_call(functools.partial(main_kernel, lay), out_shape=(pltpu.VMEM...]
    unnamed x12 -> x0, local copies, waits for them, and re-layouts: 3.17 us -> none
where the time goes in v4:
time: 175 us; the launch traced here: 174 us
  Pallas kernels  173 us (99%)
    pallas_call x1, Pallas kernels, on_device(): pl.pallas_call(functools.partial(main_kernel, lay), out_shape=(pltpu.VMEM...  166 us
    pallas_call x1, Pallas kernels, on_device(): pl.pallas_call(functools.partial(widen_kernel, lay), out_shape=(jax.Shape...  7.04 us

profile of v4, /device:TPU:0, one launch (start us, length us, event | category | flops | bytes accessed | tf_op | source)
XLA Modules:
  0.0 174.5 jit_solution(440145234539428873)
XLA Ops:
  1.3 166.0 %layers.1 = (bf16[4480,768]{1,0:T(8,128)(2,1)S(1)}, bf16[4,128,768]{2,1,0:T(8,128)(2,1)S(1)}, bf16[4,128,768]{2,1,0:T(8,128)(2,1)S(1)}, f32[16,768]{1,0:T(8,128)S(1)}) custom-call(bf16[4,128,768]{2,1,0:T(8,128)(2,1)} %x_in.1, bf16[3,192,768]{2,1,0:T(8,128)(2,1)} %bitcast.5, bf16[192,768]{1,0:T(8,128)(2,1)} %ao_in.1, bf16[2,192,768]{2,1,0:T(8,128)(2,1)} %bitcast.6, ...), custom_call_target="tpu_custom_call" | custom-call | tf_op jit(solution)/shard_map/layers/pallas_call | solution.py:1407
  167.3 7.0 %widen.1 = (bf16[4,128,768]{2,1,0:T(8,128)(2,1)}, f32[4,128,768]{2,1,0:T(8,128)}, f32[3,192,768]{2,1,0:T(8,128)}, f32[192,768]{1,0:T(8,128)}, f32[2,192,768]{2,1...) custom-call(bf16[4480,768]{1,0:T(8,128)(2,1)S(1)} %get-tuple-element, ...), custom_call_target="tpu_custom_call" | custom-call | tf_op jit(solution)/shard_map/widen/pallas_call | solution.py:1451

commit v5 on v4

--- a/solution.py
+++ b/solution.py
@@ -23,13 +23,13 @@
 KEEP = 12
 C_CUT, U_CUT, D_CUT, A_CUT = (2, 1, 2), (1, 1, 2, 2), (2, 2, 2), (2, 2, 1, 1)
 TAIL = (
-    "main", "fa", "lo", "lo", "c0", "fa", "main", "c1", "lo", "c0", "main", "fa", "fa", "c1", "lo",
-    "c2", "pw", "main", "c0", "pw", "pw", "c1", "c2", "main", "ms", "u0", "main", "u1", "lo", "ms",
-    "c0", "main", "u2", "c1", "ms", "u0", "c2", "u1", "u3", "u2", "d0", "main", "d1", "u3", "c0",
-    "lo", "d0", "d2", "d1", "ig", "c1", "a0", "ms", "u0", "c2", "a0", "d2", "ms", "u1", "a1", "a2",
-    "u2", "a3", "a1", "a2", "a0", "a3", "ms", "w1", "u3", "a1", "a2", "a3", "u0", "w1", "d0", "u1",
-    "d1", "u2", "c2", "ig", "u3", "w1", "d2", "d0", "a0", "d1", "ms", "a1", "a2", "a3", "d2", "a0",
-    "ig", "ig", "a1", "a2", "a3",
+    "main", "fa", "lo", "lo", "c0", "fa", "main", "c0", "c1", "lo", "main", "c0", "fa", "fa", "c1",
+    "pw", "c2", "main", "lo", "pw", "pw", "c0", "c1", "c2", "main", "main", "c0", "lo", "u0", "c1",
+    "main", "c1", "lo", "u0", "u2", "c2", "u3", "u0", "u1", "u2", "ms", "d0", "u3", "d1", "u1",
+    "d2", "d0", "d1", "c2", "ms", "a0", "a0", "u2", "u3", "u0", "a3", "a3", "a1", "c2", "u1", "d2",
+    "ms", "a2", "a1", "u2", "d0", "d1", "u3", "u1", "d2", "a2", "a0", "a3", "ig", "d0", "d1", "a3",
+    "a1", "a0", "a2", "d2", "ms", "a1", "ig", "w1", "a2", "ms", "a3", "ms", "a0", "ms", "ig", "w1",
+    "a1", "w1", "a2", "ig",
 )
 
 F32 = jnp.float32
@@ -193,7 +193,6 @@
     mnorm,
     mslope,
     munits,
-    partial,
     cs,
     cr,
     ys,
@@ -352,26 +351,16 @@
     def tiles(count, body, init=0):
         return lax.fori_loop(0, count, body, init)
 
-    def exchange_send(e, t):
+    def exchange_send(e, t, product):
         reuse("cs", e, t)
         reuse("ys", e, t)
-        at = SETS[e]
-
-        def body(i, carry):
-            rows = block(i * TILE, TILE)
-            cs[at, t, rows] = partial[block(part * (1 - low) + i * TILE, TILE)].astype(BF16)
-            return carry
-
-        tiles(part // TILE, body)
+        cs[SETS[e], t] = product(1 - low).astype(BF16)
         copy = send_slot("cs", cs, e, t, cr, side)
-
-        def body(i, carry):
-            rows = block(i * TILE, TILE)
-            ys[at, t, rows] = partial[block(part * low + i * TILE, TILE)].astype(BF16)
-            return carry
-
-        tiles(part // TILE, body)
+        ys[SETS[e], t] = product(low).astype(BF16)
         return copy
+
+    def half_rows(t, core):
+        return block(chunk * t + part * core, part)
 
     def sums_across(e, t, core_copy, start=True):
         core_copy.wait_recv()
@@ -406,8 +395,7 @@
     core_copies, y_copies, gathered = {}, {}, {}
 
     def begin(e, t, work):
-        work(t)
-        core_copies[e, t] = exchange_send(e, t)
+        core_copies[e, t] = exchange_send(e, t, work(t))
 
     def cross(e, t):
         y_copies[e, t] = sums_across(e, t, core_copies[e, t])
@@ -715,7 +703,7 @@
             probs[i, rows] = chances
             mixture = mixture + jnp.where(head_lanes[i], dot(chances.astype(BF16), qkv[2]), 0.0)
         mix[rows] = mixture.astype(BF16)
-        partial[...] = dot(mix[rows], wao[...])
+        return lambda core: dot(mix[half_rows(t, core)], wao[...])
 
     begin(0, 0, attention_work)
     begin(0, 1, attention_work)
@@ -733,12 +721,14 @@
             return carry
 
         tiles(lay.hidden // LANES, body)
-        partial[...] = dot(units_here[...], wdown[layer])
 
     def ffn0_work(t):
-        gathered[0, t].wait_recv()
-        rows = pl.ds(chunk * t, chunk)
-        ffn_forward(0, hid.at[1], rows, units.at[rows], slope.at[rows])
+        for core in (low, 1 - low):
+            if core is not low:
+                gathered[0, t].wait_recv()
+            rows = half_rows(t, core)
+            ffn_forward(0, hid.at[1], rows, units.at[rows], slope.at[rows])
+        return lambda core: dot(units[half_rows(t, core)], wdown[0])
 
     for name in ("gain", "bias"):
         loads[name].wait()
@@ -758,13 +748,16 @@
         buffer[PAD + lay.seq : 2 * PAD + lay.seq] = edge
 
     def conv_gates(t):
-        gathered[1, t].wait_recv()
-        rows = pl.ds(chunk * t, chunk)
-        value_here = dot_lanes(hid[2, rows], wcin[0])
-        sig_here = jax.nn.sigmoid(dot_lanes(hid[2, rows], wcin[1]))
-        value[rows] = value_here
-        sig[rows] = sig_here
-        gated[pl.ds(PAD + chunk * t, chunk)] = value_here * sig_here
+        for core in (low, 1 - low):
+            if core is not low:
+                gathered[1, t].wait_recv()
+            rows = half_rows(t, core)
+            value_here = dot_lanes(hid[2, rows], wcin[0])
+            sig_here = jax.nn.sigmoid(dot_lanes(hid[2, rows], wcin[1]))
+            value[rows] = value_here
+            sig[rows] = sig_here
+            place = pl.ds(pl.multiple_of(PAD + chunk * t + part * core, 8), part)
+            gated[place] = value_here * sig_here
 
     ffn0_finish = forward_finish(1, 1, True)
     pass_on(0)
@@ -798,11 +791,12 @@
 
 
     def conv_work(t):
-        partial[...] = dot(conv[pl.ds(chunk * t, chunk)], wco[...])
+        return lambda core: dot(conv[half_rows(t, core)], wco[...])
 
     def ffn1_work(t):
         gathered[5, t].wait_recv()
         ffn_forward(1, hid.at[3], pl.ds(chunk * t, chunk), last_units)
+        return lambda core: dot(last_units[block(part * core, part)], wdown[1])
 
     def layer_output():
         last_finish = forward_finish(5, 2, False)
@@ -953,8 +947,11 @@
         return carry + jnp.concatenate(sums, axis=0)
 
     def conv_back_work(t):
-        rows = pl.ds(chunk * t, chunk)
-        partial[...] = dot(dgates[0, rows], wcin[0]) + dot(dgates[1, rows], wcin[1])
+        def product(core):
+            rows = half_rows(t, core)
+            return dot(dgates[0, rows], wcin[0]) + dot(dgates[1, rows], wcin[1])
+
+        return product
 
     half_tiles = chunk // tap_tile
     kernel_rows = lax.fori_loop(0, half_tiles, taps_back, jnp.zeros((8, hw), F32))
@@ -977,17 +974,19 @@
         return norm_back_rows(1, t, grad_tile)
 
     def ffn0_back_work(t):
-        gathered[2, t].wait_recv()
-        rows = pl.ds(chunk * t, chunk)
-
-        def body(i, carry):
-            lanes = block(i * LANES, LANES)
-            grad_units = dot_lanes(dfull[1, rows], wdown[0, lanes])
-            dbefore[rows, lanes] = (grad_units * slope[rows, lanes]).astype(BF16)
-            return carry
-
-        tiles(lay.hidden // LANES, body)
-        partial[...] = dot_lanes(dbefore[rows], wup[0])
+        for core in (low, 1 - low):
+            if core is not low:
+                gathered[2, t].wait_recv()
+            rows = half_rows(t, core)
+
+            def body(i, carry, rows=rows):
+                lanes = block(i * LANES, LANES)
+                grad_units = dot_lanes(dfull[1, rows], wdown[0, lanes])
+                dbefore[rows, lanes] = (grad_units * slope[rows, lanes]).astype(BF16)
+                return carry
+
+            tiles(lay.hidden // LANES, body)
+        return lambda core: dot_lanes(dbefore[half_rows(t, core)], wup[0])
 
     def ffn0_back_finish(t):
         return norm_back_rows(
@@ -1021,12 +1020,15 @@
         launch(*lay.groups["d"])
 
     def attention_back_work(t):
-        rows = pl.ds(chunk * t, chunk)
-        partial[...] = (
-            dot(dqkv[0, rows], wqkv[0])
-            + dot(dqkv[1, rows], wqkv[1])
-            + dot(dqkv[2, rows], wqkv[2])
-        )
+        def product(core):
+            rows = half_rows(t, core)
+            return (
+                dot(dqkv[0, rows], wqkv[0])
+                + dot(dqkv[1, rows], wqkv[1])
+                + dot(dqkv[2, rows], wqkv[2])
+            )
+
+        return product
 
     def attention_back_rows(t):
         gathered[3, t].wait_recv()
@@ -1074,16 +1076,15 @@
         attention_back_rows(1)
         dqkv[1] = (dkv[0] * scale).astype(BF16)
         dqkv[2] = dkv[1].astype(BF16)
+        for j in range(3):
+            grads[pl.ds(lay.attn_at + j * hw, hw)] = dot_rows(dqkv[j], hid[0]).astype(BF16)
+        grads[pl.ds(lay.attn_at + 3 * hw, hw)] = dot_rows(mix[...], dfull[0]).astype(BF16)
+        launch(*lay.groups["a"])
         for t in range(2):
             begin(4, t, attention_back_work)
         for t in range(2):
             sums_across(4, t, core_copies[4, t], start=False)
         waits["input"] = send_half(4)
-        yield
-        for j in range(3):
-            grads[pl.ds(lay.attn_at + j * hw, hw)] = dot_rows(dqkv[j], hid[0]).astype(BF16)
-        grads[pl.ds(lay.attn_at + 3 * hw, hw)] = dot_rows(mix[...], dfull[0]).astype(BF16)
-        launch(*lay.groups["a"])
 
     def feed_forward_weights():
         own_weights()
@@ -1379,7 +1380,6 @@
         pltpu.VMEM((1, marked, width), F32),
         pltpu.VMEM((marked, hidden), F32),
         pltpu.VMEM((marked, hidden), BF16),
-        pltpu.VMEM((chunk, width), F32),
         pltpu.VMEM((4, 2, part, width), BF16),
         pltpu.VMEM((4, 2, part, width), BF16),
         pltpu.VMEM((4, 2, part, width), BF16),

time: 175 us -> 173 us (0.989)
  Pallas kernels: 173 us -> 171 us
where the time goes in v5:
time: 173 us
  Pallas kernels  171 us (99%)
    pallas_call x1, Pallas kernels, on_device(): pl.pallas_call(functools.partial(main_kernel, lay), out_shape=(pltpu.VMEM...  164 us
    pallas_call x1, Pallas kernels, on_device(): pl.pallas_call(functools.partial(widen_kernel, lay), out_shape=(jax.Shape...  7.04 us

profile of v5, /device:TPU:0, one launch (start us, length us, event | category | flops | bytes accessed | tf_op | source)
XLA Modules:
  0.0 172.8 jit_solution(14832345526858118682)
XLA Ops:
  1.3 164.2 %layers.1 = (bf16[4480,768]{1,0:T(8,128)(2,1)S(1)}, bf16[4,128,768]{2,1,0:T(8,128)(2,1)S(1)}, bf16[4,128,768]{2,1,0:T(8,128)(2,1)S(1)}, f32[16,768]{1,0:T(8,128)S(1)}) custom-call(bf16[4,128,768]{2,1,0:T(8,128)(2,1)} %x_in.1, bf16[3,192,768]{2,1,0:T(8,128)(2,1)} %bitcast.5, bf16[192,768]{1,0:T(8,128)(2,1)} %ao_in.1, bf16[2,192,768]{2,1,0:T(8,128)(2,1)} %bitcast.6, ...), custom_call_target="tpu_custom_call" | custom-call | tf_op jit(solution)/shard_map/layers/pallas_call | solution.py:1407
  165.5 7.0 %widen.1 = (bf16[4,128,768]{2,1,0:T(8,128)(2,1)}, f32[4,128,768]{2,1,0:T(8,128)}, f32[3,192,768]{2,1,0:T(8,128)}, f32[192,768]{1,0:T(8,128)}, f32[2,192,768]{2,1...) custom-call(bf16[4480,768]{1,0:T(8,128)(2,1)S(1)} %get-tuple-element, ...), custom_call_target="tpu_custom_call" | custom-call | tf_op jit(solution)/shard_map/widen/pallas_call | solution.py:1451

commit v6 on v5

--- a/solution.py
+++ b/solution.py
@@ -23,13 +23,13 @@
 KEEP = 12
 C_CUT, U_CUT, D_CUT, A_CUT = (2, 1, 2), (1, 1, 2, 2), (2, 2, 2), (2, 2, 1, 1)
 TAIL = (
-    "main", "fa", "lo", "lo", "c0", "fa", "main", "c0", "c1", "lo", "main", "c0", "fa", "fa", "c1",
-    "pw", "c2", "main", "lo", "pw", "pw", "c0", "c1", "c2", "main", "main", "c0", "lo", "u0", "c1",
-    "main", "c1", "lo", "u0", "u2", "c2", "u3", "u0", "u1", "u2", "ms", "d0", "u3", "d1", "u1",
-    "d2", "d0", "d1", "c2", "ms", "a0", "a0", "u2", "u3", "u0", "a3", "a3", "a1", "c2", "u1", "d2",
-    "ms", "a2", "a1", "u2", "d0", "d1", "u3", "u1", "d2", "a2", "a0", "a3", "ig", "d0", "d1", "a3",
-    "a1", "a0", "a2", "d2", "ms", "a1", "ig", "w1", "a2", "ms", "a3", "ms", "a0", "ms", "ig", "w1",
-    "a1", "w1", "a2", "ig",
+    "main", "fa", "lo", "lo", "c0", "fa", "main", "c1", "c0", "lo", "c2", "fa", "fa", "main", "c0",
+    "c1", "pw", "main", "lo", "pw", "c2", "pw", "c0", "c1", "main", "main", "u0", "lo", "main",
+    "c0", "c2", "u0", "c1", "u1", "lo", "u2", "ms", "a0", "u3", "u1", "ms", "d0", "u2", "a1", "ig",
+    "a2", "c2", "u0", "u1", "a3", "d1", "u3", "ms", "c1", "u2", "d2", "d0", "a0", "a1", "d1", "d2",
+    "a2", "a3", "a0", "a1", "a2", "a3", "c2", "ig", "u0", "u1", "u3", "ms", "ms", "d0", "u2", "w1",
+    "d1", "u3", "d0", "d2", "w1", "a0", "d1", "a1", "d2", "a2", "a0", "a3", "a1", "ig", "a2", "ig",
+    "ms", "a3", "ms", "w1",
 )
 
 F32 = jnp.float32
@@ -132,7 +132,7 @@
         assert dp == 1 << self.bits and dp <= 8
         self.misc_rows = 16
         self.arrivals = 127 + (2 * len(self.pieces) + 1) * (self.bits - 1) + dp - 2
-        self.departures = self.arrivals * 4 // 7
+        self.departures = self.arrivals * 3 // 5
 
 
 def main_kernel(
@@ -906,9 +906,9 @@
 
     tiles(lay.hidden // LANES, marked_down)
     def beside_down():
+        pair_up(1)
         pump("lo")
         pump("lo")
-        pair_up(1)
 
     dy = cotangent[...] + marked_total(2, dot_lanes(munits[...], wup[1]), beside_down)
     pump("fa")

time: 173 us -> 173 us (level)
  no operation moved by 1% of the time
where the time goes in v6:
time: 173 us
  Pallas kernels  171 us (99%)
    pallas_call x1, Pallas kernels, on_device(): pl.pallas_call(functools.partial(main_kernel, lay), out_shape=(pltpu.VMEM...  164 us
    pallas_call x1, Pallas kernels, on_device(): pl.pallas_call(functools.partial(widen_kernel, lay), out_shape=(jax.Shape...  7.04 us

profile of v6, /device:TPU:0, one launch (start us, length us, event | category | flops | bytes accessed | tf_op | source)
XLA Modules:
  0.0 172.6 jit_solution(12005992467820343900)
XLA Ops:
  1.3 164.0 %layers.1 = (bf16[4480,768]{1,0:T(8,128)(2,1)S(1)}, bf16[4,128,768]{2,1,0:T(8,128)(2,1)S(1)}, bf16[4,128,768]{2,1,0:T(8,128)(2,1)S(1)}, f32[16,768]{1,0:T(8,128)S(1)}) custom-call(bf16[4,128,768]{2,1,0:T(8,128)(2,1)} %x_in.1, bf16[3,192,768]{2,1,0:T(8,128)(2,1)} %bitcast.5, bf16[192,768]{1,0:T(8,128)(2,1)} %ao_in.1, bf16[2,192,768]{2,1,0:T(8,128)(2,1)} %bitcast.6, ...), custom_call_target="tpu_custom_call" | custom-call | tf_op jit(solution)/shard_map/layers/pallas_call | solution.py:1407
  165.3 7.0 %widen.1 = (bf16[4,128,768]{2,1,0:T(8,128)(2,1)}, f32[4,128,768]{2,1,0:T(8,128)}, f32[3,192,768]{2,1,0:T(8,128)}, f32[192,768]{1,0:T(8,128)}, f32[2,192,768]{2,1...) custom-call(bf16[4480,768]{1,0:T(8,128)(2,1)S(1)} %get-tuple-element, ...), custom_call_target="tpu_custom_call" | custom-call | tf_op jit(solution)/shard_map/widen/pallas_call | solution.py:1451
